TPU v7x, 256 devices: a whole 4x4x8 slice. The times are simulated.
256 devices in a mesh: ctx: 64 (over x, z, core), head: 4 (over y).
Axes of the slice: x: 4, y: 4, z: 8, core: 2. Of those that a mesh axis runs over, the one named last changes fastest.
Arguments:
- queries: bfloat16 [65536, 4096], P(('ctx', 'head')), may hold values from -6 to 6
- key_rows: bfloat16 [65536, 1024], P(('ctx', 'head')), may hold values from -4.5 to 4.5
- value_rows: bfloat16 [65536, 1024], P(('ctx', 'head')), may hold values from -6 to 6
- block_gates: int32 [512, 32, 3], P('ctx', 'head'), may hold values from -1 to 62, as said below
Outputs:
- attended: bfloat16 [65536, 4096], P(('ctx', 'head'))
Inputs may be any that keep to these rules, and one draw needn't show every extreme that they name: `block_gates`: entry (t, h, k) is -1 (slot unused) or a block before the block of tile t; the blocks named for one tile and head differ; the entries held by one device (one index of ctx and one of head) name any block at most 2 times, and some block exactly 2 times on every device after the first index of ctx.
All inputs are finite; a program needn't handle non-finite values.
Results may differ from a plain program's by a relative error of at most 0.005.
Values may be sent and summed in bfloat16 or wider, within the bound.
No kernel may reach another device: no remote copies, remote signals or barrier semaphores. Data moves between devices by JAX's collectives and lax.ppermute only.
A program may use at most 128 MiB of HBM per device.

v0:
```python
import math

import jax
import jax.numpy as jnp
from jax import lax
from jax.sharding import PartitionSpec as P

HEAD_DIM = 128
TILE = 128
CAP = 2


def attend_rows(query_rows, key_block, value_block, score_scale):
    scores = (
        jnp.einsum("gsd,gkd->gsk", query_rows, key_block, preferred_element_type=jnp.float32)
        * score_scale
    )
    row_peak = jnp.max(scores, axis=-1, keepdims=True)
    logsum = row_peak + jnp.log(jnp.sum(jnp.exp(scores - row_peak), axis=-1, keepdims=True))
    weights = jnp.exp(scores - logsum).astype(jnp.bfloat16)
    mixed_rows = jnp.einsum(
        "gsk,gkd->gsd", weights, value_block, preferred_element_type=jnp.float32
    )
    return (mixed_rows.astype(jnp.bfloat16), logsum[..., 0])


def own_block(query_all, key_all, value_all, score_scale):
    row_count = query_all.shape[0]
    kv_local = key_all.shape[1]
    per_group = query_all.shape[1] // kv_local
    causal = lax.broadcasted_iota(jnp.int32, (row_count, row_count), 0) >= lax.broadcasted_iota(
        jnp.int32, (row_count, row_count), 1
    )
    mixed_parts = []
    log_parts = []
    for kv_index in range(kv_local):
        query_part = query_all[:, kv_index * per_group : (kv_index + 1) * per_group, :]
        scores = (
            jnp.einsum(
                "shd,kd->hsk",
                query_part,
                key_all[:, kv_index, :],
                preferred_element_type=jnp.float32,
            )
            * score_scale
        )
        scores = jnp.where(causal[None], scores, -jnp.inf)
        row_peak = jnp.max(scores, axis=-1, keepdims=True)
        logsum = row_peak + jnp.log(jnp.sum(jnp.exp(scores - row_peak), axis=-1, keepdims=True))
        weights = jnp.exp(scores - logsum).astype(jnp.bfloat16)
        mixed_parts.append(
            jnp.einsum(
                "hsk,kd->shd",
                weights,
                value_all[:, kv_index, :],
                preferred_element_type=jnp.float32,
            )
        )
        log_parts.append(logsum[..., 0])
    return (jnp.concatenate(mixed_parts, axis=1), jnp.concatenate(log_parts, axis=0))


def local(queries, key_rows, value_rows, block_gates):
    ctx_count = lax.axis_size("ctx")
    score_scale = HEAD_DIM ** (-0.5)
    q_local, k_local, v_local = (
        lax.all_to_all(queries, "head", split_axis=1, concat_axis=0, tiled=True),
        lax.all_to_all(key_rows, "head", split_axis=1, concat_axis=0, tiled=True),
        lax.all_to_all(value_rows, "head", split_axis=1, concat_axis=0, tiled=True),
    )
    token_count = q_local.shape[0]
    q_heads = q_local.shape[1] // HEAD_DIM
    kv_local = k_local.shape[1] // HEAD_DIM
    per_group = q_heads // kv_local
    query_all = q_local.reshape(token_count, q_heads, HEAD_DIM)
    key_all = k_local.reshape(token_count, kv_local, HEAD_DIM)
    value_all = v_local.reshape(token_count, kv_local, HEAD_DIM)
    own_out, own_log = own_block(query_all, key_all, value_all, score_scale)
    tile_count = token_count // TILE
    slot_count = block_gates.shape[2]
    request_owner = block_gates.reshape(-1)
    live_mask = request_owner >= 0
    owner_onehot = (
        request_owner[:, None] == jnp.arange(ctx_count, dtype=jnp.int32)[None, :]
    ).astype(jnp.int32)
    earlier_count = jnp.cumsum(owner_onehot, axis=0) - owner_onehot
    request_rank = jnp.sum(earlier_count * owner_onehot, axis=1)
    request_head = jnp.arange(request_owner.shape[0], dtype=jnp.int32) // slot_count % q_heads
    key_store = key_all[None]
    value_store = value_all[None]
    keys_by_block = key_store.transpose(0, 2, 1, 3).reshape(-1, token_count, HEAD_DIM)
    values_by_block = value_store.transpose(0, 2, 1, 3).reshape(-1, token_count, HEAD_DIM)
    send_target = jnp.where(live_mask, request_owner, ctx_count)
    tile_queries = query_all.reshape(tile_count, TILE, q_heads, HEAD_DIM).transpose(0, 2, 1, 3)
    request_rows = jnp.broadcast_to(
        tile_queries[:, :, None], (tile_count, q_heads, slot_count, TILE, HEAD_DIM)
    ).reshape(-1, TILE, HEAD_DIM)
    send_rows = (
        jnp.zeros((ctx_count, CAP, TILE, HEAD_DIM), jnp.bfloat16)
        .at[send_target, request_rank]
        .set(request_rows, mode="drop")
    )
    send_codes = (
        jnp.full((ctx_count, CAP), -1, jnp.int32)
        .at[send_target, request_rank]
        .set(request_head, mode="drop")
    )
    recv_rows = lax.all_to_all(send_rows, "ctx", split_axis=0, concat_axis=0, tiled=True)
    recv_codes = lax.all_to_all(send_codes, "ctx", split_axis=0, concat_axis=0, tiled=True)
    senders = recv_codes.shape[0]
    slot_total = recv_codes.shape[1]
    item_total = senders * slot_total
    flat_rows = recv_rows.reshape(item_total, TILE, HEAD_DIM)
    flat_codes = recv_codes.reshape(item_total)
    present = flat_codes >= 0
    position = jnp.cumsum(present.astype(jnp.int32)) - 1
    filled = jnp.sum(present.astype(jnp.int32))
    source = (
        jnp.zeros((item_total,), jnp.int32)
        .at[jnp.where(present, position, item_total)]
        .set(jnp.arange(item_total, dtype=jnp.int32), mode="drop")
    )
    packed_rows = flat_rows[source]
    packed_codes = jnp.maximum(flat_codes[source], 0)
    which_store = packed_codes // q_heads * kv_local + packed_codes % q_heads // per_group
    step_items = math.gcd(item_total, 16)
    rounds = (filled + step_items - 1) // step_items

    def one_round(round_index, carry):
        out_buffer, log_buffer = carry
        first_item = round_index * step_items
        rows_now = lax.dynamic_slice_in_dim(packed_rows, first_item, step_items, 0)
        store_pick = lax.dynamic_slice_in_dim(which_store, first_item, step_items, 0)
        mixed_rows, log_rows = attend_rows(
            rows_now, keys_by_block[store_pick], values_by_block[store_pick], score_scale
        )
        out_buffer = lax.dynamic_update_slice_in_dim(out_buffer, mixed_rows, first_item, 0)
        log_buffer = lax.dynamic_update_slice_in_dim(log_buffer, log_rows, first_item, 0)
        return (out_buffer, log_buffer)

    start_buffers = (
        jnp.zeros((item_total, TILE, HEAD_DIM), jnp.bfloat16),
        jnp.zeros((item_total, TILE), jnp.float32),
    )
    out_buffer, log_buffer = lax.fori_loop(0, rounds, one_round, start_buffers)
    back_index = jnp.where(present, position, 0)
    item_out = out_buffer[back_index].reshape(senders, slot_total, TILE, HEAD_DIM)
    item_log = log_buffer[back_index].reshape(senders, slot_total, TILE)
    returned_out = lax.all_to_all(item_out, "ctx", split_axis=0, concat_axis=0, tiled=True)
    returned_log = lax.all_to_all(item_log, "ctx", split_axis=0, concat_axis=0, tiled=True)
    returned_out, returned_log = (returned_out, returned_log)
    safe_target = jnp.where(live_mask, request_owner, 0)
    safe_rank = jnp.where(live_mask, request_rank, 0)
    gate_out = returned_out[safe_target, safe_rank].reshape(
        tile_count, q_heads, slot_count, TILE, HEAD_DIM
    )
    gate_log = returned_log[safe_target, safe_rank].reshape(tile_count, q_heads, slot_count, TILE)
    live_grid = live_mask.reshape(tile_count, q_heads, slot_count)[..., None]
    tile_out = own_out.reshape(tile_count, TILE, q_heads, HEAD_DIM).transpose(0, 2, 1, 3)
    tile_log = own_log.reshape(q_heads, tile_count, TILE).transpose(1, 0, 2)
    top_log = jnp.maximum(
        tile_log, jnp.max(jnp.where(live_grid, gate_log, tile_log[:, :, None, :]), axis=2)
    )
    own_weight = jnp.exp(tile_log - top_log)
    gate_weight = jnp.where(live_grid, jnp.exp(gate_log - top_log[:, :, None, :]), 0.0)
    total_weight = own_weight + jnp.sum(gate_weight, axis=2)
    merged = own_weight[..., None] * tile_out + jnp.sum(
        gate_weight[..., None] * gate_out.astype(jnp.float32), axis=2
    )
    merged = (
        (merged / total_weight[..., None])
        .transpose(0, 2, 1, 3)
        .reshape(token_count, q_heads * HEAD_DIM)
        .astype(jnp.bfloat16)
    )
    return lax.all_to_all(merged, "head", split_axis=0, concat_axis=1, tiled=True)


def solution(mesh):
    return jax.shard_map(
        local,
        mesh=mesh,
        in_specs=(
            P(("ctx", "head"), None),
            P(("ctx", "head"), None),
            P(("ctx", "head"), None),
            P("ctx", "head", None),
        ),
        out_specs=P(("ctx", "head"), None),
        check_vma=False,
    )
```

profile of v0, /device:TPU:3, one launch (start us, length us, event | category | flops | bytes accessed | tf_op | source)
XLA Modules:
  0.0 517.3 jit_solution(11113010482250955085)
XLA Ops:
  2.3 9.4 %scatter_fusion = s32[64,2]{0,1:T(2,128)S(1)} fusion(s32[64,2]{0,1:T(2,128)S(1)} %broadcast_in_dim.113, s32[192]{0:T(256)S(1)} %bitcast.135, s32[192]{0:T(256)S(1)} %and_select_fusion.3), kind=kCustom, calls=%fused_computation.8 | custom fusion | bytes 3840 | tf_op jit(solution)/shard_map/scatter | solution.py:106
  12.4 12.3 %all-to-all-start.2 = ((s32[64,1,2]{2,1,0:T(1,128)}), s32[64,1,2]{2,1,0:T(1,128)S(1)}, u32[]{:S(2)}, u32[]{:S(2)}) async-start(s32[64,1,2]{2,1,0:T(1,128)} %copy.88), calls=%async_computation.2 | async-start | bytes 65536 | tf_op jit(solution)/shard_map/all_to_all | solution.py:109
  26.7 6.3 %all-to-all-done.2 = s32[64,1,2]{2,1,0:T(1,128)S(1)} async-done(((s32[64,1,2]{2,1,0:T(1,128)}), s32[64,1,2]{2,1,0:T(1,128)S(1)}, u32[]{:S(2)}, u32[]{:S(2)}) %all-to-all-start.2) | async-done | bytes 544 | tf_op jit(solution)/shard_map/all_to_all | solution.py:109
  33.0 4.2 all-to-all-start
  38.7 6.8 %all-to-all-done = bf16[256,4,256]{2,0,1:T(8,128)(2,1)S(1)} async-done(((bf16[256,4,256]{2,0,1:T(8,128)(2,1)}), bf16[256,4,256]{2,0,1:T(8,128)(2,1)S(1)}, u32[]{:S(2)}, u32[]{:S(2)}) %all-to-all-start) | async-done | bytes 524320 | tf_op jit(solution)/shard_map/all_to_all | solution.py:68
  50.7 23.3 %all-to-all-done.1 = bf16[256,4,1024]{2,0,1:T(8,128)(2,1)S(1)} async-done(((bf16[256,4,1024]{2,0,1:T(8,128)(2,1)}), bf16[256,4,1024]{2,0,1:T(8,128)(2,1)S(1)}, u32[]{:S(2)}, u32[]{:S(2)}) %all-to-all-start.1) | async-done | bytes 2097184 | tf_op jit(solution)/shard_map/all_to_all | solution.py:67
  74.0 4.1 all-to-all-start.4
  81.1 4.2 broadcast_in_dim.116
  88.4 33.1 %scatter_fusion.1 = bf16[64,2,128,128]{3,2,1,0:T(8,128)(2,1)} fusion(bf16[64,2,128,128]{3,2,1,0:T(8,128)(2,1)} %broadcast_in_dim.115, s32[192]{0:T(256)S(1)} %bitcast.136, bf16[192,128,128]{2,1,0:T(8,128)(2,1)} %bitcast.140), kind=kCustom, calls=%fused_computation.9 | custom fusion | bytes 18875904 | tf_op jit(solution)/shard_map/scatter | solution.py:101
  121.6 7.6 %all-to-all-start.3 = ((bf16[64,2,128,128]{3,2,1,0:T(8,128)(2,1)}), bf16[64,2,128,128]{3,2,1,0:T(8,128)(2,1)}, u32[]{:S(2)}, u32[]{:S(2)}) async-start(bf16[64,2,128,128]{3,2,1,0:T(8,128)(2,1)} %scatter_fusion.1), calls=%async_computation.3 | async-start | bytes 8388608 | tf_op jit(solution)/shard_map/all_to_all | solution.py:108
  140.2 84.6 %all-to-all-done.3 = bf16[64,2,128,128]{3,2,1,0:T(8,128)(2,1)} async-done(((bf16[64,2,128,128]{3,2,1,0:T(8,128)(2,1)}), bf16[64,2,128,128]{3,2,1,0:T(8,128)(2,1)}, u32[]{:S(2)}, u32[]{:S(2)}) %all-to-all-start.3) | async-done | bytes 4194336 | tf_op jit(solution)/shard_map/all_to_all | solution.py:108
  224.8 5.2 %gather_fusion.2 = bf16[128,128,128]{2,1,0:T(8,128)(2,1)} fusion(bf16[128,128,128]{2,1,0:T(8,128)(2,1)} %bitcast.17, s32[1024]{0:T(1024)S(1)} %pad_clamp_fusion.2), kind=kCustom, calls=%fused_computation.2 | custom fusion | bytes 8389120 | tf_op jit(solution)/shard_map/gather | solution.py:123
  233.1 74.3 %while.12 = (s32[]{:T(128)}, bf16[128,128,128]{2,1,0:T(8,128)(2,1)}, f32[128,128]{1,0:T(8,128)S(1)}, s32[]{:T(128)}, bf16[128,128,128]{2,1,0:T(8,128)(2,1)}, /*i...) while((s32[]{:T(128)}, ...), condition=%wide.region_15.16_spmd, body=%wide.region_12.15_spmd.sunk | while | flops 1090780160 | bytes 68227592 | solution.py:145
  239.4 3.7 multiply_reduce_fusion.2
  254.2 3.7 multiply_reduce_fusion.2
  269.1 3.7 multiply_reduce_fusion.2
  283.9 3.7 multiply_reduce_fusion.2
  298.7 3.7 multiply_reduce_fusion.2
  308.6 32.9 %all-to-all-start.5 = ((f32[64,2,128]{2,1,0:T(2,128)}), f32[64,2,128]{2,1,0:T(2,128)S(1)}, u32[]{:S(2)}, u32[]{:S(2)}) async-start(f32[64,2,128]{2,1,0:T(2,128)} %bitcast.23), calls=%async_computation.5 | async-start | bytes 131072 | tf_op jit(solution)/shard_map/all_to_all | solution.py:150
  344.7 5.3 %gather_fusion.6 = bf16[128,128,128]{2,1,0:T(8,128)(2,1)} fusion(bf16[128,128,128]{2,1,0:T(8,128)(2,1)} %get-tuple-element.50, s32[1024]{0:T(1024)S(1)} %pad_clamp_fusion.1), kind=kCustom, calls=%fused_computation.6 | custom fusion | bytes 8389120 | tf_op jit(solution)/shard_map/gather | solution.py:147
  350.3 10.8 %all-to-all-start.6 = ((bf16[64,2,128,128]{3,2,1,0:T(8,128)(2,1)}), bf16[64,2,128,128]{3,2,1,0:T(8,128)(2,1)}, u32[]{:S(2)}, u32[]{:S(2)}) async-start(bf16[64,2,128,128]{3,2,1,0:T(8,128)(2,1)} %bitcast.145), calls=%async_computation.6 | async-start | bytes 8388608 | tf_op jit(solution)/shard_map/all_to_all | solution.py:149
  368.0 7.5 %fusion.9 = (f32[4,1024]{1,0:T(4,128)S(1)}, f32[1024,1024,4]{1,0,2:T(8,128)}) fusion(pred[1024,1024]{0,1:T(8,128)(4,1)S(1)} %copy-done.6, bf16[1024,4,128]{2,1,0:T(4,128)(2,1)S(1)} %get-tuple-element.106, bf16[1024,1,128]{2,1,0:T(2,128)(2,1)S(1)} %get-tuple-element.110), kind=kOutput, calls=%fused_computation.33 | convolution fusion | flops 1086320640 | bytes 19152896 | tf_op jit(solution)/shard_map/shd,kd->hsk/dot_general | solution.py:39
  375.6 13.5 %exponential_reduce_fusion.2 = (f32[4,1024]{1,0:T(4,128)S(1)}, f32[4,1024]{1,0:T(4,128)S(1)}, f32[1024,1024,4]{1,0,2:T(8,128)}) fusion(f32[1024,1024,4]{1,0,2:T(8,128)} %get-tuple-element.114, f32[4,1024]{1,0:T(4,128)S(1)} %get-tuple-element.113, pred[1024,1024]{0,1:T(8,128)(4,1)S(1)} %copy-done.6, bf16[1024,4,128]{2,1,0:T(4,128)(2,1)S(1)} %get-tuple-element.105, ...), kind=kOutput, calls=%fused_computation.32 | convolution fusion | flops 1103093760 | bytes 35962880 | tf_op jit(solution)/shard_map/shd,kd->hsk/dot_general | solution.py:39
  389.1 9.2 %exponential_reduce_fusion.1 = f32[4,1024]{1,0:T(4,128)S(1)} fusion(f32[1024,1024,4]{1,0,2:T(8,128)} %get-tuple-element.115, f32[4,1024]{1,0:T(4,128)S(1)} %get-tuple-element.76, pred[1024,1024]{0,1:T(8,128)(4,1)S(1)} %copy-done.6), kind=kLoop, calls=%fused_computation.31 | loop fusion | flops 16773120 | bytes 17858560 | tf_op jit(solution)/shard_map/reduce_sum | solution.py:49
  398.4 8.2 %fusion.19 = f32[1024,4,128]{2,0,1:T(8,128)S(1)} fusion(f32[1024,1024,4]{1,0,2:T(8,128)} %get-tuple-element.114, f32[4,1024]{1,0:T(4,128)S(1)} %get-tuple-element.117, pred[1024,1024]{0,1:T(8,128)(4,1)S(1)} %copy-done.6, bf16[1024,1,128]{2,1,0:T(2,128)(2,1)S(1)} %copy-done.10), kind=kOutput, calls=%fused_computation.50 | convolution fusion | flops 1090519040 | bytes 20201472 | tf_op jit(solution)/shard_map/hsk,kd->shd/dot_general | solution.py:52
  406.6 5.6 %fusion.18 = f32[1024,4,128]{2,0,1:T(8,128)} fusion(f32[1024,1024,4]{1,0,2:T(8,128)S(1)} %bitcast.144, f32[4,1024]{1,0:T(4,128)S(1)} %get-tuple-element.116, pred[1024,1024]{0,1:T(8,128)(4,1)S(1)} %copy-done.6, bf16[1024,1,128]{2,1,0:T(2,128)(2,1)S(1)} %copy-done.9), kind=kOutput, calls=%fused_computation.49 | convolution fusion | flops 1090519040 | bytes 20201472 | tf_op jit(solution)/shard_map/hsk,kd->shd/dot_general | solution.py:52
  412.2 4.2 pad_maximum_fusion
  418.8 37.9 %all-to-all-done.6 = bf16[64,2,128,128]{3,2,1,0:T(8,128)(2,1)} async-done(((bf16[64,2,128,128]{3,2,1,0:T(8,128)(2,1)}), bf16[64,2,128,128]{3,2,1,0:T(8,128)(2,1)}, u32[]{:S(2)}, u32[]{:S(2)}) %all-to-all-start.6) | async-done | bytes 4194336 | tf_op jit(solution)/shard_map/all_to_all | solution.py:149
  456.6 11.0 %gather_fusion.7 = bf16[192,128,128]{2,1,0:T(8,128)(2,1)} fusion(bf16[64,2,128,128]{3,2,1,0:T(8,128)(2,1)} %all-to-all-done.6, s32[192]{0:T(256)S(1)} %bitcast.138), kind=kCustom, calls=%fused_computation.7 | custom fusion | bytes 12584448 | tf_op jit(solution)/shard_map/gather | solution.py:154
  467.7 5.9 %fusion.11 = f32[8,8,128,128]{3,2,1,0:T(8,128)S(1)} fusion(bf16[8,8,3,128,128]{4,3,2,1,0:T(8,128)(2,1)} %bitcast.139, f32[8,8,3,128]{3,2,1,0:T(4,128)S(1)} %get-tuple-element.102), kind=kLoop, calls=%fused_computation.36 | loop fusion | flops 8388608 | bytes 10584064 | tf_op jit(solution)/shard_map/reduce_sum | solution.py:167
  479.8 30.4 %all_to_all.88 = bf16[4,256,1024]{2,1,0:T(8,128)(2,1)S(1)} all-to-all(bf16[4,256,1024]{2,1,0:T(8,128)(2,1)} %convert_element_type.52), channel_id=1, replica_groups=mesh['ctx'=64,'head'=4] {'head'}, dimensions={0} | all-to-all | bytes 4194304 | tf_op jit(solution)/shard_map/all_to_all | solution.py:176
  512.8 4.1 copy.103
  (145 shorter events, 109.2 us)
Async XLA Ops:
  0.0 37.2 %copy-start.7 = (bf16[256,4096]{1,0:T(8,128)(2,1)S(1)}, bf16[256,4096]{1,0:T(8,128)(2,1)}, u32[]{:S(2)}) copy-start(bf16[256,4096]{1,0:T(8,128)(2,1)} %param.6) | copy-start | bytes 6291460
  12.4 20.6 %all-to-all-start.2 = ((s32[64,1,2]{2,1,0:T(1,128)}), s32[64,1,2]{2,1,0:T(1,128)S(1)}, u32[]{:S(2)}, u32[]{:S(2)}) async-start(s32[64,1,2]{2,1,0:T(1,128)} %copy.88), calls=%async_computation.2 | async-start | bytes 65536 | tf_op jit(solution)/shard_map/all_to_all | solution.py:109
  33.0 12.5 %all-to-all-start = ((bf16[256,4,256]{2,0,1:T(8,128)(2,1)}), bf16[256,4,256]{2,0,1:T(8,128)(2,1)S(1)}, u32[]{:S(2)}, u32[]{:S(2)}) async-start(bf16[256,4,256]{2,0,1:T(8,128)(2,1)} %bitcast.125), calls=%async_computation | async-start | bytes 1048576 | tf_op jit(solution)/shard_map/all_to_all | solution.py:68
  37.2 12.7 %copy-start.8 = (bf16[256,1024]{1,0:T(8,128)(2,1)S(1)}, bf16[256,1024]{1,0:T(8,128)(2,1)}, u32[]{:S(2)}) copy-start(bf16[256,1024]{1,0:T(8,128)(2,1)} %param.8) | copy-start | bytes 1572868
  45.5 0.8 copy-start.3
  46.3 27.8 %all-to-all-start.1 = ((bf16[256,4,1024]{2,0,1:T(8,128)(2,1)}), bf16[256,4,1024]{2,0,1:T(8,128)(2,1)S(1)}, u32[]{:S(2)}, u32[]{:S(2)}) async-start(bf16[256,4,1024]{2,0,1:T(8,128)(2,1)} %bitcast.148), calls=%async_computation.1 | async-start | bytes 4194304 | tf_op jit(solution)/shard_map/all_to_all | solution.py:67
  74.0 4.2 copy-start.2
  74.0 47.5 %all-to-all-start.4 = ((bf16[256,4,256]{2,0,1:T(8,128)(2,1)}), bf16[256,4,256]{2,0,1:T(8,128)(2,1)}, u32[]{:S(2)}, u32[]{:S(2)}) async-start(bf16[256,4,256]{2,0,1:T(8,128)(2,1)} %bitcast.124), calls=%async_computation.4 | async-start | bytes 1048576 | tf_op jit(solution)/shard_map/all_to_all | solution.py:69
  121.5 7.6 %copy-start.11 = (s32[8,8,3]{1,0,2:T(8,128)S(1)}, s32[8,8,3]{1,0,2:T(8,128)}, u32[]{:S(2)}) copy-start(s32[8,8,3]{1,0,2:T(8,128)} %param.9) | copy-start | bytes 2308
  121.5 13.6 %copy-start.4 = (bf16[256,4,256]{2,0,1:T(8,128)(2,1)S(1)}, bf16[256,4,256]{2,0,1:T(8,128)(2,1)}, u32[]{:S(2)}) copy-start(bf16[256,4,256]{2,0,1:T(8,128)(2,1)} %copy-done.3) | copy-start | bytes 1572868
  121.6 103.3 %all-to-all-start.3 = ((bf16[64,2,128,128]{3,2,1,0:T(8,128)(2,1)}), bf16[64,2,128,128]{3,2,1,0:T(8,128)(2,1)}, u32[]{:S(2)}, u32[]{:S(2)}) async-start(bf16[64,2,128,128]{3,2,1,0:T(8,128)(2,1)} %scatter_fusion.1), calls=%async_computation.3 | async-start | bytes 8388608 | tf_op jit(solution)/shard_map/all_to_all | solution.py:108
  243.1 2.2 copy-start
  257.9 2.2 copy-start
  272.8 2.2 copy-start
  287.6 2.2 copy-start
  302.4 2.2 copy-start
  308.6 41.7 %all-to-all-start.5 = ((f32[64,2,128]{2,1,0:T(2,128)}), f32[64,2,128]{2,1,0:T(2,128)S(1)}, u32[]{:S(2)}, u32[]{:S(2)}) async-start(f32[64,2,128]{2,1,0:T(2,128)} %bitcast.23), calls=%async_computation.5 | async-start | bytes 131072 | tf_op jit(solution)/shard_map/all_to_all | solution.py:150
  350.3 13.9 %copy-start.5 = (bf16[256,4,256]{2,0,1:T(8,128)(2,1)S(1)}, bf16[256,4,256]{2,0,1:T(8,128)(2,1)}, u32[]{:S(2)}) copy-start(bf16[256,4,256]{2,0,1:T(8,128)(2,1)} %copy-done.3) | copy-start | bytes 1572868
  350.3 106.3 %all-to-all-start.6 = ((bf16[64,2,128,128]{3,2,1,0:T(8,128)(2,1)}), bf16[64,2,128,128]{3,2,1,0:T(8,128)(2,1)}, u32[]{:S(2)}, u32[]{:S(2)}) async-start(bf16[64,2,128,128]{3,2,1,0:T(8,128)(2,1)} %bitcast.145), calls=%async_computation.6 | async-start | bytes 8388608 | tf_op jit(solution)/shard_map/all_to_all | solution.py:149
  365.2 2.9 copy-start.6
  389.1 9.3 %copy-start.10 = (bf16[1024,1,128]{2,1,0:T(2,128)(2,1)S(1)}, bf16[1024,1,128]{2,1,0:T(2,128)(2,1)}, u32[]{:S(2)}) copy-start(bf16[1024,1,128]{2,1,0:T(2,128)(2,1)} %get-tuple-element.107) | copy-start | bytes 786436
  389.1 17.5 %slice-start = ((s8[16777216]{0:T(1024)(128)(4,1)}), s8[4194304]{0:T(1024)(128)(4,1)S(1)}, s32[]{:S(2)}) async-start(s8[16777216]{0:T(1024)(128)(4,1)} %bitcast.143), calls=%async_computation.8 | async-start | bytes 8388608
  389.1 17.5 %slice-start.1 = ((s8[16777216]{0:T(1024)(128)(4,1)}), s8[4194304]{0:T(1024)(128)(4,1)S(1)}, s32[]{:S(2)}) async-start(s8[16777216]{0:T(1024)(128)(4,1)} %bitcast.143), calls=%async_computation.9 | async-start | bytes 8388608
  398.4 8.2 %slice-start.2 = ((s8[16777216]{0:T(1024)(128)(4,1)}), s8[4194304]{0:T(1024)(128)(4,1)S(1)}, s32[]{:S(2)}) async-start(s8[16777216]{0:T(1024)(128)(4,1)} %bitcast.143), calls=%async_computation.10 | async-start | bytes 8388608
  398.4 8.2 %slice-start.3 = ((s8[16777216]{0:T(1024)(128)(4,1)}), s8[4194304]{0:T(1024)(128)(4,1)S(1)}, s32[]{:S(2)}) async-start(s8[16777216]{0:T(1024)(128)(4,1)} %bitcast.143), calls=%async_computation.11 | async-start | bytes 8388608
  398.4 8.2 %copy-start.9 = (bf16[1024,1,128]{2,1,0:T(2,128)(2,1)S(1)}, bf16[1024,1,128]{2,1,0:T(2,128)(2,1)}, u32[]{:S(2)}) copy-start(bf16[1024,1,128]{2,1,0:T(2,128)(2,1)} %get-tuple-element.108) | copy-start | bytes 786436
  467.7 5.9 %copy-start.1 = (f32[1024,8,128]{2,0,1:T(8,128)S(1)}, f32[1024,8,128]{2,0,1:T(8,128)}, u32[]{:S(2)}) copy-start(f32[1024,8,128]{2,0,1:T(8,128)} %pad_maximum_fusion) | copy-start | bytes 12582916
where the time goes:
time: 527 us; the launch traced here: 517 us
  waiting for transfers between devices  159 us (30%)
  local copies, waits for them, and re-layouts  147 us (28%)
  starting transfers between devices  75.6 us (14%)
  matrix products  67 us (13%)
  other arithmetic  35.9 us (7%)
  blocking collectives  30.4 us (6%)
    all_to_all x1, waiting for transfers between devices, local(): lax.all_to_all(send_rows, 'ctx', split_axis=0, concat_axis=0, tiled=True)  84.6 us
    all_to_all x1, waiting for transfers between devices, local(): lax.all_to_all(item_out, 'ctx', split_axis=0, concat_axis=0, tiled=True)  37.9 us
    scatter x1, local copies, waits for them, and re-layouts, local(): send_rows = jnp.zeros((ctx_count, CAP, TILE, HEAD_DIM), jnp.bfloat16).at[...  33.1 us
    all_to_all x1, starting transfers between devices, local(): lax.all_to_all(item_log, 'ctx', split_axis=0, concat_axis=0, tiled=True)  32.9 us
    all_to_all x1, blocking collectives, local(): lax.all_to_all(merged, 'head', split_axis=0, concat_axis=1, tiled=True)  30.4 us
    all_to_all x1, waiting for transfers between devices, local(): lax.all_to_all(queries, 'head', split_axis=1, concat_axis=0, tiled=True)  23.3 us
    dot_general x2, matrix products, own_block(): jnp.einsum('shd,kd->hsk', query_part, key_all[:, kv_index, :], preferred_...  21 us
    dot_general x5, matrix products, attend_rows(): jnp.einsum('gsd,gkd->gsk', query_rows, key_block, preferred_element_type=...  18.4 us
  transfers between devices with their start and end apart: 7, of which 6 were waited for; matrix products, arithmetic and copies ran while one was open for 24% of the time, Pallas kernels for 0%

commit v1 on v0

v1 whole, which is shorter than its diff:
```python
import math

import jax
import jax.numpy as jnp
from jax import lax
from jax.experimental import pallas as pl
from jax.experimental.pallas import tpu as pltpu
from jax.sharding import PartitionSpec as P

HEAD_DIM = 128
TILE = 128
CAP = 2
N_HEAD = 4
ROW = 16
R = TILE
SLOTS = 5
GROUP = 4
EXTRA = 16
SEND = (2 * R + EXTRA, 3 * R + EXTRA)
LOG_AT = 2 * R
FAR = 2 * R + EXTRA
NEAR = EXTRA + R
FIRST = SEND[1]
FAR_AT = FIRST + SEND[0]
NEAR_AT = FAR_AT + FAR
UNUSED = NEAR_AT + NEAR
SCALE = HEAD_DIM**-0.5
SCALE2 = SCALE * math.log2(math.e)
NEG = -1e30
F32 = jnp.float32
BF16 = jnp.bfloat16
I32 = jnp.int32

SMEM = pl.BlockSpec(memory_space=pltpu.SMEM)
VMEM = pl.BlockSpec(memory_space=pltpu.VMEM)
HBM = pl.BlockSpec(memory_space=pltpu.HBM)


def params(mib):
    return pltpu.CompilerParams(vmem_limit_bytes=mib * 2**20)


def cost(flops, data, exps=0):
    return pl.CostEstimate(flops=flops, bytes_accessed=data, transcendentals=exps)


def shaped(shape, kind=BF16):
    return jax.ShapeDtypeStruct(shape, kind)


def run_copies(pairs, sems):
    copies = [pltpu.make_async_copy(a, b, sems.at[i]) for i, (a, b) in enumerate(pairs)]
    for copy in copies:
        copy.start()
    return copies


def plan_kernel(gates, table, place):
    def clear(i, _):
        table[2 * i] = -1
        table[2 * i + 1] = -1
        return 0

    def note(e, _):
        b = gates[e]
        place[e] = -1

        @pl.when(b >= 0)
        def _():
            at = 2 * b + (table[2 * b] >= 0).astype(I32)
            table[at] = e
            place[e] = at

        return 0

    lax.fori_loop(0, table.shape[0] // 2, clear, 0)
    lax.fori_loop(0, gates.shape[0], note, 0)


def plan(gates, blocks):
    return pl.pallas_call(
        plan_kernel,
        out_shape=(shaped((blocks * CAP,), I32), shaped(gates.shape, I32)),
        in_specs=[SMEM],
        out_specs=(SMEM, SMEM),
        compiler_params=params(4),
        name="plan",
    )(gates)


def split_body(meta, ins, outs, sems):
    pairs = []
    for step in range(N_HEAD):
        g = lax.rem(meta[1] + step, N_HEAD)
        at = 0
        for ref in ins:
            wide = ref.shape[1] // N_HEAD
            cols = pl.ds(pl.multiple_of(g * wide, 128), wide)
            pairs.append((ref.at[:, cols], outs[step].at[:, pl.ds(at, wide)]))
            at += wide
    for copy in run_copies(pairs, sems):
        copy.wait()


def split(meta, ins, *earlier):
    rows, wide = ins[0].shape[0], sum(x.shape[1] for x in ins) // N_HEAD

    def kernel(meta, *refs):
        n = len(ins)
        split_body(meta, refs[:n], refs[n + len(earlier) : -1], refs[-1])

    return pl.pallas_call(
        kernel,
        out_shape=[shaped((rows, wide))] * N_HEAD,
        in_specs=[SMEM] + [HBM] * (len(ins) + len(earlier)),
        out_specs=[VMEM] * N_HEAD,
        scratch_shapes=[pltpu.SemaphoreType.DMA((N_HEAD * len(ins),))],
        compiler_params=params(56),
        cost_estimate=cost(0, 4 * rows * wide * N_HEAD),
        name="split",
    )(meta, *ins, *earlier)


def over_head(parts):
    got = [parts[0]]
    for step in range(1, N_HEAD):
        pairs = [(y, (y + step) % N_HEAD) for y in range(N_HEAD)]
        got.append(lax.ppermute(parts[step], "head", pairs))
    return got


def by_source(y, refs, whole):
    size = refs[0].shape[0]
    pairs = []
    for step, ref in enumerate(refs):
        source = lax.rem(y - step + N_HEAD, N_HEAD)
        pairs.append((ref, whole.at[pl.ds(pl.multiple_of(source * size, 16), size)]))
    return pairs


def join_kernel(meta, *refs):
    pieces, whole, sems = refs[:N_HEAD], refs[N_HEAD], refs[N_HEAD + 1]
    for copy in run_copies(by_source(meta[1], pieces, whole), sems):
        copy.wait()


def join(meta, pieces):
    rows, cols = pieces[0].shape
    return pl.pallas_call(
        join_kernel,
        out_shape=shaped((N_HEAD * rows, cols)),
        in_specs=[SMEM] + [HBM] * N_HEAD,
        out_specs=VMEM,
        scratch_shapes=[pltpu.SemaphoreType.DMA((N_HEAD,))],
        compiler_params=params(6),
        cost_estimate=cost(0, 4 * N_HEAD * rows * cols),
        name="join",
    )(meta, *pieces)


def pack_kernel(meta, table, q0, q1, q2, q3, *refs):
    outs, boxes, q_all, sems = refs[:4], refs[4:8], refs[8], refs[9]
    me = meta[0] // ROW
    for copy in run_copies(by_source(meta[1], (q0, q1, q2, q3), q_all), sems):
        copy.wait()
    lane = lax.broadcasted_iota(I32, (EXTRA, 128), 1)

    def entry(j, target, rank):
        return table[2 * (jnp.maximum(target, 0) * ROW + j) + rank]

    def fill(into, j, row, target, rank):
        e = entry(j, target, rank)

        @pl.when(jnp.logical_and(target >= 0, e >= 0))
        def _():
            tile = lax.div(e, 24)
            head = lax.rem(lax.div(e, 3), 8)
            into[j, row : row + R, :] = q_all[
                pl.ds(pl.multiple_of(tile * R, R), R),
                pl.ds(pl.multiple_of(head * HEAD_DIM, HEAD_DIM), HEAD_DIM),
            ]

    def codes(j, *slots):
        marks = jnp.full((EXTRA, 128), -1, I32)
        for slot, target, rank in slots:
            e = entry(j, target, rank)
            kv_head = lax.div(lax.rem(lax.div(e, 3), 8), 4)
            code = jnp.where(jnp.logical_and(target >= 0, e >= 0), kv_head, -1)
            marks = jnp.where(lane == slot, code, marks)
        return marks.astype(F32).astype(BF16)

    z1, z2, far, near = boxes
    split_row = jnp.where(me == 3, 1, me - 1)

    def own_row(j, _):
        fill(z1, j, 0, me, 0)
        fill(z1, j, R, me, 1)
        z1[j, 2 * R :, :] = codes(j, (0, me, 0), (1, me, 1))
        return 0

    def moved(j, _):
        fill(far, j, 0, 0, 0)
        fill(far, j, R, 0, 1)
        far[j, 2 * R :, :] = codes(j, (2, 0, 0), (3, 0, 1))
        fill(near, j, 0, split_row, 1)
        near[j, R:, :] = codes(j, (4, split_row, 1))
        return 0

    def other_rows(j, _):
        fill(z2, j, 0, me - 1, 0)
        fill(z2, j, R, me - 1, 1)
        fill(z2, j, 2 * R, split_row, 0)
        z2[j, 3 * R :, :] = codes(j, (2, me - 1, 0), (3, me - 1, 1), (4, split_row, 0))
        return 0

    saves = []
    for work, group in ((moved, (2, 3)), (own_row, (0,)), (other_rows, (1,))):
        lax.fori_loop(0, ROW, work, 0)
        for i in group:
            saves.append(pltpu.make_async_copy(boxes[i], outs[i], sems.at[N_HEAD + i]))
            saves[-1].start()
    for save in saves:
        save.wait()


def pack(meta, table, q_parts):
    rows, wide = q_parts[0].shape
    sizes = (SEND[0], SEND[1], FAR, NEAR)
    return pl.pallas_call(
        pack_kernel,
        out_shape=[shaped((ROW, size, HEAD_DIM)) for size in sizes],
        in_specs=[SMEM, SMEM] + [HBM] * N_HEAD,
        out_specs=[HBM] * len(sizes),
        scratch_shapes=[pltpu.VMEM((ROW, size, HEAD_DIM), BF16) for size in sizes]
        + [
            pltpu.VMEM((N_HEAD * rows, wide), BF16),
            pltpu.SemaphoreType.DMA((N_HEAD + len(sizes),)),
        ],
        compiler_params=params(56),
        cost_estimate=cost(0, 2 * (N_HEAD * rows * wide + ROW * sum(sizes) * HEAD_DIM)),
        name="pack",
    )(meta, table, *q_parts)


def insert_kernel(meta, z_in, far, near, *refs):
    z, box, marks, sems = refs[-4:]
    me = meta[0] // ROW
    two, four, last = pl.ds(0, 2 * R), pl.ds(2 * R, R), pl.ds(3 * R, EXTRA)
    has_far, has_near = me <= 1, jnp.logical_or(me == 0, me == 2)
    reads = (
        (jnp.logical_not(has_far), z_in.at[:, two], box.at[:, two], sems.at[0]),
        (has_far, far.at[:, two], box.at[:, two], sems.at[0]),
        (jnp.logical_not(has_near), z_in.at[:, four], box.at[:, four], sems.at[1]),
        (has_near, near.at[:, pl.ds(0, R)], box.at[:, four], sems.at[1]),
    )
    for cond, source, target, sem in reads:

        @pl.when(cond)
        def _(source=source, target=target, sem=sem):
            pltpu.make_async_copy(source, target, sem).start()

    loads = [
        pltpu.make_async_copy(source, marks.at[i], sems.at[2 + i])
        for i, source in enumerate(
            (z_in.at[:, last], far.at[:, pl.ds(2 * R, EXTRA)], near.at[:, pl.ds(R, EXTRA)])
        )
    ]
    for load in loads:
        load.start()
    for load in loads:
        load.wait()
    lane = lax.broadcasted_iota(I32, (EXTRA, 128), 1)
    from_far = jnp.logical_and(lane < 4, me <= 1)
    from_near = jnp.logical_and(lane == 4, lax.rem(me, 2) == 0)
    for j in range(ROW):
        mine, theirs, one = (marks[i, j].astype(F32) for i in range(3))
        mine = jnp.where(from_far, theirs, jnp.where(from_near, one, mine))
        box[j, 3 * R :, :] = mine.astype(BF16)
    saves = []
    for i, region in enumerate((two, four, last)):
        if i < 2:
            pltpu.make_async_copy(z_in.at[:, region], box.at[:, region], sems.at[i]).wait()
        saves.append(pltpu.make_async_copy(box.at[:, region], z.at[:, region], sems.at[5 + i]))
        saves[-1].start()
    for save in saves:
        save.wait()


def insert(meta, z, far, near, *earlier):
    return pl.pallas_call(
        insert_kernel,
        out_shape=shaped(z.shape),
        in_specs=[SMEM] + [HBM] * (3 + len(earlier)),
        out_specs=HBM,
        scratch_shapes=[
            pltpu.VMEM(z.shape, BF16),
            pltpu.VMEM((3, ROW, EXTRA, 128), BF16),
            pltpu.SemaphoreType.DMA((8,)),
        ],
        compiler_params=params(8),
        cost_estimate=cost(0, 4 * z.size),
        name="insert",
    )(meta, z, far, near, *earlier)


def cut_kernel(back, far, near, sems):
    pairs = [
        (back.at[:, pl.ds(0, FAR)], far),
        (back.at[:, pl.ds(LOG_AT, NEAR)], near),
    ]
    for copy in run_copies(pairs, sems):
        copy.wait()


def cut(back):
    return pl.pallas_call(
        cut_kernel,
        out_shape=(shaped((ROW, FAR, HEAD_DIM)), shaped((ROW, NEAR, HEAD_DIM))),
        in_specs=[HBM],
        out_specs=(VMEM, VMEM),
        scratch_shapes=[pltpu.SemaphoreType.DMA((2,))],
        compiler_params=params(6),
        cost_estimate=cost(0, 4 * ROW * (FAR + NEAR) * HEAD_DIM),
        name="cut",
    )(back)


def dot_t(a, b):
    return lax.dot_general(a, b, (((1,), (1,)), ((), ())), preferred_element_type=F32)


def dot(a, b):
    return lax.dot_general(a, b, (((1,), (0,)), ((), ())), preferred_element_type=F32)


def to_row(log):
    lane = lax.broadcasted_iota(I32, (R, R), 1)
    row = lax.broadcasted_iota(I32, (R, R), 0)
    wide = jnp.broadcast_to(log, (R, R))
    return jnp.sum(jnp.where(lane == row, wide, 0.0), axis=0, keepdims=True)


def attend(q, keys, values):
    scores = dot_t(q, keys)
    top = jnp.max(scores, axis=-1, keepdims=True)
    weights = jnp.exp2((scores - top) * SCALE2)
    total = jnp.sum(weights, axis=-1, keepdims=True)
    mixed = dot(weights.astype(BF16), values) / total
    return mixed, top * SCALE + jnp.log(total)


def gate_kernel(part, meta, *refs):
    n_kv = 3 if part else 1
    z, kvs, out = refs[0], refs[1 : 1 + n_kv], refs[1 + n_kv]
    kv, logs, codes, lists, counts, marks, sems = refs[2 + n_kv :]
    me = meta[0] // ROW
    copies = run_copies([(kvs[i], kv.at[i]) for i in range(n_kv)], sems)
    for j in range(ROW):
        marks[j : j + 1, :] = z[j, SEND[part] - EXTRA :, :].astype(F32)[:1].astype(I32)
    known = pltpu.make_async_copy(marks, codes, sems.at[n_kv])
    known.start()
    known.wait()
    groups = ((2, 3), (4,)) if part else ((0, 1),)
    for i in range(2 * len(groups)):
        counts[i] = 0

    def scan(j, _):
        for group, slots in enumerate(groups):
            for slot in slots:
                code = codes[j, slot]

                @pl.when(code >= 0)
                def _(group=group, slot=slot, code=code):
                    i = 2 * group + code
                    n = counts[i]
                    lists[i, n] = j * 8 + slot
                    counts[i] = n + 1

        return 0

    lax.fori_loop(0, ROW, scan, 0)
    for copy in copies:
        copy.wait()
    stores = (jnp.where(me == 0, 0, 1), jnp.where(me == 0, 0, jnp.where(me == 3, 2, 1)))
    for i in range(2 * len(groups)):
        store, kv_head = stores[i // 2] if part else 0, i % 2
        count = counts[i]

        def batch(n, _, i=i, store=store, kv_head=kv_head, count=count):
            keys = kv[store, :, kv_head * HEAD_DIM : (kv_head + 1) * HEAD_DIM]
            values = kv[store, :, (2 + kv_head) * HEAD_DIM : (3 + kv_head) * HEAD_DIM]
            where = []
            for u in range(GROUP):
                item = lists[i, jnp.minimum(n * GROUP + u, count - 1)]
                where.append((lax.div(item, 8), lax.rem(item, 8)))
            done = []
            for u in range(0, GROUP, 2):
                q = [
                    z[j, pl.ds(pl.multiple_of((s - 2 * part) * R, R), R), :]
                    for j, s in where[u : u + 2]
                ]
                done.append(attend(jnp.concatenate(q, axis=0), keys, values))
            for u, (j, s) in enumerate(where):
                mixed, log = done[u // 2]
                rows = slice(u % 2 * R, (u % 2 + 1) * R)
                at = (s - 2 * part) * R + jnp.where(s >= 4, EXTRA, 0)
                out[j, pl.ds(pl.multiple_of(at, 16), R), :] = mixed[rows].astype(BF16)
                log = to_row(log[rows])
                high = log.astype(BF16).astype(F32)
                logs[j, pl.ds(s, 1), :] = high
                logs[j, pl.ds(8 + s, 1), :] = log - high
            return 0

        lax.fori_loop(0, lax.div(count + GROUP - 1, GROUP), batch, 0)
    for j in range(ROW):
        out[j, LOG_AT : LOG_AT + EXTRA, :] = logs[j].astype(BF16)


def gate(meta, part, z, kvs, *held):
    keys = kvs[0].shape[0]
    items = ROW * (2 + part)
    n_kv = len(kvs)

    def kernel(*refs):
        ins = 2 + n_kv + len(held)
        gate_kernel(part, *refs[: 2 + n_kv], refs[ins], *refs[ins + 1 + len(held) :])

    return pl.pallas_call(
        kernel,
        out_shape=[shaped((ROW, SEND[part], HEAD_DIM))] + [shaped(x.shape) for x in held],
        in_specs=[SMEM, VMEM] + [HBM] * (n_kv + len(held)),
        out_specs=[VMEM] + [HBM] * len(held),
        input_output_aliases={2 + n_kv + i: 1 + i for i in range(len(held))},
        scratch_shapes=[
            pltpu.VMEM((n_kv,) + kvs[0].shape, BF16),
            pltpu.VMEM((ROW, 16, 128), F32),
            pltpu.SMEM((ROW, 128), I32),
            pltpu.SMEM((4, ROW * CAP), I32),
            pltpu.SMEM((8,), I32),
            pltpu.VMEM((ROW, 128), I32),
            pltpu.SemaphoreType.DMA((n_kv + 1,)),
        ],
        compiler_params=params(56),
        cost_estimate=cost(4 * items * R * keys * HEAD_DIM, 8 * 2**20, items * R * keys),
        name="gate",
    )(meta, z, *kvs, *held)


def own_kernel(meta, q0, q1, q2, q3, kv, out0, out1, log0, log1, q_all, sems):
    for copy in run_copies(by_source(meta[1], (q0, q1, q2, q3), q_all), sems):
        copy.wait()
    tiles = q_all.shape[0] // R
    heads = q_all.shape[1] // HEAD_DIM
    row = lax.rem(lax.broadcasted_iota(I32, (2 * R, TILE), 0), R)
    seen = row >= lax.broadcasted_iota(I32, (2 * R, TILE), 1)
    for tile in range(tiles):
        rows = slice(tile * R, (tile + 1) * R)
        past, now = slice(0, tile * TILE), slice(tile * TILE, (tile + 1) * TILE)
        out, logs = (out0, log0) if tile % 2 == 0 else (out1, log1)
        to = slice(tile // 2 * R, (tile // 2 + 1) * R)
        for pair in range(0, heads, 2):
            kv_head = pair // (heads // 2)
            q = jnp.concatenate(
                [q_all[rows, h * HEAD_DIM : (h + 1) * HEAD_DIM] for h in (pair, pair + 1)], axis=0
            )
            k_col = slice(kv_head * HEAD_DIM, (kv_head + 1) * HEAD_DIM)
            v_col = slice((2 + kv_head) * HEAD_DIM, (3 + kv_head) * HEAD_DIM)
            near = jnp.where(seen, dot_t(q, kv[now, k_col]), NEG)
            top = jnp.max(near, axis=-1, keepdims=True)
            if tile:
                far = dot_t(q, kv[past, k_col])
                top = jnp.maximum(top, jnp.max(far, axis=-1, keepdims=True))
            near = jnp.exp2((near - top) * SCALE2)
            total = jnp.sum(near, axis=-1, keepdims=True)
            mixed = dot(near.astype(BF16), kv[now, v_col])
            if tile:
                far = jnp.exp2((far - top) * SCALE2)
                total = total + jnp.sum(far, axis=-1, keepdims=True)
                mixed = mixed + dot(far.astype(BF16), kv[past, v_col])
            mixed = mixed / total
            log = top * SCALE + jnp.log(total)
            for u in range(2):
                head = pair + u
                out[to, head * HEAD_DIM : (head + 1) * HEAD_DIM] = mixed[u * R : (u + 1) * R]
                at = tile // 2 * heads + head
                logs[at : at + 1, :] = to_row(log[u * R : (u + 1) * R])


def own(meta, q_parts, kv):
    rows, wide = q_parts[0].shape
    rows = N_HEAD * rows
    units = rows * wide // HEAD_DIM
    out, logs = shaped((rows // 2, wide), F32), shaped((units // R // 2, 128), F32)
    return pl.pallas_call(
        own_kernel,
        out_shape=(out, out, logs, logs),
        in_specs=[SMEM] + [HBM] * N_HEAD + [VMEM],
        out_specs=(VMEM, VMEM, VMEM, VMEM),
        scratch_shapes=[pltpu.VMEM((rows, wide), BF16), pltpu.SemaphoreType.DMA((N_HEAD,))],
        compiler_params=params(56),
        cost_estimate=cost(4 * units * 640 * HEAD_DIM, 8 * 2**20, units * 640),
        name="own",
    )(meta, *q_parts, kv)


def merge_kernel(
    half, meta, place, far_back, z_back, farb, nearb, own_ref, own_log,
    o0, o1, o2, o3, items, logs, got, done, sems
):
    me, y = meta[0] // ROW, meta[1]
    copies = run_copies(
        [
            (far_back, items.at[:, pl.ds(0, SEND[1])]),
            (z_back, items.at[:, pl.ds(FIRST, SEND[0])]),
            (farb, items.at[:, pl.ds(FAR_AT, FAR)]),
            (nearb, items.at[:, pl.ds(NEAR_AT, NEAR)]),
        ],
        sems,
    )
    heads = own_ref.shape[1] // HEAD_DIM
    items[0, UNUSED : UNUSED + R, :] = jnp.zeros((R, HEAD_DIM), BF16)
    logs[0, 32:40, :] = jnp.full((8, 128), NEG, F32)
    for copy in copies:
        copy.wait()
    for j in range(ROW):
        for group, at in enumerate((LOG_AT, FIRST + LOG_AT, FAR_AT + LOG_AT, NEAR_AT)):
            halves = items[j, at : at + EXTRA, :].astype(F32)
            logs[j, 8 * group : 8 * group + 8, :] = halves[:8] + halves[8:]

    def each(pair, _):
        rows = pl.ds(pl.multiple_of(pair * R, R), R)
        where = {}
        for head in range(heads):
            for k in range(3):
                at = place[((2 * pair + half) * heads + head) * 3 + k]
                live = at >= 0
                rank = lax.rem(at, 2)
                j = jnp.where(live, lax.rem(lax.div(at, 2), ROW), 0)
                away = me - lax.div(at, 2 * ROW)
                target = me - away
                far = jnp.logical_and(me >= 2, target == 0)
                four = jnp.logical_or(
                    jnp.logical_and(me == 1, away == 1), jnp.logical_and(me == 3, away == 2)
                )
                base = jnp.where(away == 0, FIRST, jnp.where(far, FAR_AT, 0))
                row = base + rank * R
                row = jnp.where(
                    four, EXTRA + jnp.where(rank == 0, LOG_AT, NEAR_AT), row
                )
                row = jnp.where(live, row, UNUSED)
                slot = jnp.where(away == 0, 8, jnp.where(far, 18, 2)) + rank
                slot = jnp.where(four, 4 + 24 * rank, slot)
                slot = jnp.where(live, slot, 32)
                where[head, k] = (j, row)
                got[k * heads + head : k * heads + head + 1, :] = logs[j, pl.ds(slot, 1), :]
        first = own_log[pl.ds(pl.multiple_of(pair * heads, heads), heads), :]
        others = [got[k * heads : (k + 1) * heads, :] for k in range(3)]
        top = first
        for other in others:
            top = jnp.maximum(top, other)
        weights = [jnp.exp(x - top) for x in [first] + others]
        total = weights[0] + weights[1] + weights[2] + weights[3]
        shares = jnp.concatenate([w / total for w in weights], axis=0)
        shares = jnp.transpose(shares)
        for head in range(heads):
            cols = slice(head * HEAD_DIM, (head + 1) * HEAD_DIM)
            mixed = shares[:, head : head + 1] * own_ref[rows, cols]
            for k in range(3):
                j, row = where[head, k]
                item = items[j, pl.ds(pl.multiple_of(row, 16), R), :].astype(F32)
                at = (k + 1) * heads + head
                mixed = mixed + shares[:, at : at + 1] * item
            done[rows, cols] = mixed.astype(BF16)
        return 0

    lax.fori_loop(0, N_HEAD, each, 0)
    pairs = []
    for step, ref in enumerate((o0, o1, o2, o3)):
        target = lax.rem(y + step, N_HEAD)
        pairs.append((done.at[pl.ds(pl.multiple_of(target * R, R), R)], ref))
    for copy in run_copies(pairs, sems):
        copy.wait()


def merge(half, meta, place, backs, own_out, own_log):
    rows, wide = own_out.shape

    def kernel(*refs):
        merge_kernel(half, *refs)

    return pl.pallas_call(
        kernel,
        out_shape=[shaped((R, wide))] * N_HEAD,
        in_specs=[SMEM, SMEM] + [HBM] * 4 + [VMEM] * 2,
        out_specs=[HBM] * N_HEAD,
        scratch_shapes=[
            pltpu.VMEM((ROW, UNUSED + R, HEAD_DIM), BF16),
            pltpu.VMEM((ROW, 40, 128), F32),
            pltpu.VMEM((24, 128), F32),
            pltpu.VMEM((rows, wide), BF16),
            pltpu.SemaphoreType.DMA((5,)),
        ],
        compiler_params=params(20),
        cost_estimate=cost(20 * rows * wide, 8 * 2**20),
        name="merge",
    )(meta, place, *backs, own_out, own_log)


def finish_kernel(meta, *refs):
    parts, out, sems = refs[:-2], refs[-2], refs[-1]
    y = meta[1]
    wide = parts[0].shape[1]
    pairs = []
    for half in range(2):
        for step in range(N_HEAD):
            source = lax.rem(y - step + N_HEAD, N_HEAD)
            cols = pl.ds(pl.multiple_of(source * wide, 128), wide)
            pairs.append((parts[half * N_HEAD + step], out.at[pl.ds(half * R, R), cols]))
    for copy in run_copies(pairs, sems):
        copy.wait()


def finish(meta, parts):
    wide = parts[0].shape[1]
    return pl.pallas_call(
        finish_kernel,
        out_shape=shaped((2 * TILE, N_HEAD * wide)),
        in_specs=[SMEM] + [HBM] * len(parts),
        out_specs=VMEM,
        scratch_shapes=[pltpu.SemaphoreType.DMA((len(parts),))],
        compiler_params=params(8),
        cost_estimate=cost(0, 4 * 2 * TILE * N_HEAD * wide),
        name="finish",
    )(meta, *parts)


def rows_to(pairs):
    return [(a * ROW + j, b * ROW + j) for a, b in pairs for j in range(ROW)]


def over_row(x):
    groups = [[a * ROW + j for j in range(ROW)] for a in range(4)]
    return lax.all_to_all(
        x, "ctx", split_axis=0, concat_axis=0, tiled=True, axis_index_groups=groups
    )


def local(queries, key_rows, value_rows, block_gates):
    meta = jnp.stack([lax.axis_index("ctx"), lax.axis_index("head")]).astype(I32)
    q_parts = over_head(split(meta, (queries,)))
    table, place = plan(block_gates.reshape(-1), lax.axis_size("ctx"))
    first, second, far, near = pack(meta, table, q_parts)
    first = over_row(first)
    far = lax.ppermute(far, "ctx", rows_to([(3, 0), (2, 1)]))
    near = lax.ppermute(near, "ctx", rows_to([(1, 0), (3, 2)]))
    kv = join(meta, over_head(split(meta, (key_rows, value_rows), near)))
    kv_one = lax.ppermute(kv, "ctx", rows_to([(0, 1), (1, 2), (2, 3)]))
    kv_two = lax.ppermute(kv, "ctx", rows_to([(1, 3)]))
    out0, out1, log0, log1 = own(meta, q_parts, kv)
    second = over_row(insert(meta, second, far, near))
    (first,) = gate(meta, 0, first, (kv,))
    second, first = gate(meta, 1, second, (kv, kv_one, kv_two), first)
    second = over_row(second)
    first = over_row(first)
    far, near = cut(second)
    far = lax.ppermute(far, "ctx", rows_to([(0, 3), (1, 2)]))
    near = lax.ppermute(near, "ctx", rows_to([(0, 1), (2, 3)]))
    backs = (second, first, far, near)
    done = []
    for half, owned in enumerate(((out0, log0), (out1, log1))):
        done += over_head(merge(half, meta, place, backs, *owned))
    return finish(meta, done)


def solution(mesh):
    return jax.shard_map(
        local,
        mesh=mesh,
        in_specs=(
            P(("ctx", "head"), None),
            P(("ctx", "head"), None),
            P(("ctx", "head"), None),
            P("ctx", "head", None),
        ),
        out_specs=P(("ctx", "head"), None),
        check_vma=False,
    )
```

time: 527 us -> 278 us (0.53)
  the two profiles are of different devices: /device:TPU:3 before, /device:TPU:6 now
where the time goes in v1:
time: 278 us; the launch traced here: 277 us
  waiting for transfers between devices  86.2 us (31%)
  Pallas kernels  81.8 us (29%)
  starting transfers between devices  51.5 us (19%)
  blocking collectives  48.4 us (17%)
  local copies, waits for them, and re-layouts  7.7 us (3%)
    all_to_all x1, blocking collectives, over_row(): lax.all_to_all(x, 'ctx', split_axis=0, concat_axis=0, tiled=True, axis_in...  48.4 us
    ppermute x12, waiting for transfers between devices, over_head(): got.append(lax.ppermute(parts[step], 'head', pairs))  38.9 us
    pallas_call x2, Pallas kernels, gate(): pl.pallas_call(kernel, out_shape=[shaped((ROW, SEND[part], HEAD_DIM))] +...  28.4 us
    ppermute x12, starting transfers between devices, over_head(): got.append(lax.ppermute(parts[step], 'head', pairs))  21.3 us
    all_to_all x3, starting transfers between devices, over_row(): lax.all_to_all(x, 'ctx', split_axis=0, concat_axis=0, tiled=True, axis_in...  19.4 us
    pallas_call x1, Pallas kernels, own(): pl.pallas_call(own_kernel, out_shape=(out, out, logs, logs), in_specs=[SM...  15.2 us
    ppermute x1, waiting for transfers between devices, local(): kv_two = lax.ppermute(kv, 'ctx', rows_to([(1, 3)]))  14.2 us
    pallas_call x2, Pallas kernels, merge(): pl.pallas_call(kernel, out_shape=[shaped((R, wide))] * N_HEAD, in_specs=[...  13.7 us
  transfers between devices with their start and end apart: 21, of which 12 were waited for; matrix products, arithmetic and copies ran while one was open for 0% of the time, Pallas kernels for 16%

profile of v1, /device:TPU:6, one launch (start us, length us, event | category | flops | bytes accessed | tf_op | source)
XLA Modules:
  0.0 276.7 jit_solution(219145205971782056)
XLA Ops:
  0.6 3.5 %split.2 = (bf16[256,1024]{1,0:T(8,128)(2,1)}, bf16[256,1024]{1,0:T(8,128)(2,1)}, bf16[256,1024]{1,0:T(8,128)(2,1)}, bf16[256,1024]{1,0:T(8,128)(2,1)}) custom-call(s32[2]{0:T(128)} %pad_add_fusion.meta.refs_0_, bf16[256,4096]{1,0:T(8,128)(2,1)} %refs_0_.2), custom_call_target="tpu_custom_call" | custom-call | bytes 4194304 | tf_op jit(solution)/shard_map/split/pallas_call | solution.py:112
  4.1 1.7 collective-permute-start
  5.8 2.9 %collective-permute-start.1 = (bf16[256,1024]{1,0:T(8,128)(2,1)}, bf16[256,1024]{1,0:T(8,128)(2,1)S(1)}, u32[]{:S(2)}, u32[]{:S(2)}) collective-permute-start(bf16[256,1024]{1,0:T(8,128)(2,1)} %get-tuple-element.39), channel_id=1, source_target_pairs={{0,2},{1,3},{2,0},{3,1},{4,6},{5,7},{6,4},{7,5},{8,10},{9,11},{10,... | collective-permute-start | bytes 1572872 | tf_op jit(solution)/shard_map/ppermute | solution.py:128
  10.3 4.8 %plan.1 = (s32[128]{0:T(128)S(1)}, s32[192]{0:T(256)S(1)}) custom-call(s32[192]{0:T(256)S(1)} %reshape.3.gates), custom_call_target="tpu_custom_call" | custom-call | tf_op jit(solution)/shard_map/plan/pallas_call | solution.py:81
  15.1 4.2 %collective-permute-done.q1 = bf16[256,1024]{1,0:T(8,128)(2,1)S(1)} collective-permute-done((bf16[256,1024]{1,0:T(8,128)(2,1)}, bf16[256,1024]{1,0:T(8,128)(2,1)S(1)}, u32[]{:S(2)}, u32[]{:S(2)}) %collective-permute-start) | collective-permute-done | bytes 524320 | tf_op jit(solution)/shard_map/ppermute | solution.py:128
  19.4 12.4 %collective-permute-done.1.q2 = bf16[256,1024]{1,0:T(8,128)(2,1)S(1)} collective-permute-done((bf16[256,1024]{1,0:T(8,128)(2,1)}, bf16[256,1024]{1,0:T(8,128)(2,1)S(1)}, u32[]{:S(2)}, u32[]{:S(2)}) %collective-permute-start.1) | collective-permute-done | bytes 524320 | tf_op jit(solution)/shard_map/ppermute | solution.py:128
  32.8 7.0 %pack.1 = (bf16[16,272,128]{2,1,0:T(8,128)(2,1)}, bf16[16,400,128]{2,1,0:T(8,128)(2,1)}, bf16[16,272,128]{2,1,0:T(8,128)(2,1)}, bf16[16,144,128]{2,1,0:T(8,128)(2,1)}) custom-call(s32[2]{0:T(128)} %pad_add_fusion.meta.refs_0_, s32[128]{0:T(128)} %copy-done.11, bf16[256,1024]{1,0:T(8,128)(2,1)} %get-tuple-element.37.q0, bf16[256,1024]{1,0:T(8,128)(2,1)} %copy-done.14, ...), custom_call_target="tpu_custom_call" | custom-call | bytes 6553600 | tf_op jit(solution)/shard_map/pack/pallas_call | solution.py:229
  39.9 8.8 %all-to-all-start.1 = ((bf16[16,272,128]{2,1,0:T(8,128)(2,1)}), bf16[16,272,128]{2,1,0:T(8,128)(2,1)S(1)}, u32[]{:S(2)}, u32[]{:S(2)}) async-start(bf16[16,272,128]{2,1,0:T(8,128)(2,1)} %get-tuple-element.48), calls=%async_computation.1 | async-start | bytes 2228224 | tf_op jit(solution)/shard_map/all_to_all | solution.py:643
  50.2 3.9 %collective-permute-start.4 = (bf16[16,144,128]{2,1,0:T(8,128)(2,1)}, bf16[16,144,128]{2,1,0:T(8,128)(2,1)S(1)}, u32[]{:S(2)}, u32[]{:S(2)}) collective-permute-start(bf16[16,144,128]{2,1,0:T(8,128)(2,1)} %get-tuple-element.43), channel_id=1, source_target_pairs={{64,0},{68,4},{72,8},{76,12},{80,16},{84,20},{88,24},{92,28},{96,3... | collective-permute-start | bytes 1769480 | tf_op jit(solution)/shard_map/ppermute | solution.py:655
  54.1 13.2 %collective-permute-done.4.near.refs_2_ = bf16[16,144,128]{2,1,0:T(8,128)(2,1)S(1)} collective-permute-done((bf16[16,144,128]{2,1,0:T(8,128)(2,1)}, bf16[16,144,128]{2,1,0:T(8,128)(2,1)S(1)}, u32[]{:S(2)}, u32[]{:S(2)}) %collective-permute-start.4) | collective-permute-done | bytes 589856 | tf_op jit(solution)/shard_map/ppermute | solution.py:655
  67.3 7.6 %collective-permute-done.3.far = bf16[16,272,128]{2,1,0:T(8,128)(2,1)S(1)} collective-permute-done((bf16[16,272,128]{2,1,0:T(8,128)(2,1)}, bf16[16,272,128]{2,1,0:T(8,128)(2,1)S(1)}, u32[]{:S(2)}, u32[]{:S(2)}) %collective-permute-start.3) | collective-permute-done | bytes 1114144 | tf_op jit(solution)/shard_map/ppermute | solution.py:654
  74.9 1.9 insert.1
  77.9 7.0 %all-to-all-start = ((bf16[16,400,128]{2,1,0:T(8,128)(2,1)}), bf16[16,400,128]{2,1,0:T(8,128)(2,1)S(1)}, u32[]{:S(2)}, u32[]{:S(2)}) async-start(bf16[16,400,128]{2,1,0:T(8,128)(2,1)} %insert.1), calls=%async_computation | async-start | bytes 3276800 | tf_op jit(solution)/shard_map/all_to_all | solution.py:643
  84.9 3.1 %split.3 = (bf16[256,512]{1,0:T(8,128)(2,1)}, bf16[256,512]{1,0:T(8,128)(2,1)}, bf16[256,512]{1,0:T(8,128)(2,1)}, bf16[256,512]{1,0:T(8,128)(2,1)}) custom-call(s32[2]{0:T(128)} %pad_add_fusion.meta.refs_0_, bf16[256,1024]{1,0:T(8,128)(2,1)} %refs_0_.3, bf16[256,1024]{1,0:T(8,128)(2,1)} %refs_1_.1, bf16[16,144,128]{2,1,0:T(8,128)(2,1)} %copy-done), custom_call_target="tpu_custom_call" | custom-call | bytes 2097152 | tf_op jit(solution)/shard_map/split/pallas_call | solution.py:112
  89.2 2.3 collective-permute-start.6
  91.4 1.7 collective-permute-start.7
  93.1 5.3 %collective-permute-done.5.refs_1_ = bf16[256,512]{1,0:T(8,128)(2,1)S(1)} collective-permute-done((bf16[256,512]{1,0:T(8,128)(2,1)}, bf16[256,512]{1,0:T(8,128)(2,1)S(1)}, u32[]{:S(2)}, u32[]{:S(2)}) %collective-permute-start.5) | collective-permute-done | bytes 262176 | tf_op jit(solution)/shard_map/ppermute | solution.py:128
  98.4 5.5 %collective-permute-done.6.refs_2_ = bf16[256,512]{1,0:T(8,128)(2,1)S(1)} collective-permute-done((bf16[256,512]{1,0:T(8,128)(2,1)}, bf16[256,512]{1,0:T(8,128)(2,1)S(1)}, u32[]{:S(2)}, u32[]{:S(2)}) %collective-permute-start.6) | collective-permute-done | bytes 262176 | tf_op jit(solution)/shard_map/ppermute | solution.py:128
  108.6 11.3 %gate.2.refs_5_ = bf16[16,272,128]{2,1,0:T(8,128)(2,1)} custom-call(s32[2]{0:T(128)} %pad_add_fusion.meta.refs_0_, bf16[16,272,128]{2,1,0:T(8,128)(2,1)} %copy-done.13, bf16[1024,512]{1,0:T(8,128)(2,1)} %copy-done.4), custom_call_target="tpu_custom_call" | custom-call | flops 2147483648 | bytes 8388608 | tf_op jit(solution)/shard_map/gate/pallas_call | solution.py:428
  119.9 14.2 %collective-permute-done.9.refs_4_ = bf16[1024,512]{1,0:T(8,128)(2,1)S(1)} collective-permute-done((bf16[1024,512]{1,0:T(8,128)(2,1)S(1)}, bf16[1024,512]{1,0:T(8,128)(2,1)S(1)}, u32[]{:S(2)}, u32[]{:S(2)}) %collective-permute-start.9) | collective-permute-done | bytes 1048608 | tf_op jit(solution)/shard_map/ppermute | solution.py:658
  136.3 17.1 %gate.3 = (bf16[16,400,128]{2,1,0:T(8,128)(2,1)}, bf16[16,272,128]{2,1,0:T(8,128)(2,1)}) custom-call(s32[2]{0:T(128)} %pad_add_fusion.meta.refs_0_, bf16[16,400,128]{2,1,0:T(8,128)(2,1)} %copy-done.12, bf16[1024,512]{1,0:T(8,128)(2,1)} %copy-done.4, bf16[1024,512]{1,0:T(8,128)(2,1)} %collective-permute-done.8.refs_3_, ...), custom_call_target="tpu_custom_call", output_to_operand_aliasing={{1}: (5, {})} | custom-call | flops 3221225472 | bytes 8388608 | tf_op jit(solution)/shard_map/gate/pallas_call | solution.py:428
  153.4 48.4 %all_to_all.20.back.refs_2_ = bf16[16,400,128]{2,1,0:T(8,128)(2,1)S(1)} all-to-all(bf16[16,400,128]{2,1,0:T(8,128)(2,1)} %get-tuple-element.49), channel_id=1, replica_groups={{0,4,8,12,16,20,24,28,32,36,40,44,48,52,56,60},{64,68,72,76,80,84,88,92..., dimensions={0} | all-to-all | bytes 3276800 | tf_op jit(solution)/shard_map/all_to_all | solution.py:643
  201.8 3.7 %all-to-all-start.3 = ((bf16[16,272,128]{2,1,0:T(8,128)(2,1)}), bf16[16,272,128]{2,1,0:T(8,128)(2,1)S(1)}, u32[]{:S(2)}, u32[]{:S(2)}) async-start(bf16[16,272,128]{2,1,0:T(8,128)(2,1)} %get-tuple-element.50), calls=%async_computation.3 | async-start | bytes 2228224 | tf_op jit(solution)/shard_map/all_to_all | solution.py:643
  209.6 15.2 %own.1 = (f32[512,1024]{1,0:T(8,128)}, f32[512,1024]{1,0:T(8,128)}, f32[32,128]{1,0:T(8,128)}, f32[32,128]{1,0:T(8,128)}) custom-call(s32[2]{0:T(128)} %pad_add_fusion.meta.refs_0_, bf16[256,1024]{1,0:T(8,128)(2,1)} %get-tuple-element.37.q0, bf16[256,1024]{1,0:T(8,128)(2,1)} %copy-done.14, bf16[256,1024]{1,0:T(8,128)(2,1)} %copy-done.15, ...), custom_call_target="tpu_custom_call" | custom-call | flops 2684354560 | bytes 8388608 | tf_op jit(solution)/shard_map/own/pallas_call | solution.py:494
  224.8 8.7 %all-to-all-done.3.refs_3_ = bf16[16,272,128]{2,1,0:T(8,128)(2,1)S(1)} async-done(((bf16[16,272,128]{2,1,0:T(8,128)(2,1)}), bf16[16,272,128]{2,1,0:T(8,128)(2,1)S(1)}, u32[]{:S(2)}, u32[]{:S(2)}) %all-to-all-start.3) | async-done | bytes 1114144 | tf_op jit(solution)/shard_map/all_to_all | solution.py:643
  233.5 3.5 %collective-permute-done.10.refs_4_ = bf16[16,272,128]{2,1,0:T(8,128)(2,1)} collective-permute-done((bf16[16,272,128]{2,1,0:T(8,128)(2,1)}, bf16[16,272,128]{2,1,0:T(8,128)(2,1)}, u32[]{:S(2)}, u32[]{:S(2)}) %collective-permute-start.10) | collective-permute-done | bytes 1114144 | tf_op jit(solution)/shard_map/ppermute | solution.py:666
  239.3 6.9 %merge.3 = (bf16[128,1024]{1,0:T(8,128)(2,1)S(1)}, bf16[128,1024]{1,0:T(8,128)(2,1)S(1)}, bf16[128,1024]{1,0:T(8,128)(2,1)S(1)}, bf16[128,1024]{1,0:T(8,128)(2,1)S(1)}) custom-call(s32[2]{0:T(128)S(1)} %copy-done.8, s32[192]{0:T(256)S(1)} %get-tuple-element.35.refs_1_, bf16[16,400,128]{2,1,0:T(8,128)(2,1)S(1)} %all_to_all.20.back.refs_2_, ...), custom_call_target="tpu_custom_call" | custom-call | flops 10485760 | bytes 8388608 | tf_op jit(solution)/shard_map/merge/pallas_call | solution.py:591
  246.2 3.7 %collective-permute-start.15 = (bf16[128,1024]{1,0:T(8,128)(2,1)S(1)}, bf16[128,1024]{1,0:T(8,128)(2,1)S(1)}, u32[]{:S(2)}, u32[]{:S(2)}) collective-permute-start(bf16[128,1024]{1,0:T(8,128)(2,1)S(1)} %get-tuple-element.62), channel_id=1, source_target_pairs={{0,1},{1,2},{2,3},{3,0},{4,5},{5,6},{6,7},{7,4},{8,9},{9,10},{10,1... | collective-permute-start | bytes 786440 | tf_op jit(solution)/shard_map/ppermute | solution.py:128
  252.7 6.9 %merge.2 = (bf16[128,1024]{1,0:T(8,128)(2,1)S(1)}, bf16[128,1024]{1,0:T(8,128)(2,1)S(1)}, bf16[128,1024]{1,0:T(8,128)(2,1)S(1)}, bf16[128,1024]{1,0:T(8,128)(2,1)S(1)}) custom-call(s32[2]{0:T(128)S(1)} %copy-done.8, s32[192]{0:T(256)S(1)} %get-tuple-element.35.refs_1_, bf16[16,400,128]{2,1,0:T(8,128)(2,1)S(1)} %all_to_all.20.back.refs_2_, ...), custom_call_target="tpu_custom_call" | custom-call | flops 10485760 | bytes 8388608 | tf_op jit(solution)/shard_map/merge/pallas_call | solution.py:591
  260.5 1.9 collective-permute-start.13
  264.0 10.4 %collective-permute-done.12.refs_1_ = bf16[128,1024]{1,0:T(8,128)(2,1)S(1)} collective-permute-done((bf16[128,1024]{1,0:T(8,128)(2,1)S(1)}, bf16[128,1024]{1,0:T(8,128)(2,1)S(1)}, u32[]{:S(2)}, u32[]{:S(2)}) %collective-permute-start.12) | collective-permute-done | bytes 262176 | tf_op jit(solution)/shard_map/ppermute | solution.py:128
  274.4 2.1 finish.1
  (65 shorter events, 25.5 us)
Async XLA Ops:
  0.0 10.0 %copy-start.17 = (s32[8,8,3]{1,0,2:T(8,128)S(1)}, s32[8,8,3]{1,0,2:T(8,128)}, u32[]{:S(2)}) copy-start(s32[8,8,3]{1,0,2:T(8,128)} %param.7) | copy-start | bytes 2308
  4.1 15.2 %collective-permute-start = (bf16[256,1024]{1,0:T(8,128)(2,1)}, bf16[256,1024]{1,0:T(8,128)(2,1)S(1)}, u32[]{:S(2)}, u32[]{:S(2)}) collective-permute-start(bf16[256,1024]{1,0:T(8,128)(2,1)} %get-tuple-element.38), channel_id=1, source_target_pairs={{0,1},{1,2},{2,3},{3,0},{4,5},{5,6},{6,7},{7,4},{8,9},{9,10},{10,1... | collective-permute-start | bytes 1572872 | tf_op jit(solution)/shard_map/ppermute | solution.py:128
  5.8 26.0 %collective-permute-start.1 = (bf16[256,1024]{1,0:T(8,128)(2,1)}, bf16[256,1024]{1,0:T(8,128)(2,1)S(1)}, u32[]{:S(2)}, u32[]{:S(2)}) collective-permute-start(bf16[256,1024]{1,0:T(8,128)(2,1)} %get-tuple-element.39), channel_id=1, source_target_pairs={{0,2},{1,3},{2,0},{3,1},{4,6},{5,7},{6,4},{7,5},{8,10},{9,11},{10,... | collective-permute-start | bytes 1572872 | tf_op jit(solution)/shard_map/ppermute | solution.py:128
  8.7 23.1 %collective-permute-start.2 = (bf16[256,1024]{1,0:T(8,128)(2,1)}, bf16[256,1024]{1,0:T(8,128)(2,1)S(1)}, u32[]{:S(2)}, u32[]{:S(2)}) collective-permute-start(bf16[256,1024]{1,0:T(8,128)(2,1)} %get-tuple-element.40), channel_id=1, source_target_pairs={{0,3},{1,0},{2,1},{3,2},{4,7},{5,4},{6,5},{7,6},{8,11},{9,8},{10,9... | collective-permute-start | bytes 1572872 | tf_op jit(solution)/shard_map/ppermute | solution.py:128
  15.1 16.6 %copy-start.11 = (s32[128]{0:T(128)}, s32[128]{0:T(128)S(1)}, u32[]{:S(2)}) copy-start(s32[128]{0:T(128)S(1)} %get-tuple-element.36.table) | copy-start | bytes 1540
  19.4 12.4 %copy-start.14 = (bf16[256,1024]{1,0:T(8,128)(2,1)}, bf16[256,1024]{1,0:T(8,128)(2,1)S(1)}, u32[]{:S(2)}) copy-start(bf16[256,1024]{1,0:T(8,128)(2,1)S(1)} %collective-permute-done.q1) | copy-start | bytes 1572868
  39.8 35.1 %copy-start.3 = (bf16[16,400,128]{2,1,0:T(8,128)(2,1)S(1)}, bf16[16,400,128]{2,1,0:T(8,128)(2,1)}, u32[]{:S(2)}) copy-start(bf16[16,400,128]{2,1,0:T(8,128)(2,1)} %get-tuple-element.41.z_in) | copy-start | bytes 4915204
  39.9 35.1 %copy-start.6 = (s32[2]{0:T(128)S(1)}, s32[2]{0:T(128)}, u32[]{:S(2)}) copy-start(s32[2]{0:T(128)} %pad_add_fusion.meta.refs_0_) | copy-start | bytes 28
  39.9 37.0 %all-to-all-start.1 = ((bf16[16,272,128]{2,1,0:T(8,128)(2,1)}), bf16[16,272,128]{2,1,0:T(8,128)(2,1)S(1)}, u32[]{:S(2)}, u32[]{:S(2)}) async-start(bf16[16,272,128]{2,1,0:T(8,128)(2,1)} %get-tuple-element.48), calls=%async_computation.1 | async-start | bytes 2228224 | tf_op jit(solution)/shard_map/all_to_all | solution.py:643
  48.6 26.3 %collective-permute-start.3 = (bf16[16,272,128]{2,1,0:T(8,128)(2,1)}, bf16[16,272,128]{2,1,0:T(8,128)(2,1)S(1)}, u32[]{:S(2)}, u32[]{:S(2)}) collective-permute-start(bf16[16,272,128]{2,1,0:T(8,128)(2,1)} %get-tuple-element.42), channel_id=1, source_target_pairs={{192,0},{196,4},{200,8},{204,12},{208,16},{212,20},{216,24},{220,2... | collective-permute-start | bytes 3342344 | tf_op jit(solution)/shard_map/ppermute | solution.py:654
  50.2 17.1 %collective-permute-start.4 = (bf16[16,144,128]{2,1,0:T(8,128)(2,1)}, bf16[16,144,128]{2,1,0:T(8,128)(2,1)S(1)}, u32[]{:S(2)}, u32[]{:S(2)}) collective-permute-start(bf16[16,144,128]{2,1,0:T(8,128)(2,1)} %get-tuple-element.43), channel_id=1, source_target_pairs={{64,0},{68,4},{72,8},{76,12},{80,16},{84,20},{88,24},{92,28},{96,3... | collective-permute-start | bytes 1769480 | tf_op jit(solution)/shard_map/ppermute | solution.py:655
  67.3 9.6 %copy-start = (bf16[16,144,128]{2,1,0:T(8,128)(2,1)}, bf16[16,144,128]{2,1,0:T(8,128)(2,1)S(1)}, u32[]{:S(2)}) copy-start(bf16[16,144,128]{2,1,0:T(8,128)(2,1)S(1)} %collective-permute-done.4.near.refs_2_) | copy-start | bytes 1769476
  77.9 56.3 %all-to-all-start = ((bf16[16,400,128]{2,1,0:T(8,128)(2,1)}), bf16[16,400,128]{2,1,0:T(8,128)(2,1)S(1)}, u32[]{:S(2)}, u32[]{:S(2)}) async-start(bf16[16,400,128]{2,1,0:T(8,128)(2,1)} %insert.1), calls=%async_computation | async-start | bytes 3276800 | tf_op jit(solution)/shard_map/all_to_all | solution.py:643
  84.9 19.5 %copy-start.7 = (s32[2]{0:T(128)S(1)}, s32[2]{0:T(128)}, u32[]{:S(2)}) copy-start(s32[2]{0:T(128)} %pad_add_fusion.meta.refs_0_) | copy-start | bytes 28
  87.9 10.4 %collective-permute-start.5 = (bf16[256,512]{1,0:T(8,128)(2,1)}, bf16[256,512]{1,0:T(8,128)(2,1)S(1)}, u32[]{:S(2)}, u32[]{:S(2)}) collective-permute-start(bf16[256,512]{1,0:T(8,128)(2,1)} %get-tuple-element.45), channel_id=1, source_target_pairs={{0,1},{1,2},{2,3},{3,0},{4,5},{5,6},{6,7},{7,4},{8,9},{9,10},{10,1... | collective-permute-start | bytes 786440 | tf_op jit(solution)/shard_map/ppermute | solution.py:128
  89.2 14.7 %collective-permute-start.6 = (bf16[256,512]{1,0:T(8,128)(2,1)}, bf16[256,512]{1,0:T(8,128)(2,1)S(1)}, u32[]{:S(2)}, u32[]{:S(2)}) collective-permute-start(bf16[256,512]{1,0:T(8,128)(2,1)} %get-tuple-element.46), channel_id=1, source_target_pairs={{0,2},{1,3},{2,0},{3,1},{4,6},{5,7},{6,4},{7,5},{8,10},{9,11},{10,... | collective-permute-start | bytes 786440 | tf_op jit(solution)/shard_map/ppermute | solution.py:128
  91.4 12.9 %collective-permute-start.7 = (bf16[256,512]{1,0:T(8,128)(2,1)}, bf16[256,512]{1,0:T(8,128)(2,1)S(1)}, u32[]{:S(2)}, u32[]{:S(2)}) collective-permute-start(bf16[256,512]{1,0:T(8,128)(2,1)} %get-tuple-element.47), channel_id=1, source_target_pairs={{0,3},{1,0},{2,1},{3,2},{4,7},{5,4},{6,5},{7,6},{8,11},{9,8},{10,9... | collective-permute-start | bytes 786440 | tf_op jit(solution)/shard_map/ppermute | solution.py:128
  106.0 2.6 copy-start.4
  106.0 28.2 %collective-permute-start.9 = (bf16[1024,512]{1,0:T(8,128)(2,1)S(1)}, bf16[1024,512]{1,0:T(8,128)(2,1)S(1)}, u32[]{:S(2)}, u32[]{:S(2)}) collective-permute-start(bf16[1024,512]{1,0:T(8,128)(2,1)S(1)} %join.1.refs_2_.kv), channel_id=1, source_target_pairs={{64,192},{68,196},{72,200},{76,204},{80,208},{84,212},{88,216},{92... | collective-permute-start | bytes 3145736 | tf_op jit(solution)/shard_map/ppermute | solution.py:658
  107.3 26.9 %collective-permute-start.8 = (bf16[1024,512]{1,0:T(8,128)(2,1)S(1)}, bf16[1024,512]{1,0:T(8,128)(2,1)}, u32[]{:S(2)}, u32[]{:S(2)}) collective-permute-start(bf16[1024,512]{1,0:T(8,128)(2,1)S(1)} %join.1.refs_2_.kv), channel_id=1, source_target_pairs={{0,64},{4,68},{8,72},{12,76},{16,80},{20,84},{24,88},{28,92},{32,9... | collective-permute-start | bytes 3145736 | tf_op jit(solution)/shard_map/ppermute | solution.py:657
  201.8 31.7 %all-to-all-start.3 = ((bf16[16,272,128]{2,1,0:T(8,128)(2,1)}), bf16[16,272,128]{2,1,0:T(8,128)(2,1)S(1)}, u32[]{:S(2)}, u32[]{:S(2)}) async-start(bf16[16,272,128]{2,1,0:T(8,128)(2,1)} %get-tuple-element.50), calls=%async_computation.3 | async-start | bytes 2228224 | tf_op jit(solution)/shard_map/all_to_all | solution.py:643
  206.8 30.2 %collective-permute-start.10 = (bf16[16,272,128]{2,1,0:T(8,128)(2,1)}, bf16[16,272,128]{2,1,0:T(8,128)(2,1)}, u32[]{:S(2)}, u32[]{:S(2)}) collective-permute-start(bf16[16,272,128]{2,1,0:T(8,128)(2,1)} %get-tuple-element.51), channel_id=1, source_target_pairs={{0,192},{4,196},{8,200},{12,204},{16,208},{20,212},{24,216},{28,22... | collective-permute-start | bytes 3342344 | tf_op jit(solution)/shard_map/ppermute | solution.py:666
  208.1 28.9 %copy-start.8 = (s32[2]{0:T(128)S(1)}, s32[2]{0:T(128)}, u32[]{:S(2)}) copy-start(s32[2]{0:T(128)} %pad_add_fusion.meta.refs_0_) | copy-start | bytes 28
  208.1 25.4 %collective-permute-start.11 = (bf16[16,144,128]{2,1,0:T(8,128)(2,1)}, bf16[16,144,128]{2,1,0:T(8,128)(2,1)S(1)}, u32[]{:S(2)}, u32[]{:S(2)}) collective-permute-start(bf16[16,144,128]{2,1,0:T(8,128)(2,1)} %get-tuple-element.52), channel_id=1, source_target_pairs={{0,64},{4,68},{8,72},{12,76},{16,80},{20,84},{24,88},{28,92},{32,9... | collective-permute-start | bytes 1769480 | tf_op jit(solution)/shard_map/ppermute | solution.py:667
  239.3 13.4 %copy-start.1 = (f32[512,1024]{1,0:T(8,128)S(1)}, f32[512,1024]{1,0:T(8,128)}, u32[]{:S(2)}) copy-start(f32[512,1024]{1,0:T(8,128)} %get-tuple-element.53.refs_6_) | copy-start | bytes 6291460
  239.3 13.4 %copy-start.9 = (f32[32,128]{1,0:T(8,128)S(1)}, f32[32,128]{1,0:T(8,128)}, u32[]{:S(2)}) copy-start(f32[32,128]{1,0:T(8,128)} %get-tuple-element.54.refs_7_) | copy-start | bytes 49156
  246.2 16.2 %collective-permute-start.15 = (bf16[128,1024]{1,0:T(8,128)(2,1)S(1)}, bf16[128,1024]{1,0:T(8,128)(2,1)S(1)}, u32[]{:S(2)}, u32[]{:S(2)}) collective-permute-start(bf16[128,1024]{1,0:T(8,128)(2,1)S(1)} %get-tuple-element.62), channel_id=1, source_target_pairs={{0,1},{1,2},{2,3},{3,0},{4,5},{5,6},{6,7},{7,4},{8,9},{9,10},{10,1... | collective-permute-start | bytes 786440 | tf_op jit(solution)/shard_map/ppermute | solution.py:128
  249.9 14.1 %collective-permute-start.16 = (bf16[128,1024]{1,0:T(8,128)(2,1)S(1)}, bf16[128,1024]{1,0:T(8,128)(2,1)S(1)}, u32[]{:S(2)}, u32[]{:S(2)}) collective-permute-start(bf16[128,1024]{1,0:T(8,128)(2,1)S(1)} %get-tuple-element.63), channel_id=1, source_target_pairs={{0,2},{1,3},{2,0},{3,1},{4,6},{5,7},{6,4},{7,5},{8,10},{9,11},{10,... | collective-permute-start | bytes 786440 | tf_op jit(solution)/shard_map/ppermute | solution.py:128
  251.5 12.4 %collective-permute-start.17 = (bf16[128,1024]{1,0:T(8,128)(2,1)S(1)}, bf16[128,1024]{1,0:T(8,128)(2,1)S(1)}, u32[]{:S(2)}, u32[]{:S(2)}) collective-permute-start(bf16[128,1024]{1,0:T(8,128)(2,1)S(1)} %get-tuple-element.64), channel_id=1, source_target_pairs={{0,3},{1,0},{2,1},{3,2},{4,7},{5,4},{6,5},{7,6},{8,11},{9,8},{10,9... | collective-permute-start | bytes 786440 | tf_op jit(solution)/shard_map/ppermute | solution.py:128
  259.5 14.8 %collective-permute-start.12 = (bf16[128,1024]{1,0:T(8,128)(2,1)S(1)}, bf16[128,1024]{1,0:T(8,128)(2,1)S(1)}, u32[]{:S(2)}, u32[]{:S(2)}) collective-permute-start(bf16[128,1024]{1,0:T(8,128)(2,1)S(1)} %get-tuple-element.56), channel_id=1, source_target_pairs={{0,1},{1,2},{2,3},{3,0},{4,5},{5,6},{6,7},{7,4},{8,9},{9,10},{10,1... | collective-permute-start | bytes 786440 | tf_op jit(solution)/shard_map/ppermute | solution.py:128
  260.5 13.9 %collective-permute-start.13 = (bf16[128,1024]{1,0:T(8,128)(2,1)S(1)}, bf16[128,1024]{1,0:T(8,128)(2,1)S(1)}, u32[]{:S(2)}, u32[]{:S(2)}) collective-permute-start(bf16[128,1024]{1,0:T(8,128)(2,1)S(1)} %get-tuple-element.57), channel_id=1, source_target_pairs={{0,2},{1,3},{2,0},{3,1},{4,6},{5,7},{6,4},{7,5},{8,10},{9,11},{10,... | collective-permute-start | bytes 786440 | tf_op jit(solution)/shard_map/ppermute | solution.py:128
  262.4 12.0 %collective-permute-start.14 = (bf16[128,1024]{1,0:T(8,128)(2,1)S(1)}, bf16[128,1024]{1,0:T(8,128)(2,1)S(1)}, u32[]{:S(2)}, u32[]{:S(2)}) collective-permute-start(bf16[128,1024]{1,0:T(8,128)(2,1)S(1)} %get-tuple-element.58), channel_id=1, source_target_pairs={{0,3},{1,0},{2,1},{3,2},{4,7},{5,4},{6,5},{7,6},{8,11},{9,8},{10,9... | collective-permute-start | bytes 786440 | tf_op jit(solution)/shard_map/ppermute | solution.py:128
  (8 other events, 8.3 us)

commit v2 on v1

--- a/solution.py
+++ b/solution.py
@@ -55,7 +55,9 @@
     return copies
 
 
-def plan_kernel(gates, table, place):
+def plan_kernel(meta, gates, table, place):
+    me = meta[0] // ROW
+
     def clear(i, _):
         table[2 * i] = -1
         table[2 * i + 1] = -1
@@ -63,13 +65,23 @@
 
     def note(e, _):
         b = gates[e]
-        place[e] = -1
+        place[e] = UNUSED // 16 * 1024 + 32 * 16
 
         @pl.when(b >= 0)
         def _():
-            at = 2 * b + (table[2 * b] >= 0).astype(I32)
-            table[at] = e
-            place[e] = at
+            rank = (table[2 * b] >= 0).astype(I32)
+            table[2 * b + rank] = e
+            target = lax.div(b, ROW)
+            away = me - target
+            far = jnp.logical_and(me >= 2, target == 0)
+            four = jnp.logical_or(
+                jnp.logical_and(me == 1, away == 1), jnp.logical_and(me == 3, away == 2)
+            )
+            row = jnp.where(away == 0, FIRST, jnp.where(far, FAR_AT, 0)) + rank * R
+            row = jnp.where(four, EXTRA + jnp.where(rank == 0, LOG_AT, NEAR_AT), row)
+            slot = jnp.where(away == 0, 8, jnp.where(far, 18, 2)) + rank
+            slot = jnp.where(four, 4 + 24 * rank, slot)
+            place[e] = lax.div(row, 16) * 1024 + slot * 16 + lax.rem(b, ROW)
 
         return 0
 
@@ -77,46 +89,59 @@
     lax.fori_loop(0, gates.shape[0], note, 0)
 
 
-def plan(gates, blocks):
+def plan(meta, gates, blocks):
     return pl.pallas_call(
         plan_kernel,
         out_shape=(shaped((blocks * CAP,), I32), shaped(gates.shape, I32)),
-        in_specs=[SMEM],
+        in_specs=[SMEM, SMEM],
         out_specs=(SMEM, SMEM),
         compiler_params=params(4),
         name="plan",
-    )(gates)
-
-
-def split_body(meta, ins, outs, sems):
-    pairs = []
-    for step in range(N_HEAD):
-        g = lax.rem(meta[1] + step, N_HEAD)
-        at = 0
+    )(meta, gates)
+
+
+def split_kernel(count, first, meta, *refs):
+    ins, outs = refs[:count], refs[-2 - 2 * (N_HEAD - first) : -2 - (N_HEAD - first)]
+    boxes, (reads, saves) = refs[-2 - (N_HEAD - first) : -2], refs[-2:]
+    loads = []
+    for i, box in enumerate(boxes):
+        g = lax.rem(meta[1] + first + i, N_HEAD)
+        at, pairs = 0, []
         for ref in ins:
             wide = ref.shape[1] // N_HEAD
             cols = pl.ds(pl.multiple_of(g * wide, 128), wide)
-            pairs.append((ref.at[:, cols], outs[step].at[:, pl.ds(at, wide)]))
+            pairs.append((ref.at[:, cols], box.at[:, pl.ds(at, wide)]))
             at += wide
-    for copy in run_copies(pairs, sems):
-        copy.wait()
-
-
-def split(meta, ins, *earlier):
+        loads.append(run_copies(pairs, reads.at[i]))
+    done = []
+    for i, load in enumerate(loads):
+        for copy in load:
+            copy.wait()
+        done.append(pltpu.make_async_copy(boxes[i], outs[i], saves.at[i]))
+        done[-1].start()
+    for copy in done:
+        copy.wait()
+
+
+def split(meta, first, ins, *earlier):
     rows, wide = ins[0].shape[0], sum(x.shape[1] for x in ins) // N_HEAD
-
-    def kernel(meta, *refs):
-        n = len(ins)
-        split_body(meta, refs[:n], refs[n + len(earlier) : -1], refs[-1])
+    parts = N_HEAD - first
+
+    def kernel(*refs):
+        split_kernel(len(ins), first, *refs)
 
     return pl.pallas_call(
         kernel,
-        out_shape=[shaped((rows, wide))] * N_HEAD,
+        out_shape=[shaped((rows, wide))] * parts,
         in_specs=[SMEM] + [HBM] * (len(ins) + len(earlier)),
-        out_specs=[VMEM] * N_HEAD,
-        scratch_shapes=[pltpu.SemaphoreType.DMA((N_HEAD * len(ins),))],
-        compiler_params=params(56),
-        cost_estimate=cost(0, 4 * rows * wide * N_HEAD),
+        out_specs=[HBM] * parts,
+        scratch_shapes=[pltpu.VMEM((rows, wide), BF16)] * parts
+        + [
+            pltpu.SemaphoreType.DMA((parts, len(ins))),
+            pltpu.SemaphoreType.DMA((parts,)),
+        ],
+        compiler_params=params(8 if earlier else 56),
+        cost_estimate=cost(0, 4 * rows * wide * parts),
         name="split",
     )(meta, *ins, *earlier)
 
@@ -132,6 +157,10 @@
 def by_source(y, refs, whole):
     size = refs[0].shape[0]
     pairs = []
+    if refs[0].shape[1] != whole.shape[1]:
+        wide = whole.shape[1]
+        own = refs[0].at[:, pl.ds(pl.multiple_of(y * wide, 128), wide)]
+        refs = (own,) + tuple(refs[1:])
     for step, ref in enumerate(refs):
         source = lax.rem(y - step + N_HEAD, N_HEAD)
         pairs.append((ref, whole.at[pl.ds(pl.multiple_of(source * size, 16), size)]))
@@ -224,7 +253,7 @@
 
 
 def pack(meta, table, q_parts):
-    rows, wide = q_parts[0].shape
+    rows, wide = q_parts[1].shape
     sizes = (SEND[0], SEND[1], FAR, NEAR)
     return pl.pallas_call(
         pack_kernel,
@@ -340,8 +369,7 @@
     return jnp.sum(jnp.where(lane == row, wide, 0.0), axis=0, keepdims=True)
 
 
-def attend(q, keys, values):
-    scores = dot_t(q, keys)
+def attend(scores, values):
     top = jnp.max(scores, axis=-1, keepdims=True)
     weights = jnp.exp2((scores - top) * SCALE2)
     total = jnp.sum(weights, axis=-1, keepdims=True)
@@ -351,16 +379,38 @@
 
 def gate_kernel(part, meta, *refs):
     n_kv = 3 if part else 1
-    z, kvs, out = refs[0], refs[1 : 1 + n_kv], refs[1 + n_kv]
-    kv, logs, codes, lists, counts, marks, sems = refs[2 + n_kv :]
+    z_in, kvs, out_ref = refs[0], refs[1 : 1 + n_kv], refs[1 + n_kv]
+    z, out, kv, logs, codes, lists, counts, marks, sems, kv_sems, out_sems = refs[2 + n_kv :]
     me = meta[0] // ROW
-    copies = run_copies([(kvs[i], kv.at[i]) for i in range(n_kv)], sems)
+    groups = ((2, 3), (4,)) if part else ((0, 1),)
+    size = SEND[part]
+    known = pltpu.make_async_copy(
+        z_in.at[:, pl.ds(size - EXTRA, EXTRA)], z.at[:, pl.ds(size - EXTRA, EXTRA)], sems.at[0]
+    )
+    known.start()
+    loads = []
+    for group in range(len(groups)):
+        rows = pl.ds(2 * R * group, R * len(groups[group]))
+        loads.append(pltpu.make_async_copy(z_in.at[:, rows], z.at[:, rows], sems.at[1 + group]))
+        loads[-1].start()
+        if part:
+            stores = (me == 0, me > 0, False) if group == 0 else (
+                me == 0, jnp.logical_or(me == 1, me == 2), me == 3
+            )
+            for i, chosen in enumerate(stores):
+                if chosen is not False:
+
+                    @pl.when(chosen)
+                    def _(i=i, group=group):
+                        pltpu.make_async_copy(kvs[i], kv.at[group], kv_sems.at[group]).start()
+        else:
+            pltpu.make_async_copy(kvs[0], kv.at[0], kv_sems.at[0]).start()
+    known.wait()
     for j in range(ROW):
-        marks[j : j + 1, :] = z[j, SEND[part] - EXTRA :, :].astype(F32)[:1].astype(I32)
-    known = pltpu.make_async_copy(marks, codes, sems.at[n_kv])
+        marks[j : j + 1, :] = z[j, size - EXTRA :, :].astype(F32)[:1].astype(I32)
+    known = pltpu.make_async_copy(marks, codes, sems.at[0])
     known.start()
     known.wait()
-    groups = ((2, 3), (4,)) if part else ((0, 1),)
     for i in range(2 * len(groups)):
         counts[i] = 0
 
@@ -379,27 +429,37 @@
         return 0
 
     lax.fori_loop(0, ROW, scan, 0)
-    for copy in copies:
-        copy.wait()
-    stores = (jnp.where(me == 0, 0, 1), jnp.where(me == 0, 0, jnp.where(me == 3, 2, 1)))
+    saves = []
+
+    def save(first, rows):
+        region = pl.ds(first, rows)
+        copy = pltpu.make_async_copy(
+            out.at[:, region], out_ref.at[:, region], out_sems.at[len(saves)]
+        )
+        copy.start()
+        saves.append(copy)
+
     for i in range(2 * len(groups)):
-        store, kv_head = stores[i // 2] if part else 0, i % 2
+        group, kv_head = i // 2, i % 2
         count = counts[i]
-
-        def batch(n, _, i=i, store=store, kv_head=kv_head, count=count):
-            keys = kv[store, :, kv_head * HEAD_DIM : (kv_head + 1) * HEAD_DIM]
-            values = kv[store, :, (2 + kv_head) * HEAD_DIM : (3 + kv_head) * HEAD_DIM]
-            where = []
+        if kv_head == 0:
+            loads[group].wait()
+            pltpu.make_async_copy(kvs[0], kv.at[group], kv_sems.at[group]).wait()
+
+        def batch(n, _, i=i, group=group, kv_head=kv_head, count=count):
+            keys = kv[group, :, kv_head * HEAD_DIM : (kv_head + 1) * HEAD_DIM]
+            values = kv[group, :, (2 + kv_head) * HEAD_DIM : (3 + kv_head) * HEAD_DIM]
+            where, scores = [], []
             for u in range(GROUP):
                 item = lists[i, jnp.minimum(n * GROUP + u, count - 1)]
                 where.append((lax.div(item, 8), lax.rem(item, 8)))
-            done = []
             for u in range(0, GROUP, 2):
                 q = [
                     z[j, pl.ds(pl.multiple_of((s - 2 * part) * R, R), R), :]
                     for j, s in where[u : u + 2]
                 ]
-                done.append(attend(jnp.concatenate(q, axis=0), keys, values))
+                scores.append(dot_t(jnp.concatenate(q, axis=0), keys))
+            done = [attend(x, values) for x in scores]
             for u, (j, s) in enumerate(where):
                 mixed, log = done[u // 2]
                 rows = slice(u % 2 * R, (u % 2 + 1) * R)
@@ -412,8 +472,13 @@
             return 0
 
         lax.fori_loop(0, lax.div(count + GROUP - 1, GROUP), batch, 0)
+        if i == 1:
+            save(0, 2 * R)
     for j in range(ROW):
         out[j, LOG_AT : LOG_AT + EXTRA, :] = logs[j].astype(BF16)
+    save(LOG_AT, size - 2 * R)
+    for copy in saves:
+        copy.wait()
 
 
 def gate(meta, part, z, kvs, *held):
@@ -428,17 +493,21 @@
     return pl.pallas_call(
         kernel,
         out_shape=[shaped((ROW, SEND[part], HEAD_DIM))] + [shaped(x.shape) for x in held],
-        in_specs=[SMEM, VMEM] + [HBM] * (n_kv + len(held)),
-        out_specs=[VMEM] + [HBM] * len(held),
+        in_specs=[SMEM, HBM] + [HBM] * (n_kv + len(held)),
+        out_specs=[HBM] * (1 + len(held)),
         input_output_aliases={2 + n_kv + i: 1 + i for i in range(len(held))},
         scratch_shapes=[
-            pltpu.VMEM((n_kv,) + kvs[0].shape, BF16),
+            pltpu.VMEM((ROW, SEND[part], HEAD_DIM), BF16),
+            pltpu.VMEM((ROW, SEND[part], HEAD_DIM), BF16),
+            pltpu.VMEM((1 + part,) + kvs[0].shape, BF16),
             pltpu.VMEM((ROW, 16, 128), F32),
             pltpu.SMEM((ROW, 128), I32),
             pltpu.SMEM((4, ROW * CAP), I32),
             pltpu.SMEM((8,), I32),
             pltpu.VMEM((ROW, 128), I32),
-            pltpu.SemaphoreType.DMA((n_kv + 1,)),
+            pltpu.SemaphoreType.DMA((3,)),
+            pltpu.SemaphoreType.DMA((2,)),
+            pltpu.SemaphoreType.DMA((2,)),
         ],
         compiler_params=params(56),
         cost_estimate=cost(4 * items * R * keys * HEAD_DIM, 8 * 2**20, items * R * keys),
@@ -446,7 +515,7 @@
     )(meta, z, *kvs, *held)
 
 
-def own_kernel(meta, q0, q1, q2, q3, kv, out0, out1, log0, log1, q_all, sems):
+def own_kernel(meta, q0, q1, q2, q3, kv, _, out0, out1, log0, log1, __, q_all, sems):
     for copy in run_copies(by_source(meta[1], (q0, q1, q2, q3), q_all), sems):
         copy.wait()
     tiles = q_all.shape[0] // R
@@ -486,28 +555,29 @@
                 logs[at : at + 1, :] = to_row(log[u * R : (u + 1) * R])
 
 
-def own(meta, q_parts, kv):
-    rows, wide = q_parts[0].shape
+def own(meta, q_parts, kv, held):
+    rows, wide = q_parts[1].shape
     rows = N_HEAD * rows
     units = rows * wide // HEAD_DIM
     out, logs = shaped((rows // 2, wide), F32), shaped((units // R // 2, 128), F32)
     return pl.pallas_call(
         own_kernel,
-        out_shape=(out, out, logs, logs),
-        in_specs=[SMEM] + [HBM] * N_HEAD + [VMEM],
-        out_specs=(VMEM, VMEM, VMEM, VMEM),
+        out_shape=(out, out, logs, logs, shaped(held.shape)),
+        in_specs=[SMEM] + [HBM] * N_HEAD + [VMEM, HBM],
+        out_specs=(VMEM, VMEM, VMEM, VMEM, HBM),
+        input_output_aliases={2 + N_HEAD: 4},
         scratch_shapes=[pltpu.VMEM((rows, wide), BF16), pltpu.SemaphoreType.DMA((N_HEAD,))],
         compiler_params=params(56),
         cost_estimate=cost(4 * units * 640 * HEAD_DIM, 8 * 2**20, units * 640),
         name="own",
-    )(meta, *q_parts, kv)
+    )(meta, *q_parts, kv, held)
 
 
 def merge_kernel(
     half, meta, place, far_back, z_back, farb, nearb, own_ref, own_log,
     o0, o1, o2, o3, items, logs, got, done, sems
 ):
-    me, y = meta[0] // ROW, meta[1]
+    y = meta[1]
     copies = run_copies(
         [
             (far_back, items.at[:, pl.ds(0, SEND[1])]),
@@ -533,24 +603,9 @@
         for head in range(heads):
             for k in range(3):
                 at = place[((2 * pair + half) * heads + head) * 3 + k]
-                live = at >= 0
-                rank = lax.rem(at, 2)
-                j = jnp.where(live, lax.rem(lax.div(at, 2), ROW), 0)
-                away = me - lax.div(at, 2 * ROW)
-                target = me - away
-                far = jnp.logical_and(me >= 2, target == 0)
-                four = jnp.logical_or(
-                    jnp.logical_and(me == 1, away == 1), jnp.logical_and(me == 3, away == 2)
-                )
-                base = jnp.where(away == 0, FIRST, jnp.where(far, FAR_AT, 0))
-                row = base + rank * R
-                row = jnp.where(
-                    four, EXTRA + jnp.where(rank == 0, LOG_AT, NEAR_AT), row
-                )
-                row = jnp.where(live, row, UNUSED)
-                slot = jnp.where(away == 0, 8, jnp.where(far, 18, 2)) + rank
-                slot = jnp.where(four, 4 + 24 * rank, slot)
-                slot = jnp.where(live, slot, 32)
+                row = lax.shift_right_logical(at, 10) * 16
+                slot = jnp.bitwise_and(lax.shift_right_logical(at, 4), 63)
+                j = jnp.bitwise_and(at, 15)
                 where[head, k] = (j, row)
                 got[k * heads + head : k * heads + head + 1, :] = logs[j, pl.ds(slot, 1), :]
         first = own_log[pl.ds(pl.multiple_of(pair * heads, heads), heads), :]
@@ -647,20 +702,21 @@
 
 def local(queries, key_rows, value_rows, block_gates):
     meta = jnp.stack([lax.axis_index("ctx"), lax.axis_index("head")]).astype(I32)
-    q_parts = over_head(split(meta, (queries,)))
-    table, place = plan(block_gates.reshape(-1), lax.axis_size("ctx"))
+    q_parts = over_head([queries, *split(meta, 1, (queries,))])
+    table, place = plan(meta, block_gates.reshape(-1), lax.axis_size("ctx"))
     first, second, far, near = pack(meta, table, q_parts)
     first = over_row(first)
     far = lax.ppermute(far, "ctx", rows_to([(3, 0), (2, 1)]))
     near = lax.ppermute(near, "ctx", rows_to([(1, 0), (3, 2)]))
-    kv = join(meta, over_head(split(meta, (key_rows, value_rows), near)))
+    kv_cut = split(meta, 0, (key_rows, value_rows), near)
+    kv = join(meta, over_head(kv_cut))
     kv_one = lax.ppermute(kv, "ctx", rows_to([(0, 1), (1, 2), (2, 3)]))
     kv_two = lax.ppermute(kv, "ctx", rows_to([(1, 3)]))
-    out0, out1, log0, log1 = own(meta, q_parts, kv)
     second = over_row(insert(meta, second, far, near))
     (first,) = gate(meta, 0, first, (kv,))
     second, first = gate(meta, 1, second, (kv, kv_one, kv_two), first)
     second = over_row(second)
+    out0, out1, log0, log1, first = own(meta, q_parts, kv, first)
     first = over_row(first)
     far, near = cut(second)
     far = lax.ppermute(far, "ctx", rows_to([(0, 3), (1, 2)]))

time: 278 us -> 268 us (0.964)
  blocking collectives: 48.4 us -> 0 us
  waiting for transfers between devices: 86.2 us -> 129 us
  Pallas kernels: 81.8 us -> 72.6 us
  starting transfers between devices: 51.5 us -> 59.5 us
  local copies, waits for them, and re-layouts: 7.7 us -> 3.93 us
    all_to_all x1 -> x0, blocking collectives: 48.4 us -> none  [over_row(): lax.all_to_all(x, 'ctx', split_axis=0, concat_axis=0, tiled=True, axis_in...]
    all_to_all x3 -> x4, waiting for transfers between devices: 8.74 us -> 47.9 us  [over_row(): lax.all_to_all(x, 'ctx', split_axis=0, concat_axis=0, tiled=True, axis_in...]
    ppermute x1, waiting for transfers between devices: 0.01 us -> 14.6 us  [local(): kv_one = lax.ppermute(kv, 'ctx', rows_to([(0, 1), (1, 2), (2, 3)]))]
    ppermute x1, waiting for transfers between devices: 14.2 us -> 3.72 us  [local(): kv_two = lax.ppermute(kv, 'ctx', rows_to([(1, 3)]))]
    all_to_all x3 -> x4, starting transfers between devices: 19.4 us -> 27.6 us  [over_row(): lax.all_to_all(x, 'ctx', split_axis=0, concat_axis=0, tiled=True, axis_in...]
    pallas_call x2, Pallas kernels: 28.4 us -> 23 us  [gate(): pl.pallas_call(kernel, out_shape=[shaped((ROW, SEND[part], HEAD_DIM))] +...]
    unnamed x39, local copies, waits for them, and re-layouts: 7.57 us -> 3.8 us
  transfers between devices with their start and end apart: 21 -> 22, of which waited for: 12 -> 15; matrix products, arithmetic and copies ran while one was open for 0% -> 0% of each run, Pallas kernels for 16% -> 15%
where the time goes in v2:
time: 268 us; the launch traced here: 266 us
  waiting for transfers between devices  129 us (48%)
  Pallas kernels  72.6 us (27%)
  starting transfers between devices  59.5 us (22%)
  local copies, waits for them, and re-layouts  3.93 us (1%)
    all_to_all x4, waiting for transfers between devices, over_row(): lax.all_to_all(x, 'ctx', split_axis=0, concat_axis=0, tiled=True, axis_in...  47.9 us
    ppermute x12, waiting for transfers between devices, over_head(): got.append(lax.ppermute(parts[step], 'head', pairs))  38.4 us
    all_to_all x4, starting transfers between devices, over_row(): lax.all_to_all(x, 'ctx', split_axis=0, concat_axis=0, tiled=True, axis_in...  27.6 us
    pallas_call x2, Pallas kernels, gate(): pl.pallas_call(kernel, out_shape=[shaped((ROW, SEND[part], HEAD_DIM))] +...  23 us
    ppermute x12, starting transfers between devices, over_head(): got.append(lax.ppermute(parts[step], 'head', pairs))  21.1 us
    pallas_call x1, Pallas kernels, own(): pl.pallas_call(own_kernel, out_shape=(out, out, logs, logs, shaped(held.s...  15.2 us
    ppermute x1, waiting for transfers between devices, local(): kv_one = lax.ppermute(kv, 'ctx', rows_to([(0, 1), (1, 2), (2, 3)]))  14.6 us
    ppermute x1, waiting for transfers between devices, local(): near = lax.ppermute(near, 'ctx', rows_to([(1, 0), (3, 2)]))  12.8 us
  transfers between devices with their start and end apart: 22, of which 15 were waited for; matrix products, arithmetic and copies ran while one was open for 0% of the time, Pallas kernels for 15%

profile of v2, /device:TPU:6, one launch (start us, length us, event | category | flops | bytes accessed | tf_op | source)
XLA Modules:
  0.0 266.3 jit_solution(9293718192165317425)
XLA Ops:
  0.6 3.0 %split.2 = (bf16[256,1024]{1,0:T(8,128)(2,1)}, bf16[256,1024]{1,0:T(8,128)(2,1)}, bf16[256,1024]{1,0:T(8,128)(2,1)}) custom-call(s32[2]{0:T(128)} %pad_add_fusion.meta.refs_0_, bf16[256,4096]{1,0:T(8,128)(2,1)} %q0.3), custom_call_target="tpu_custom_call" | custom-call | bytes 3145728 | tf_op jit(solution)/shard_map/split/pallas_call | solution.py:133
  5.3 2.9 %collective-permute-start.1 = (bf16[256,1024]{1,0:T(8,128)(2,1)}, bf16[256,1024]{1,0:T(8,128)(2,1)S(1)}, u32[]{:S(2)}, u32[]{:S(2)}) collective-permute-start(bf16[256,1024]{1,0:T(8,128)(2,1)} %get-tuple-element.38), channel_id=1, source_target_pairs={{0,2},{1,3},{2,0},{3,1},{4,6},{5,7},{6,4},{7,5},{8,10},{9,11},{10,... | collective-permute-start | bytes 1572872 | tf_op jit(solution)/shard_map/ppermute | solution.py:153
  9.9 6.2 %plan.1 = (s32[128]{0:T(128)S(1)}, s32[192]{0:T(256)S(1)}) custom-call(s32[2]{0:T(128)S(1)} %copy-done.6, s32[192]{0:T(256)S(1)} %reshape.3.gates), custom_call_target="tpu_custom_call" | custom-call | tf_op jit(solution)/shard_map/plan/pallas_call | solution.py:93
  16.0 2.9 %collective-permute-done.q1 = bf16[256,1024]{1,0:T(8,128)(2,1)S(1)} collective-permute-done((bf16[256,1024]{1,0:T(8,128)(2,1)}, bf16[256,1024]{1,0:T(8,128)(2,1)S(1)}, u32[]{:S(2)}, u32[]{:S(2)}) %collective-permute-start) | collective-permute-done | bytes 524320 | tf_op jit(solution)/shard_map/ppermute | solution.py:153
  18.9 12.4 %collective-permute-done.1.q2 = bf16[256,1024]{1,0:T(8,128)(2,1)S(1)} collective-permute-done((bf16[256,1024]{1,0:T(8,128)(2,1)}, bf16[256,1024]{1,0:T(8,128)(2,1)S(1)}, u32[]{:S(2)}, u32[]{:S(2)}) %collective-permute-start.1) | collective-permute-done | bytes 524320 | tf_op jit(solution)/shard_map/ppermute | solution.py:153
  32.3 7.0 %pack.1 = (bf16[16,272,128]{2,1,0:T(8,128)(2,1)}, bf16[16,400,128]{2,1,0:T(8,128)(2,1)}, bf16[16,272,128]{2,1,0:T(8,128)(2,1)}, bf16[16,144,128]{2,1,0:T(8,128)(2,1)}) custom-call(s32[2]{0:T(128)} %pad_add_fusion.meta.refs_0_, s32[128]{0:T(128)} %copy-done.11, bf16[256,4096]{1,0:T(8,128)(2,1)} %q0.3, bf16[256,1024]{1,0:T(8,128)(2,1)} %copy-done.12, ...), custom_call_target="tpu_custom_call" | custom-call | bytes 6553600 | tf_op jit(solution)/shard_map/pack/pallas_call | solution.py:258
  39.3 8.9 %all-to-all-start.1 = ((bf16[16,272,128]{2,1,0:T(8,128)(2,1)}), bf16[16,272,128]{2,1,0:T(8,128)(2,1)}, u32[]{:S(2)}, u32[]{:S(2)}) async-start(bf16[16,272,128]{2,1,0:T(8,128)(2,1)} %get-tuple-element.47), calls=%async_computation.1 | async-start | bytes 2228224 | tf_op jit(solution)/shard_map/all_to_all | solution.py:698
  49.8 3.8 %collective-permute-start.4 = (bf16[16,144,128]{2,1,0:T(8,128)(2,1)S(1)}, bf16[16,144,128]{2,1,0:T(8,128)(2,1)S(1)}, u32[]{:S(2)}, u32[]{:S(2)}) collective-permute-start(bf16[16,144,128]{2,1,0:T(8,128)(2,1)S(1)} %copy-done.18), channel_id=1, source_target_pairs={{64,0},{68,4},{72,8},{76,12},{80,16},{84,20},{88,24},{92,28},{96,3... | collective-permute-start | bytes 1769480 | tf_op jit(solution)/shard_map/ppermute | solution.py:710
  53.6 12.8 %collective-permute-done.4.near.refs_3_ = bf16[16,144,128]{2,1,0:T(8,128)(2,1)S(1)} collective-permute-done((bf16[16,144,128]{2,1,0:T(8,128)(2,1)S(1)}, bf16[16,144,128]{2,1,0:T(8,128)(2,1)S(1)}, u32[]{:S(2)}, u32[]{:S(2)}) %collective-permute-start.4) | collective-permute-done | bytes 589856 | tf_op jit(solution)/shard_map/ppermute | solution.py:710
  66.4 8.0 %collective-permute-done.3.far = bf16[16,272,128]{2,1,0:T(8,128)(2,1)S(1)} collective-permute-done((bf16[16,272,128]{2,1,0:T(8,128)(2,1)}, bf16[16,272,128]{2,1,0:T(8,128)(2,1)S(1)}, u32[]{:S(2)}, u32[]{:S(2)}) %collective-permute-start.3) | collective-permute-done | bytes 1114144 | tf_op jit(solution)/shard_map/ppermute | solution.py:709
  76.4 7.1 %all-to-all-start = ((bf16[16,400,128]{2,1,0:T(8,128)(2,1)}), bf16[16,400,128]{2,1,0:T(8,128)(2,1)}, u32[]{:S(2)}, u32[]{:S(2)}) async-start(bf16[16,400,128]{2,1,0:T(8,128)(2,1)} %insert.1), calls=%async_computation | async-start | bytes 3276800 | tf_op jit(solution)/shard_map/all_to_all | solution.py:698
  85.7 2.3 collective-permute-start.6
  89.6 5.1 %collective-permute-done.5.refs_1_ = bf16[256,512]{1,0:T(8,128)(2,1)S(1)} collective-permute-done((bf16[256,512]{1,0:T(8,128)(2,1)S(1)}, bf16[256,512]{1,0:T(8,128)(2,1)S(1)}, u32[]{:S(2)}, u32[]{:S(2)}) %collective-permute-start.5) | collective-permute-done | bytes 262176 | tf_op jit(solution)/shard_map/ppermute | solution.py:153
  94.7 5.5 %collective-permute-done.6.refs_2_ = bf16[256,512]{1,0:T(8,128)(2,1)S(1)} collective-permute-done((bf16[256,512]{1,0:T(8,128)(2,1)S(1)}, bf16[256,512]{1,0:T(8,128)(2,1)S(1)}, u32[]{:S(2)}, u32[]{:S(2)}) %collective-permute-start.6) | collective-permute-done | bytes 262176 | tf_op jit(solution)/shard_map/ppermute | solution.py:153
  103.9 9.1 %gate.2.refs_5_ = bf16[16,272,128]{2,1,0:T(8,128)(2,1)} custom-call(s32[2]{0:T(128)} %pad_add_fusion.meta.refs_0_, bf16[16,272,128]{2,1,0:T(8,128)(2,1)} %all-to-all-done.1.refs_1_, bf16[1024,512]{1,0:T(8,128)(2,1)} %copy-done.3), custom_call_target="tpu_custom_call" | custom-call | flops 2147483648 | bytes 8388608 | tf_op jit(solution)/shard_map/gate/pallas_call | solution.py:493
  113.0 14.6 %collective-permute-done.8.refs_3_ = bf16[1024,512]{1,0:T(8,128)(2,1)S(1)} collective-permute-done((bf16[1024,512]{1,0:T(8,128)(2,1)S(1)}, bf16[1024,512]{1,0:T(8,128)(2,1)S(1)}, u32[]{:S(2)}, u32[]{:S(2)}) %collective-permute-start.8) | collective-permute-done | bytes 1048608 | tf_op jit(solution)/shard_map/ppermute | solution.py:713
  127.7 3.7 %collective-permute-done.9.refs_4_ = bf16[1024,512]{1,0:T(8,128)(2,1)S(1)} collective-permute-done((bf16[1024,512]{1,0:T(8,128)(2,1)S(1)}, bf16[1024,512]{1,0:T(8,128)(2,1)S(1)}, u32[]{:S(2)}, u32[]{:S(2)}) %collective-permute-start.9) | collective-permute-done | bytes 1048608 | tf_op jit(solution)/shard_map/ppermute | solution.py:714
  132.5 13.9 %gate.3 = (bf16[16,400,128]{2,1,0:T(8,128)(2,1)}, bf16[16,272,128]{2,1,0:T(8,128)(2,1)}) custom-call(s32[2]{0:T(128)} %pad_add_fusion.meta.refs_0_, bf16[16,400,128]{2,1,0:T(8,128)(2,1)} %all-to-all-done.refs_1_, bf16[1024,512]{1,0:T(8,128)(2,1)} %copy-done.3, bf16[1024,512]{1,0:T(8,128)(2,1)} %copy-done.16, ...), custom_call_target="tpu_custom_call", output_to_operand_aliasing={{1}: (5, {})} | custom-call | flops 3221225472 | bytes 8388608 | tf_op jit(solution)/shard_map/gate/pallas_call | solution.py:493
  146.4 6.8 %all-to-all-start.2 = ((bf16[16,400,128]{2,1,0:T(8,128)(2,1)}), bf16[16,400,128]{2,1,0:T(8,128)(2,1)S(1)}, u32[]{:S(2)}, u32[]{:S(2)}) async-start(bf16[16,400,128]{2,1,0:T(8,128)(2,1)} %get-tuple-element.48), calls=%async_computation.2 | async-start | bytes 3276800 | tf_op jit(solution)/shard_map/all_to_all | solution.py:698
  153.1 15.2 %own.1 = (f32[512,1024]{1,0:T(8,128)}, f32[512,1024]{1,0:T(8,128)}, f32[32,128]{1,0:T(8,128)}, f32[32,128]{1,0:T(8,128)}, bf16[16,272,128]{2,1,0:T(8,128)(2,1)}) custom-call(s32[2]{0:T(128)} %pad_add_fusion.meta.refs_0_, bf16[256,4096]{1,0:T(8,128)(2,1)} %q0.3, bf16[256,1024]{1,0:T(8,128)(2,1)} %copy-done.12, ...), custom_call_target="tpu_custom_call", output_to_operand_aliasing={{4}: (6, {})} | custom-call | flops 2684354560 | bytes 8388608 | tf_op jit(solution)/shard_map/own/pallas_call | solution.py:563
  168.3 24.1 %all-to-all-done.2.back.refs_2_ = bf16[16,400,128]{2,1,0:T(8,128)(2,1)S(1)} async-done(((bf16[16,400,128]{2,1,0:T(8,128)(2,1)}), bf16[16,400,128]{2,1,0:T(8,128)(2,1)S(1)}, u32[]{:S(2)}, u32[]{:S(2)}) %all-to-all-start.2) | async-done | bytes 1638432 | tf_op jit(solution)/shard_map/all_to_all | solution.py:698
  192.4 4.8 %all-to-all-start.3 = ((bf16[16,272,128]{2,1,0:T(8,128)(2,1)}), bf16[16,272,128]{2,1,0:T(8,128)(2,1)S(1)}, u32[]{:S(2)}, u32[]{:S(2)}) async-start(bf16[16,272,128]{2,1,0:T(8,128)(2,1)} %get-tuple-element.50), calls=%async_computation.3 | async-start | bytes 2228224 | tf_op jit(solution)/shard_map/all_to_all | solution.py:698
  201.5 23.8 %all-to-all-done.3.refs_3_ = bf16[16,272,128]{2,1,0:T(8,128)(2,1)S(1)} async-done(((bf16[16,272,128]{2,1,0:T(8,128)(2,1)}), bf16[16,272,128]{2,1,0:T(8,128)(2,1)S(1)}, u32[]{:S(2)}, u32[]{:S(2)}) %all-to-all-start.3) | async-done | bytes 1114144 | tf_op jit(solution)/shard_map/all_to_all | solution.py:698
  225.3 3.7 %collective-permute-done.10.refs_4_ = bf16[16,272,128]{2,1,0:T(8,128)(2,1)} collective-permute-done((bf16[16,272,128]{2,1,0:T(8,128)(2,1)}, bf16[16,272,128]{2,1,0:T(8,128)(2,1)}, u32[]{:S(2)}, u32[]{:S(2)}) %collective-permute-start.10) | collective-permute-done | bytes 1114144 | tf_op jit(solution)/shard_map/ppermute | solution.py:722
  230.6 5.6 %merge.2 = (bf16[128,1024]{1,0:T(8,128)(2,1)S(1)}, bf16[128,1024]{1,0:T(8,128)(2,1)S(1)}, bf16[128,1024]{1,0:T(8,128)(2,1)S(1)}, bf16[128,1024]{1,0:T(8,128)(2,1)S(1)}) custom-call(s32[2]{0:T(128)S(1)} %copy-done.8, s32[192]{0:T(256)S(1)} %get-tuple-element.35.refs_1_, bf16[16,400,128]{2,1,0:T(8,128)(2,1)S(1)} %all-to-all-done.2.back.refs_2_, ...), custom_call_target="tpu_custom_call" | custom-call | flops 10485760 | bytes 8388608 | tf_op jit(solution)/shard_map/merge/pallas_call | solution.py:646
  236.2 2.7 %collective-permute-start.12 = (bf16[128,1024]{1,0:T(8,128)(2,1)S(1)}, bf16[128,1024]{1,0:T(8,128)(2,1)S(1)}, u32[]{:S(2)}, u32[]{:S(2)}) collective-permute-start(bf16[128,1024]{1,0:T(8,128)(2,1)S(1)} %get-tuple-element.56), channel_id=1, source_target_pairs={{0,1},{1,2},{2,3},{3,0},{4,5},{5,6},{6,7},{7,4},{8,9},{9,10},{10,1... | collective-permute-start | bytes 786440 | tf_op jit(solution)/shard_map/ppermute | solution.py:153
  238.9 2.5 collective-permute-start.13
  243.0 5.6 %merge.3 = (bf16[128,1024]{1,0:T(8,128)(2,1)S(1)}, bf16[128,1024]{1,0:T(8,128)(2,1)S(1)}, bf16[128,1024]{1,0:T(8,128)(2,1)S(1)}, bf16[128,1024]{1,0:T(8,128)(2,1)S(1)}) custom-call(s32[2]{0:T(128)S(1)} %copy-done.8, s32[192]{0:T(256)S(1)} %get-tuple-element.35.refs_1_, bf16[16,400,128]{2,1,0:T(8,128)(2,1)S(1)} %all-to-all-done.2.back.refs_2_, ...), custom_call_target="tpu_custom_call" | custom-call | flops 10485760 | bytes 8388608 | tf_op jit(solution)/shard_map/merge/pallas_call | solution.py:646
  252.0 2.2 collective-permute-done.13.refs_2_
  254.2 5.6 %collective-permute-done.15.refs_5_ = bf16[128,1024]{1,0:T(8,128)(2,1)S(1)} collective-permute-done((bf16[128,1024]{1,0:T(8,128)(2,1)S(1)}, bf16[128,1024]{1,0:T(8,128)(2,1)S(1)}, u32[]{:S(2)}, u32[]{:S(2)}) %collective-permute-start.15) | collective-permute-done | bytes 262176 | tf_op jit(solution)/shard_map/ppermute | solution.py:153
  259.8 4.2 %collective-permute-done.16.refs_6_ = bf16[128,1024]{1,0:T(8,128)(2,1)S(1)} collective-permute-done((bf16[128,1024]{1,0:T(8,128)(2,1)S(1)}, bf16[128,1024]{1,0:T(8,128)(2,1)S(1)}, u32[]{:S(2)}, u32[]{:S(2)}) %collective-permute-start.16) | collective-permute-done | bytes 262176 | tf_op jit(solution)/shard_map/ppermute | solution.py:153
  264.1 2.1 finish.1
  (66 shorter events, 27.7 us)
Async XLA Ops:
  0.0 9.6 %copy-start.15 = (s32[8,8,3]{1,0,2:T(8,128)S(1)}, s32[8,8,3]{1,0,2:T(8,128)}, u32[]{:S(2)}) copy-start(s32[8,8,3]{1,0,2:T(8,128)} %param.7) | copy-start | bytes 2308
  3.7 15.2 %collective-permute-start = (bf16[256,1024]{1,0:T(8,128)(2,1)}, bf16[256,1024]{1,0:T(8,128)(2,1)S(1)}, u32[]{:S(2)}, u32[]{:S(2)}) collective-permute-start(bf16[256,1024]{1,0:T(8,128)(2,1)} %get-tuple-element.37), channel_id=1, source_target_pairs={{0,1},{1,2},{2,3},{3,0},{4,5},{5,6},{6,7},{7,4},{8,9},{9,10},{10,1... | collective-permute-start | bytes 1572872 | tf_op jit(solution)/shard_map/ppermute | solution.py:153
  5.3 26.0 %collective-permute-start.1 = (bf16[256,1024]{1,0:T(8,128)(2,1)}, bf16[256,1024]{1,0:T(8,128)(2,1)S(1)}, u32[]{:S(2)}, u32[]{:S(2)}) collective-permute-start(bf16[256,1024]{1,0:T(8,128)(2,1)} %get-tuple-element.38), channel_id=1, source_target_pairs={{0,2},{1,3},{2,0},{3,1},{4,6},{5,7},{6,4},{7,5},{8,10},{9,11},{10,... | collective-permute-start | bytes 1572872 | tf_op jit(solution)/shard_map/ppermute | solution.py:153
  8.2 23.1 %collective-permute-start.2 = (bf16[256,1024]{1,0:T(8,128)(2,1)}, bf16[256,1024]{1,0:T(8,128)(2,1)S(1)}, u32[]{:S(2)}, u32[]{:S(2)}) collective-permute-start(bf16[256,1024]{1,0:T(8,128)(2,1)} %get-tuple-element.39), channel_id=1, source_target_pairs={{0,3},{1,0},{2,1},{3,2},{4,7},{5,4},{6,5},{7,6},{8,11},{9,8},{10,9... | collective-permute-start | bytes 1572872 | tf_op jit(solution)/shard_map/ppermute | solution.py:153
  16.0 15.3 %copy-start.11 = (s32[128]{0:T(128)}, s32[128]{0:T(128)S(1)}, u32[]{:S(2)}) copy-start(s32[128]{0:T(128)S(1)} %get-tuple-element.36.table) | copy-start | bytes 1540
  18.9 12.4 %copy-start.12 = (bf16[256,1024]{1,0:T(8,128)(2,1)}, bf16[256,1024]{1,0:T(8,128)(2,1)S(1)}, u32[]{:S(2)}) copy-start(bf16[256,1024]{1,0:T(8,128)(2,1)S(1)} %collective-permute-done.q1) | copy-start | bytes 1572868
  39.3 10.6 %copy-start.18 = (bf16[16,144,128]{2,1,0:T(8,128)(2,1)S(1)}, bf16[16,144,128]{2,1,0:T(8,128)(2,1)}, u32[]{:S(2)}) copy-start(bf16[16,144,128]{2,1,0:T(8,128)(2,1)} %get-tuple-element.42) | copy-start | bytes 1769476
  39.3 35.1 %copy-start.2 = (bf16[16,400,128]{2,1,0:T(8,128)(2,1)S(1)}, bf16[16,400,128]{2,1,0:T(8,128)(2,1)}, u32[]{:S(2)}) copy-start(bf16[16,400,128]{2,1,0:T(8,128)(2,1)} %get-tuple-element.40.z_in) | copy-start | bytes 4915204
  39.3 35.1 %copy-start.7 = (s32[2]{0:T(128)S(1)}, s32[2]{0:T(128)}, u32[]{:S(2)}) copy-start(s32[2]{0:T(128)} %pad_add_fusion.meta.refs_0_) | copy-start | bytes 28
  39.3 37.1 %all-to-all-start.1 = ((bf16[16,272,128]{2,1,0:T(8,128)(2,1)}), bf16[16,272,128]{2,1,0:T(8,128)(2,1)}, u32[]{:S(2)}, u32[]{:S(2)}) async-start(bf16[16,272,128]{2,1,0:T(8,128)(2,1)} %get-tuple-element.47), calls=%async_computation.1 | async-start | bytes 2228224 | tf_op jit(solution)/shard_map/all_to_all | solution.py:698
  48.2 26.2 %collective-permute-start.3 = (bf16[16,272,128]{2,1,0:T(8,128)(2,1)}, bf16[16,272,128]{2,1,0:T(8,128)(2,1)S(1)}, u32[]{:S(2)}, u32[]{:S(2)}) collective-permute-start(bf16[16,272,128]{2,1,0:T(8,128)(2,1)} %get-tuple-element.41), channel_id=1, source_target_pairs={{192,0},{196,4},{200,8},{204,12},{208,16},{212,20},{216,24},{220,2... | collective-permute-start | bytes 3342344 | tf_op jit(solution)/shard_map/ppermute | solution.py:709
  49.8 16.5 %collective-permute-start.4 = (bf16[16,144,128]{2,1,0:T(8,128)(2,1)S(1)}, bf16[16,144,128]{2,1,0:T(8,128)(2,1)S(1)}, u32[]{:S(2)}, u32[]{:S(2)}) collective-permute-start(bf16[16,144,128]{2,1,0:T(8,128)(2,1)S(1)} %copy-done.18), channel_id=1, source_target_pairs={{64,0},{68,4},{72,8},{76,12},{80,16},{84,20},{88,24},{92,28},{96,3... | collective-permute-start | bytes 1769480 | tf_op jit(solution)/shard_map/ppermute | solution.py:710
  76.4 55.0 %all-to-all-start = ((bf16[16,400,128]{2,1,0:T(8,128)(2,1)}), bf16[16,400,128]{2,1,0:T(8,128)(2,1)}, u32[]{:S(2)}, u32[]{:S(2)}) async-start(bf16[16,400,128]{2,1,0:T(8,128)(2,1)} %insert.1), calls=%async_computation | async-start | bytes 3276800 | tf_op jit(solution)/shard_map/all_to_all | solution.py:698
  84.5 10.2 %collective-permute-start.5 = (bf16[256,512]{1,0:T(8,128)(2,1)S(1)}, bf16[256,512]{1,0:T(8,128)(2,1)S(1)}, u32[]{:S(2)}, u32[]{:S(2)}) collective-permute-start(bf16[256,512]{1,0:T(8,128)(2,1)S(1)} %get-tuple-element.44), channel_id=1, source_target_pairs={{0,1},{1,2},{2,3},{3,0},{4,5},{5,6},{6,7},{7,4},{8,9},{9,10},{10,1... | collective-permute-start | bytes 786440 | tf_op jit(solution)/shard_map/ppermute | solution.py:153
  85.7 14.5 %collective-permute-start.6 = (bf16[256,512]{1,0:T(8,128)(2,1)S(1)}, bf16[256,512]{1,0:T(8,128)(2,1)S(1)}, u32[]{:S(2)}, u32[]{:S(2)}) collective-permute-start(bf16[256,512]{1,0:T(8,128)(2,1)S(1)} %get-tuple-element.45), channel_id=1, source_target_pairs={{0,2},{1,3},{2,0},{3,1},{4,6},{5,7},{6,4},{7,5},{8,10},{9,11},{10,... | collective-permute-start | bytes 786440 | tf_op jit(solution)/shard_map/ppermute | solution.py:153
  88.0 12.6 %collective-permute-start.7 = (bf16[256,512]{1,0:T(8,128)(2,1)S(1)}, bf16[256,512]{1,0:T(8,128)(2,1)S(1)}, u32[]{:S(2)}, u32[]{:S(2)}) collective-permute-start(bf16[256,512]{1,0:T(8,128)(2,1)S(1)} %get-tuple-element.46), channel_id=1, source_target_pairs={{0,3},{1,0},{2,1},{3,2},{4,7},{5,4},{6,5},{7,6},{8,11},{9,8},{10,9... | collective-permute-start | bytes 786440 | tf_op jit(solution)/shard_map/ppermute | solution.py:153
  101.3 26.4 %collective-permute-start.8 = (bf16[1024,512]{1,0:T(8,128)(2,1)S(1)}, bf16[1024,512]{1,0:T(8,128)(2,1)S(1)}, u32[]{:S(2)}, u32[]{:S(2)}) collective-permute-start(bf16[1024,512]{1,0:T(8,128)(2,1)S(1)} %join.1.refs_2_.kv), channel_id=1, source_target_pairs={{0,64},{4,68},{8,72},{12,76},{16,80},{20,84},{24,88},{28,92},{32,9... | collective-permute-start | bytes 3145736 | tf_op jit(solution)/shard_map/ppermute | solution.py:713
  102.6 28.8 %collective-permute-start.9 = (bf16[1024,512]{1,0:T(8,128)(2,1)S(1)}, bf16[1024,512]{1,0:T(8,128)(2,1)S(1)}, u32[]{:S(2)}, u32[]{:S(2)}) collective-permute-start(bf16[1024,512]{1,0:T(8,128)(2,1)S(1)} %join.1.refs_2_.kv), channel_id=1, source_target_pairs={{64,192},{68,196},{72,200},{76,204},{80,208},{84,212},{88,216},{92... | collective-permute-start | bytes 3145736 | tf_op jit(solution)/shard_map/ppermute | solution.py:714
  146.4 46.0 %all-to-all-start.2 = ((bf16[16,400,128]{2,1,0:T(8,128)(2,1)}), bf16[16,400,128]{2,1,0:T(8,128)(2,1)S(1)}, u32[]{:S(2)}, u32[]{:S(2)}) async-start(bf16[16,400,128]{2,1,0:T(8,128)(2,1)} %get-tuple-element.48), calls=%async_computation.2 | async-start | bytes 3276800 | tf_op jit(solution)/shard_map/all_to_all | solution.py:698
  192.4 32.9 %all-to-all-start.3 = ((bf16[16,272,128]{2,1,0:T(8,128)(2,1)}), bf16[16,272,128]{2,1,0:T(8,128)(2,1)S(1)}, u32[]{:S(2)}, u32[]{:S(2)}) async-start(bf16[16,272,128]{2,1,0:T(8,128)(2,1)} %get-tuple-element.50), calls=%async_computation.3 | async-start | bytes 2228224 | tf_op jit(solution)/shard_map/all_to_all | solution.py:698
  197.2 31.7 %copy-start.8 = (s32[2]{0:T(128)S(1)}, s32[2]{0:T(128)}, u32[]{:S(2)}) copy-start(s32[2]{0:T(128)} %pad_add_fusion.meta.refs_0_) | copy-start | bytes 28
  197.3 31.7 %copy-start.10 = (f32[32,128]{1,0:T(8,128)S(1)}, f32[32,128]{1,0:T(8,128)}, u32[]{:S(2)}) copy-start(f32[32,128]{1,0:T(8,128)} %get-tuple-element.54.refs_7_) | copy-start | bytes 49156
  198.6 30.3 %collective-permute-start.10 = (bf16[16,272,128]{2,1,0:T(8,128)(2,1)}, bf16[16,272,128]{2,1,0:T(8,128)(2,1)}, u32[]{:S(2)}, u32[]{:S(2)}) collective-permute-start(bf16[16,272,128]{2,1,0:T(8,128)(2,1)} %get-tuple-element.51), channel_id=1, source_target_pairs={{0,192},{4,196},{8,200},{12,204},{16,208},{20,212},{24,216},{28,22... | collective-permute-start | bytes 3342344 | tf_op jit(solution)/shard_map/ppermute | solution.py:722
  199.9 25.4 %collective-permute-start.11 = (bf16[16,144,128]{2,1,0:T(8,128)(2,1)}, bf16[16,144,128]{2,1,0:T(8,128)(2,1)S(1)}, u32[]{:S(2)}, u32[]{:S(2)}) collective-permute-start(bf16[16,144,128]{2,1,0:T(8,128)(2,1)} %get-tuple-element.52), channel_id=1, source_target_pairs={{0,64},{4,68},{8,72},{12,76},{16,80},{20,84},{24,88},{28,92},{32,9... | collective-permute-start | bytes 1769480 | tf_op jit(solution)/shard_map/ppermute | solution.py:723
  230.6 12.5 %copy-start = (f32[512,1024]{1,0:T(8,128)S(1)}, f32[512,1024]{1,0:T(8,128)}, u32[]{:S(2)}) copy-start(f32[512,1024]{1,0:T(8,128)} %get-tuple-element.59.refs_6_) | copy-start | bytes 6291460
  230.6 12.5 %copy-start.9 = (f32[32,128]{1,0:T(8,128)S(1)}, f32[32,128]{1,0:T(8,128)}, u32[]{:S(2)}) copy-start(f32[32,128]{1,0:T(8,128)} %get-tuple-element.60.refs_7_) | copy-start | bytes 49156
  236.2 14.0 %collective-permute-start.12 = (bf16[128,1024]{1,0:T(8,128)(2,1)S(1)}, bf16[128,1024]{1,0:T(8,128)(2,1)S(1)}, u32[]{:S(2)}, u32[]{:S(2)}) collective-permute-start(bf16[128,1024]{1,0:T(8,128)(2,1)S(1)} %get-tuple-element.56), channel_id=1, source_target_pairs={{0,1},{1,2},{2,3},{3,0},{4,5},{5,6},{6,7},{7,4},{8,9},{9,10},{10,1... | collective-permute-start | bytes 786440 | tf_op jit(solution)/shard_map/ppermute | solution.py:153
  238.9 15.3 %collective-permute-start.13 = (bf16[128,1024]{1,0:T(8,128)(2,1)S(1)}, bf16[128,1024]{1,0:T(8,128)(2,1)S(1)}, u32[]{:S(2)}, u32[]{:S(2)}) collective-permute-start(bf16[128,1024]{1,0:T(8,128)(2,1)S(1)} %get-tuple-element.57), channel_id=1, source_target_pairs={{0,2},{1,3},{2,0},{3,1},{4,6},{5,7},{6,4},{7,5},{8,10},{9,11},{10,... | collective-permute-start | bytes 786440 | tf_op jit(solution)/shard_map/ppermute | solution.py:153
  241.4 12.8 %collective-permute-start.14 = (bf16[128,1024]{1,0:T(8,128)(2,1)S(1)}, bf16[128,1024]{1,0:T(8,128)(2,1)S(1)}, u32[]{:S(2)}, u32[]{:S(2)}) collective-permute-start(bf16[128,1024]{1,0:T(8,128)(2,1)S(1)} %get-tuple-element.58), channel_id=1, source_target_pairs={{0,3},{1,0},{2,1},{3,2},{4,7},{5,4},{6,5},{7,6},{8,11},{9,8},{10,9... | collective-permute-start | bytes 786440 | tf_op jit(solution)/shard_map/ppermute | solution.py:153
  248.7 11.1 %collective-permute-start.15 = (bf16[128,1024]{1,0:T(8,128)(2,1)S(1)}, bf16[128,1024]{1,0:T(8,128)(2,1)S(1)}, u32[]{:S(2)}, u32[]{:S(2)}) collective-permute-start(bf16[128,1024]{1,0:T(8,128)(2,1)S(1)} %get-tuple-element.62), channel_id=1, source_target_pairs={{0,1},{1,2},{2,3},{3,0},{4,5},{5,6},{6,7},{7,4},{8,9},{9,10},{10,1... | collective-permute-start | bytes 786440 | tf_op jit(solution)/shard_map/ppermute | solution.py:153
  249.1 14.9 %collective-permute-start.16 = (bf16[128,1024]{1,0:T(8,128)(2,1)S(1)}, bf16[128,1024]{1,0:T(8,128)(2,1)S(1)}, u32[]{:S(2)}, u32[]{:S(2)}) collective-permute-start(bf16[128,1024]{1,0:T(8,128)(2,1)S(1)} %get-tuple-element.63), channel_id=1, source_target_pairs={{0,2},{1,3},{2,0},{3,1},{4,6},{5,7},{6,4},{7,5},{8,10},{9,11},{10,... | collective-permute-start | bytes 786440 | tf_op jit(solution)/shard_map/ppermute | solution.py:153
  250.2 13.8 %collective-permute-start.17 = (bf16[128,1024]{1,0:T(8,128)(2,1)S(1)}, bf16[128,1024]{1,0:T(8,128)(2,1)S(1)}, u32[]{:S(2)}, u32[]{:S(2)}) collective-permute-start(bf16[128,1024]{1,0:T(8,128)(2,1)S(1)} %get-tuple-element.64), channel_id=1, source_target_pairs={{0,3},{1,0},{2,1},{3,2},{4,7},{5,4},{6,5},{7,6},{8,11},{9,8},{10,9... | collective-permute-start | bytes 786440 | tf_op jit(solution)/shard_map/ppermute | solution.py:153
  (9 other events, 34.3 us)

commit v3 on v2

--- a/solution.py
+++ b/solution.py
@@ -63,15 +63,16 @@
         table[2 * i + 1] = -1
         return 0
 
-    def note(e, _):
+    def note(pair, k):
+        e = 3 * pair + k
         b = gates[e]
         place[e] = UNUSED // 16 * 1024 + 32 * 16
 
         @pl.when(b >= 0)
         def _():
             rank = (table[2 * b] >= 0).astype(I32)
-            table[2 * b + rank] = e
-            target = lax.div(b, ROW)
+            table[2 * b + rank] = pair
+            target = lax.shift_right_logical(b, 4)
             away = me - target
             far = jnp.logical_and(me >= 2, target == 0)
             four = jnp.logical_or(
@@ -81,12 +82,15 @@
             row = jnp.where(four, EXTRA + jnp.where(rank == 0, LOG_AT, NEAR_AT), row)
             slot = jnp.where(away == 0, 8, jnp.where(far, 18, 2)) + rank
             slot = jnp.where(four, 4 + 24 * rank, slot)
-            place[e] = lax.div(row, 16) * 1024 + slot * 16 + lax.rem(b, ROW)
-
+            place[e] = row * 64 + slot * 16 + jnp.bitwise_and(b, 15)
+
+    def notes(pair, _):
+        for k in range(3):
+            note(pair, k)
         return 0
 
     lax.fori_loop(0, table.shape[0] // 2, clear, 0)
-    lax.fori_loop(0, gates.shape[0], note, 0)
+    lax.fori_loop(0, gates.shape[0] // 3, notes, 0)
 
 
 def plan(meta, gates, blocks):
@@ -100,9 +104,9 @@
     )(meta, gates)
 
 
-def split_kernel(count, first, meta, *refs):
-    ins, outs = refs[:count], refs[-2 - 2 * (N_HEAD - first) : -2 - (N_HEAD - first)]
-    boxes, (reads, saves) = refs[-2 - (N_HEAD - first) : -2], refs[-2:]
+def split_kernel(count, first, parts, meta, *refs):
+    ins, outs = refs[:count], refs[-2 - 2 * parts : -2 - parts]
+    boxes, (reads, saves) = refs[-2 - parts : -2], refs[-2:]
     loads = []
     for i, box in enumerate(boxes):
         g = lax.rem(meta[1] + first + i, N_HEAD)
@@ -123,12 +127,12 @@
         copy.wait()
 
 
-def split(meta, first, ins, *earlier):
+def split(meta, first, end, ins, *earlier):
     rows, wide = ins[0].shape[0], sum(x.shape[1] for x in ins) // N_HEAD
-    parts = N_HEAD - first
+    parts = end - first
 
     def kernel(*refs):
-        split_kernel(len(ins), first, *refs)
+        split_kernel(len(ins), first, parts, *refs)
 
     return pl.pallas_call(
         kernel,
@@ -187,8 +191,9 @@
     )(meta, *pieces)
 
 
-def pack_kernel(meta, table, q0, q1, q2, q3, *refs):
-    outs, boxes, q_all, sems = refs[:4], refs[4:8], refs[8], refs[9]
+def pack_kernel(late, meta, table, q0, q1, q2, q3, *refs):
+    count = (len(refs) - 2) // 2
+    outs, boxes, q_all, sems = refs[:count], refs[count : 2 * count], refs[-2], refs[-1]
     me = meta[0] // ROW
     for copy in run_copies(by_source(meta[1], (q0, q1, q2, q3), q_all), sems):
         copy.wait()
@@ -198,36 +203,34 @@
         return table[2 * (jnp.maximum(target, 0) * ROW + j) + rank]
 
     def fill(into, j, row, target, rank):
-        e = entry(j, target, rank)
-
-        @pl.when(jnp.logical_and(target >= 0, e >= 0))
-        def _():
-            tile = lax.div(e, 24)
-            head = lax.rem(lax.div(e, 3), 8)
-            into[j, row : row + R, :] = q_all[
-                pl.ds(pl.multiple_of(tile * R, R), R),
-                pl.ds(pl.multiple_of(head * HEAD_DIM, HEAD_DIM), HEAD_DIM),
-            ]
+        e = jnp.maximum(entry(j, target, rank), 0)
+        tile = lax.shift_right_logical(e, 3)
+        head = jnp.bitwise_and(e, 7)
+        into[j, row : row + R, :] = q_all[
+            pl.ds(pl.multiple_of(tile * R, R), R),
+            pl.ds(pl.multiple_of(head * HEAD_DIM, HEAD_DIM), HEAD_DIM),
+        ]
 
     def codes(j, *slots):
         marks = jnp.full((EXTRA, 128), -1, I32)
         for slot, target, rank in slots:
             e = entry(j, target, rank)
-            kv_head = lax.div(lax.rem(lax.div(e, 3), 8), 4)
+            kv_head = jnp.bitwise_and(lax.shift_right_logical(e, 2), 1)
             code = jnp.where(jnp.logical_and(target >= 0, e >= 0), kv_head, -1)
             marks = jnp.where(lane == slot, code, marks)
         return marks.astype(F32).astype(BF16)
 
-    z1, z2, far, near = boxes
     split_row = jnp.where(me == 3, 1, me - 1)
 
     def own_row(j, _):
+        z1 = boxes[2]
         fill(z1, j, 0, me, 0)
         fill(z1, j, R, me, 1)
         z1[j, 2 * R :, :] = codes(j, (0, me, 0), (1, me, 1))
         return 0
 
     def moved(j, _):
+        far, near = boxes[:2]
         fill(far, j, 0, 0, 0)
         fill(far, j, R, 0, 1)
         far[j, 2 * R :, :] = codes(j, (2, 0, 0), (3, 0, 1))
@@ -236,6 +239,7 @@
         return 0
 
     def other_rows(j, _):
+        z2 = boxes[0]
         fill(z2, j, 0, me - 1, 0)
         fill(z2, j, R, me - 1, 1)
         fill(z2, j, 2 * R, split_row, 0)
@@ -243,8 +247,9 @@
         return 0
 
     saves = []
-    for work, group in ((moved, (2, 3)), (own_row, (0,)), (other_rows, (1,))):
-        lax.fori_loop(0, ROW, work, 0)
+    works = ((other_rows, (0,)),) if late else ((moved, (0, 1)), (own_row, (2,)))
+    for work, group in works:
+        lax.fori_loop(0, ROW, work, 0, unroll=2)
         for i in group:
             saves.append(pltpu.make_async_copy(boxes[i], outs[i], sems.at[N_HEAD + i]))
             saves[-1].start()
@@ -252,11 +257,15 @@
         save.wait()
 
 
-def pack(meta, table, q_parts):
+def pack(meta, late, table, q_parts):
     rows, wide = q_parts[1].shape
-    sizes = (SEND[0], SEND[1], FAR, NEAR)
-    return pl.pallas_call(
-        pack_kernel,
+    sizes = (SEND[1],) if late else (FAR, NEAR, SEND[0])
+
+    def kernel(*refs):
+        pack_kernel(late, *refs)
+
+    return pl.pallas_call(
+        kernel,
         out_shape=[shaped((ROW, size, HEAD_DIM)) for size in sizes],
         in_specs=[SMEM, SMEM] + [HBM] * N_HEAD,
         out_specs=[HBM] * len(sizes),
@@ -265,7 +274,7 @@
             pltpu.VMEM((N_HEAD * rows, wide), BF16),
             pltpu.SemaphoreType.DMA((N_HEAD + len(sizes),)),
         ],
-        compiler_params=params(56),
+        compiler_params=params(8 if late else 56),
         cost_estimate=cost(0, 2 * (N_HEAD * rows * wide + ROW * sum(sizes) * HEAD_DIM)),
         name="pack",
     )(meta, table, *q_parts)
@@ -446,14 +455,14 @@
             loads[group].wait()
             pltpu.make_async_copy(kvs[0], kv.at[group], kv_sems.at[group]).wait()
 
-        def batch(n, _, i=i, group=group, kv_head=kv_head, count=count):
+        def batch(first, width, i=i, group=group, kv_head=kv_head, count=count):
             keys = kv[group, :, kv_head * HEAD_DIM : (kv_head + 1) * HEAD_DIM]
             values = kv[group, :, (2 + kv_head) * HEAD_DIM : (3 + kv_head) * HEAD_DIM]
             where, scores = [], []
-            for u in range(GROUP):
-                item = lists[i, jnp.minimum(n * GROUP + u, count - 1)]
-                where.append((lax.div(item, 8), lax.rem(item, 8)))
-            for u in range(0, GROUP, 2):
+            for u in range(width):
+                item = lists[i, jnp.minimum(first + u, count - 1)]
+                where.append((lax.shift_right_logical(item, 3), jnp.bitwise_and(item, 7)))
+            for u in range(0, width, 2):
                 q = [
                     z[j, pl.ds(pl.multiple_of((s - 2 * part) * R, R), R), :]
                     for j, s in where[u : u + 2]
@@ -469,9 +478,18 @@
                 high = log.astype(BF16).astype(F32)
                 logs[j, pl.ds(s, 1), :] = high
                 logs[j, pl.ds(8 + s, 1), :] = log - high
+
+        def whole(n, _, batch=batch):
+            batch(n * GROUP, GROUP)
             return 0
 
-        lax.fori_loop(0, lax.div(count + GROUP - 1, GROUP), batch, 0)
+        fours = lax.shift_right_logical(count + 1, 2)
+        lax.fori_loop(0, fours, whole, 0)
+
+        @pl.when(count > GROUP * fours)
+        def _(batch=batch, fours=fours):
+            batch(GROUP * fours, 2)
+
         if i == 1:
             save(0, 2 * R)
     for j in range(ROW):
@@ -702,14 +720,15 @@
 
 def local(queries, key_rows, value_rows, block_gates):
     meta = jnp.stack([lax.axis_index("ctx"), lax.axis_index("head")]).astype(I32)
-    q_parts = over_head([queries, *split(meta, 1, (queries,))])
+    q_parts = over_head([queries, *split(meta, 1, N_HEAD, (queries,))])
     table, place = plan(meta, block_gates.reshape(-1), lax.axis_size("ctx"))
-    first, second, far, near = pack(meta, table, q_parts)
+    far, near, first = pack(meta, False, table, q_parts)
+    (second,) = pack(meta, True, table, q_parts)
     first = over_row(first)
     far = lax.ppermute(far, "ctx", rows_to([(3, 0), (2, 1)]))
     near = lax.ppermute(near, "ctx", rows_to([(1, 0), (3, 2)]))
-    kv_cut = split(meta, 0, (key_rows, value_rows), near)
-    kv = join(meta, over_head(kv_cut))
+    kv_parts = over_head(split(meta, 0, N_HEAD, (key_rows, value_rows), near))
+    kv = join(meta, kv_parts)
     kv_one = lax.ppermute(kv, "ctx", rows_to([(0, 1), (1, 2), (2, 3)]))
     kv_two = lax.ppermute(kv, "ctx", rows_to([(1, 3)]))
     second = over_row(insert(meta, second, far, near))

time: 268 us -> 264 us (0.985)
  Pallas kernels: 72.6 us -> 68 us
  local copies, waits for them, and re-layouts: 3.93 us -> 7.52 us
    ppermute x1, waiting for transfers between devices: 12.8 us -> 8.44 us  [local(): near = lax.ppermute(near, 'ctx', rows_to([(1, 0), (3, 2)]))]
    unnamed x39 -> x45, local copies, waits for them, and re-layouts: 3.8 us -> 7.38 us
    pallas_call x1 -> x2, Pallas kernels: 6.99 us -> 5.81 us  [pack(): pl.pallas_call(kernel, out_shape=[shaped((ROW, size, HEAD_DIM)) for size...]
where the time goes in v3:
time: 264 us; the launch traced here: 263 us
  waiting for transfers between devices  127 us (48%)
  Pallas kernels  68 us (26%)
  starting transfers between devices  59.8 us (23%)
  local copies, waits for them, and re-layouts  7.52 us (3%)
    all_to_all x4, waiting for transfers between devices, over_row(): lax.all_to_all(x, 'ctx', split_axis=0, concat_axis=0, tiled=True, axis_in...  48.1 us
    ppermute x12, waiting for transfers between devices, over_head(): got.append(lax.ppermute(parts[step], 'head', pairs))  39.4 us
    all_to_all x4, starting transfers between devices, over_row(): lax.all_to_all(x, 'ctx', split_axis=0, concat_axis=0, tiled=True, axis_in...  28.8 us
    pallas_call x2, Pallas kernels, gate(): pl.pallas_call(kernel, out_shape=[shaped((ROW, SEND[part], HEAD_DIM))] +...  21 us
    ppermute x12, starting transfers between devices, over_head(): got.append(lax.ppermute(parts[step], 'head', pairs))  20.6 us
    ppermute x1, waiting for transfers between devices, local(): kv_one = lax.ppermute(kv, 'ctx', rows_to([(0, 1), (1, 2), (2, 3)]))  15.4 us
    pallas_call x1, Pallas kernels, own(): pl.pallas_call(own_kernel, out_shape=(out, out, logs, logs, shaped(held.s...  15.2 us
    pallas_call x2, Pallas kernels, merge(): pl.pallas_call(kernel, out_shape=[shaped((R, wide))] * N_HEAD, in_specs=[...  11.3 us
  transfers between devices with their start and end apart: 22, of which 15 were waited for; matrix products, arithmetic and copies ran while one was open for 0% of the time, Pallas kernels for 15%

profile of v3, /device:TPU:6, one launch (start us, length us, event | category | flops | bytes accessed | tf_op | source)
XLA Modules:
  0.0 263.0 jit_solution(6192088377814542234)
XLA Ops:
  0.6 3.0 %split.2 = (bf16[256,1024]{1,0:T(8,128)(2,1)}, bf16[256,1024]{1,0:T(8,128)(2,1)}, bf16[256,1024]{1,0:T(8,128)(2,1)}) custom-call(s32[2]{0:T(128)} %pad_add_fusion.meta.refs_0_, bf16[256,4096]{1,0:T(8,128)(2,1)} %q0.1), custom_call_target="tpu_custom_call" | custom-call | bytes 3145728 | tf_op jit(solution)/shard_map/split/pallas_call | solution.py:137
  5.3 2.9 %collective-permute-start.1 = (bf16[256,1024]{1,0:T(8,128)(2,1)}, bf16[256,1024]{1,0:T(8,128)(2,1)S(1)}, u32[]{:S(2)}, u32[]{:S(2)}) collective-permute-start(bf16[256,1024]{1,0:T(8,128)(2,1)} %get-tuple-element.37), channel_id=1, source_target_pairs={{0,2},{1,3},{2,0},{3,1},{4,6},{5,7},{6,4},{7,5},{8,10},{9,11},{10,... | collective-permute-start | bytes 1572872 | tf_op jit(solution)/shard_map/ppermute | solution.py:157
  9.8 4.7 %plan.1 = (s32[128]{0:T(128)S(1)}, s32[192]{0:T(256)S(1)}) custom-call(s32[2]{0:T(128)S(1)} %copy-done.12, s32[192]{0:T(256)S(1)} %reshape.3.gates), custom_call_target="tpu_custom_call" | custom-call | tf_op jit(solution)/shard_map/plan/pallas_call | solution.py:97
  15.0 3.8 %collective-permute-done.refs_3_.q1 = bf16[256,1024]{1,0:T(8,128)(2,1)S(1)} collective-permute-done((bf16[256,1024]{1,0:T(8,128)(2,1)}, bf16[256,1024]{1,0:T(8,128)(2,1)S(1)}, u32[]{:S(2)}, u32[]{:S(2)}) %collective-permute-start) | collective-permute-done | bytes 524320 | tf_op jit(solution)/shard_map/ppermute | solution.py:157
  18.8 12.4 %collective-permute-done.1.refs_4_.q2 = bf16[256,1024]{1,0:T(8,128)(2,1)S(1)} collective-permute-done((bf16[256,1024]{1,0:T(8,128)(2,1)}, bf16[256,1024]{1,0:T(8,128)(2,1)S(1)}, u32[]{:S(2)}, u32[]{:S(2)}) %collective-permute-start.1) | collective-permute-done | bytes 524320 | tf_op jit(solution)/shard_map/ppermute | solution.py:157
  32.2 4.3 %pack.3 = (bf16[16,272,128]{2,1,0:T(8,128)(2,1)}, bf16[16,144,128]{2,1,0:T(8,128)(2,1)}, bf16[16,272,128]{2,1,0:T(8,128)(2,1)}) custom-call(s32[2]{0:T(128)} %pad_add_fusion.meta.refs_0_, s32[128]{0:T(128)} %copy-done.17, bf16[256,4096]{1,0:T(8,128)(2,1)} %q0.1, bf16[256,1024]{1,0:T(8,128)(2,1)} %copy-done.3, bf16[256,1024]{1,0:T(8,128)(2,1)} %copy-done.5, ...), custom_call_target="tpu_custom_call" | custom-call | bytes 4915200 | tf_op jit(solution)/shard_map/pack/pallas_call | solution.py:267
  36.6 8.8 %all-to-all-start.1 = ((bf16[16,272,128]{2,1,0:T(8,128)(2,1)}), bf16[16,272,128]{2,1,0:T(8,128)(2,1)}, u32[]{:S(2)}, u32[]{:S(2)}) async-start(bf16[16,272,128]{2,1,0:T(8,128)(2,1)} %get-tuple-element.45), calls=%async_computation.1 | async-start | bytes 2228224 | tf_op jit(solution)/shard_map/all_to_all | solution.py:716
  45.4 2.5 collective-permute-start.3
  47.8 2.8 %collective-permute-start.4 = (bf16[16,144,128]{2,1,0:T(8,128)(2,1)}, bf16[16,144,128]{2,1,0:T(8,128)(2,1)S(1)}, u32[]{:S(2)}, u32[]{:S(2)}) collective-permute-start(bf16[16,144,128]{2,1,0:T(8,128)(2,1)} %get-tuple-element.40), channel_id=1, source_target_pairs={{64,0},{68,4},{72,8},{76,12},{80,16},{84,20},{88,24},{92,28},{96,3... | collective-permute-start | bytes 1769480 | tf_op jit(solution)/shard_map/ppermute | solution.py:729
  55.3 8.4 %collective-permute-done.4.near.refs_3_ = bf16[16,144,128]{2,1,0:T(8,128)(2,1)S(1)} collective-permute-done((bf16[16,144,128]{2,1,0:T(8,128)(2,1)}, bf16[16,144,128]{2,1,0:T(8,128)(2,1)S(1)}, u32[]{:S(2)}, u32[]{:S(2)}) %collective-permute-start.4) | collective-permute-done | bytes 589856 | tf_op jit(solution)/shard_map/ppermute | solution.py:729
  63.7 8.6 %collective-permute-done.3.far = bf16[16,272,128]{2,1,0:T(8,128)(2,1)S(1)} collective-permute-done((bf16[16,272,128]{2,1,0:T(8,128)(2,1)}, bf16[16,272,128]{2,1,0:T(8,128)(2,1)S(1)}, u32[]{:S(2)}, u32[]{:S(2)}) %collective-permute-start.3) | collective-permute-done | bytes 1114144 | tf_op jit(solution)/shard_map/ppermute | solution.py:728
  74.4 7.1 %all-to-all-start = ((bf16[16,400,128]{2,1,0:T(8,128)(2,1)}), bf16[16,400,128]{2,1,0:T(8,128)(2,1)}, u32[]{:S(2)}, u32[]{:S(2)}) async-start(bf16[16,400,128]{2,1,0:T(8,128)(2,1)} %insert.1), calls=%async_computation | async-start | bytes 3276800 | tf_op jit(solution)/shard_map/all_to_all | solution.py:716
  83.6 2.4 collective-permute-start.6
  87.6 5.1 %collective-permute-done.5.refs_1_ = bf16[256,512]{1,0:T(8,128)(2,1)S(1)} collective-permute-done((bf16[256,512]{1,0:T(8,128)(2,1)S(1)}, bf16[256,512]{1,0:T(8,128)(2,1)S(1)}, u32[]{:S(2)}, u32[]{:S(2)}) %collective-permute-start.5) | collective-permute-done | bytes 262176 | tf_op jit(solution)/shard_map/ppermute | solution.py:157
  92.7 5.5 %collective-permute-done.6.refs_2_ = bf16[256,512]{1,0:T(8,128)(2,1)S(1)} collective-permute-done((bf16[256,512]{1,0:T(8,128)(2,1)S(1)}, bf16[256,512]{1,0:T(8,128)(2,1)S(1)}, u32[]{:S(2)}, u32[]{:S(2)}) %collective-permute-start.6) | collective-permute-done | bytes 262176 | tf_op jit(solution)/shard_map/ppermute | solution.py:157
  101.9 8.2 %gate.2.refs_5_ = bf16[16,272,128]{2,1,0:T(8,128)(2,1)} custom-call(s32[2]{0:T(128)} %pad_add_fusion.meta.refs_0_, bf16[16,272,128]{2,1,0:T(8,128)(2,1)} %all-to-all-done.1.refs_1_, bf16[1024,512]{1,0:T(8,128)(2,1)} %copy-done.9), custom_call_target="tpu_custom_call" | custom-call | flops 2147483648 | bytes 8388608 | tf_op jit(solution)/shard_map/gate/pallas_call | solution.py:511
  110.1 15.4 %collective-permute-done.8.refs_3_ = bf16[1024,512]{1,0:T(8,128)(2,1)S(1)} collective-permute-done((bf16[1024,512]{1,0:T(8,128)(2,1)S(1)}, bf16[1024,512]{1,0:T(8,128)(2,1)S(1)}, u32[]{:S(2)}, u32[]{:S(2)}) %collective-permute-start.8) | collective-permute-done | bytes 1048608 | tf_op jit(solution)/shard_map/ppermute | solution.py:732
  125.5 2.9 %collective-permute-done.9.refs_4_ = bf16[1024,512]{1,0:T(8,128)(2,1)S(1)} collective-permute-done((bf16[1024,512]{1,0:T(8,128)(2,1)S(1)}, bf16[1024,512]{1,0:T(8,128)(2,1)S(1)}, u32[]{:S(2)}, u32[]{:S(2)}) %collective-permute-start.9) | collective-permute-done | bytes 1048608 | tf_op jit(solution)/shard_map/ppermute | solution.py:733
  129.5 12.7 %gate.3 = (bf16[16,400,128]{2,1,0:T(8,128)(2,1)}, bf16[16,272,128]{2,1,0:T(8,128)(2,1)}) custom-call(s32[2]{0:T(128)} %pad_add_fusion.meta.refs_0_, bf16[16,400,128]{2,1,0:T(8,128)(2,1)} %all-to-all-done.refs_1_, bf16[1024,512]{1,0:T(8,128)(2,1)} %copy-done.9, bf16[1024,512]{1,0:T(8,128)(2,1)} %copy-done.20, ...), custom_call_target="tpu_custom_call", output_to_operand_aliasing={{1}: (5, {})} | custom-call | flops 3221225472 | bytes 8388608 | tf_op jit(solution)/shard_map/gate/pallas_call | solution.py:511
  142.2 8.0 %all-to-all-start.2 = ((bf16[16,400,128]{2,1,0:T(8,128)(2,1)}), bf16[16,400,128]{2,1,0:T(8,128)(2,1)S(1)}, u32[]{:S(2)}, u32[]{:S(2)}) async-start(bf16[16,400,128]{2,1,0:T(8,128)(2,1)} %get-tuple-element.46), calls=%async_computation.2 | async-start | bytes 3276800 | tf_op jit(solution)/shard_map/all_to_all | solution.py:716
  150.3 15.2 %own.1 = (f32[512,1024]{1,0:T(8,128)}, f32[512,1024]{1,0:T(8,128)}, f32[32,128]{1,0:T(8,128)}, f32[32,128]{1,0:T(8,128)}, bf16[16,272,128]{2,1,0:T(8,128)(2,1)}) custom-call(s32[2]{0:T(128)} %pad_add_fusion.meta.refs_0_, bf16[256,4096]{1,0:T(8,128)(2,1)} %q0.1, bf16[256,1024]{1,0:T(8,128)(2,1)} %copy-done.3, ...), custom_call_target="tpu_custom_call", output_to_operand_aliasing={{4}: (6, {})} | custom-call | flops 2684354560 | bytes 8388608 | tf_op jit(solution)/shard_map/own/pallas_call | solution.py:581
  165.4 24.1 %all-to-all-done.2.back.refs_2_ = bf16[16,400,128]{2,1,0:T(8,128)(2,1)S(1)} async-done(((bf16[16,400,128]{2,1,0:T(8,128)(2,1)}), bf16[16,400,128]{2,1,0:T(8,128)(2,1)S(1)}, u32[]{:S(2)}, u32[]{:S(2)}) %all-to-all-start.2) | async-done | bytes 1638432 | tf_op jit(solution)/shard_map/all_to_all | solution.py:716
  189.5 4.8 %all-to-all-start.3 = ((bf16[16,272,128]{2,1,0:T(8,128)(2,1)}), bf16[16,272,128]{2,1,0:T(8,128)(2,1)S(1)}, u32[]{:S(2)}, u32[]{:S(2)}) async-start(bf16[16,272,128]{2,1,0:T(8,128)(2,1)} %get-tuple-element.48), calls=%async_computation.3 | async-start | bytes 2228224 | tf_op jit(solution)/shard_map/all_to_all | solution.py:716
  198.3 24.1 %all-to-all-done.3.refs_3_ = bf16[16,272,128]{2,1,0:T(8,128)(2,1)S(1)} async-done(((bf16[16,272,128]{2,1,0:T(8,128)(2,1)}), bf16[16,272,128]{2,1,0:T(8,128)(2,1)S(1)}, u32[]{:S(2)}, u32[]{:S(2)}) %all-to-all-start.3) | async-done | bytes 1114144 | tf_op jit(solution)/shard_map/all_to_all | solution.py:716
  222.4 3.7 %collective-permute-done.10.refs_4_ = bf16[16,272,128]{2,1,0:T(8,128)(2,1)} collective-permute-done((bf16[16,272,128]{2,1,0:T(8,128)(2,1)}, bf16[16,272,128]{2,1,0:T(8,128)(2,1)}, u32[]{:S(2)}, u32[]{:S(2)}) %collective-permute-start.10) | collective-permute-done | bytes 1114144 | tf_op jit(solution)/shard_map/ppermute | solution.py:741
  227.7 5.6 %merge.2 = (bf16[128,1024]{1,0:T(8,128)(2,1)S(1)}, bf16[128,1024]{1,0:T(8,128)(2,1)S(1)}, bf16[128,1024]{1,0:T(8,128)(2,1)S(1)}, bf16[128,1024]{1,0:T(8,128)(2,1)S(1)}) custom-call(s32[2]{0:T(128)S(1)} %copy-done.14, s32[192]{0:T(256)S(1)} %get-tuple-element.34.refs_1_, bf16[16,400,128]{2,1,0:T(8,128)(2,1)S(1)} %all-to-all-done.2.back.refs_2_, ...), custom_call_target="tpu_custom_call" | custom-call | flops 10485760 | bytes 8388608 | tf_op jit(solution)/shard_map/merge/pallas_call | solution.py:664
  233.3 3.3 %collective-permute-start.12 = (bf16[128,1024]{1,0:T(8,128)(2,1)S(1)}, bf16[128,1024]{1,0:T(8,128)(2,1)S(1)}, u32[]{:S(2)}, u32[]{:S(2)}) collective-permute-start(bf16[128,1024]{1,0:T(8,128)(2,1)S(1)} %get-tuple-element.54), channel_id=1, source_target_pairs={{0,1},{1,2},{2,3},{3,0},{4,5},{5,6},{6,7},{7,4},{8,9},{9,10},{10,1... | collective-permute-start | bytes 786440 | tf_op jit(solution)/shard_map/ppermute | solution.py:157
  239.4 5.6 %merge.3 = (bf16[128,1024]{1,0:T(8,128)(2,1)S(1)}, bf16[128,1024]{1,0:T(8,128)(2,1)S(1)}, bf16[128,1024]{1,0:T(8,128)(2,1)S(1)}, bf16[128,1024]{1,0:T(8,128)(2,1)S(1)}) custom-call(s32[2]{0:T(128)S(1)} %copy-done.14, s32[192]{0:T(256)S(1)} %get-tuple-element.34.refs_1_, bf16[16,400,128]{2,1,0:T(8,128)(2,1)S(1)} %all-to-all-done.2.back.refs_2_, ...), custom_call_target="tpu_custom_call" | custom-call | flops 10485760 | bytes 8388608 | tf_op jit(solution)/shard_map/merge/pallas_call | solution.py:664
  248.6 2.3 collective-permute-done.13.refs_2_
  250.9 5.6 %collective-permute-done.15.refs_5_ = bf16[128,1024]{1,0:T(8,128)(2,1)S(1)} collective-permute-done((bf16[128,1024]{1,0:T(8,128)(2,1)S(1)}, bf16[128,1024]{1,0:T(8,128)(2,1)S(1)}, u32[]{:S(2)}, u32[]{:S(2)}) %collective-permute-start.15) | collective-permute-done | bytes 262176 | tf_op jit(solution)/shard_map/ppermute | solution.py:157
  256.5 4.2 %collective-permute-done.16.refs_6_ = bf16[128,1024]{1,0:T(8,128)(2,1)S(1)} collective-permute-done((bf16[128,1024]{1,0:T(8,128)(2,1)S(1)}, bf16[128,1024]{1,0:T(8,128)(2,1)S(1)}, u32[]{:S(2)}, u32[]{:S(2)}) %collective-permute-start.16) | collective-permute-done | bytes 262176 | tf_op jit(solution)/shard_map/ppermute | solution.py:157
  260.7 2.1 finish.1
  (73 shorter events, 32.1 us)
Async XLA Ops:
  0.0 9.5 %copy-start.19 = (s32[8,8,3]{1,0,2:T(8,128)S(1)}, s32[8,8,3]{1,0,2:T(8,128)}, u32[]{:S(2)}) copy-start(s32[8,8,3]{1,0,2:T(8,128)} %param.7) | copy-start | bytes 2308
  0.6 9.2 %copy-start.12 = (s32[2]{0:T(128)S(1)}, s32[2]{0:T(128)}, u32[]{:S(2)}) copy-start(s32[2]{0:T(128)} %pad_add_fusion.meta.refs_0_) | copy-start | bytes 28
  3.6 15.2 %collective-permute-start = (bf16[256,1024]{1,0:T(8,128)(2,1)}, bf16[256,1024]{1,0:T(8,128)(2,1)S(1)}, u32[]{:S(2)}, u32[]{:S(2)}) collective-permute-start(bf16[256,1024]{1,0:T(8,128)(2,1)} %get-tuple-element.36), channel_id=1, source_target_pairs={{0,1},{1,2},{2,3},{3,0},{4,5},{5,6},{6,7},{7,4},{8,9},{9,10},{10,1... | collective-permute-start | bytes 1572872 | tf_op jit(solution)/shard_map/ppermute | solution.py:157
  5.3 26.0 %collective-permute-start.1 = (bf16[256,1024]{1,0:T(8,128)(2,1)}, bf16[256,1024]{1,0:T(8,128)(2,1)S(1)}, u32[]{:S(2)}, u32[]{:S(2)}) collective-permute-start(bf16[256,1024]{1,0:T(8,128)(2,1)} %get-tuple-element.37), channel_id=1, source_target_pairs={{0,2},{1,3},{2,0},{3,1},{4,6},{5,7},{6,4},{7,5},{8,10},{9,11},{10,... | collective-permute-start | bytes 1572872 | tf_op jit(solution)/shard_map/ppermute | solution.py:157
  8.2 23.1 %collective-permute-start.2 = (bf16[256,1024]{1,0:T(8,128)(2,1)}, bf16[256,1024]{1,0:T(8,128)(2,1)S(1)}, u32[]{:S(2)}, u32[]{:S(2)}) collective-permute-start(bf16[256,1024]{1,0:T(8,128)(2,1)} %get-tuple-element.38), channel_id=1, source_target_pairs={{0,3},{1,0},{2,1},{3,2},{4,7},{5,4},{6,5},{7,6},{8,11},{9,8},{10,9... | collective-permute-start | bytes 1572872 | tf_op jit(solution)/shard_map/ppermute | solution.py:157
  18.8 12.4 %copy-start.3 = (bf16[256,1024]{1,0:T(8,128)(2,1)}, bf16[256,1024]{1,0:T(8,128)(2,1)S(1)}, u32[]{:S(2)}) copy-start(bf16[256,1024]{1,0:T(8,128)(2,1)S(1)} %collective-permute-done.refs_3_.q1) | copy-start | bytes 1572868
  36.6 14.1 %copy-start = (bf16[256,4096]{1,0:T(8,128)(2,1)S(1)}, bf16[256,4096]{1,0:T(8,128)(2,1)}, u32[]{:S(2)}) copy-start(bf16[256,4096]{1,0:T(8,128)(2,1)} %q0.1) | copy-start | bytes 6291460
  36.6 14.1 %copy-start.13 = (s32[2]{0:T(128)S(1)}, s32[2]{0:T(128)}, u32[]{:S(2)}) copy-start(s32[2]{0:T(128)} %pad_add_fusion.meta.refs_0_) | copy-start | bytes 28
  36.6 14.1 %copy-start.18 = (s32[128]{0:T(128)S(1)}, s32[128]{0:T(128)}, u32[]{:S(2)}) copy-start(s32[128]{0:T(128)} %copy-done.17) | copy-start | bytes 1540
  36.6 37.8 %all-to-all-start.1 = ((bf16[16,272,128]{2,1,0:T(8,128)(2,1)}), bf16[16,272,128]{2,1,0:T(8,128)(2,1)}, u32[]{:S(2)}, u32[]{:S(2)}) async-start(bf16[16,272,128]{2,1,0:T(8,128)(2,1)} %get-tuple-element.45), calls=%async_computation.1 | async-start | bytes 2228224 | tf_op jit(solution)/shard_map/all_to_all | solution.py:716
  45.4 27.0 %collective-permute-start.3 = (bf16[16,272,128]{2,1,0:T(8,128)(2,1)}, bf16[16,272,128]{2,1,0:T(8,128)(2,1)S(1)}, u32[]{:S(2)}, u32[]{:S(2)}) collective-permute-start(bf16[16,272,128]{2,1,0:T(8,128)(2,1)} %get-tuple-element.39), channel_id=1, source_target_pairs={{192,0},{196,4},{200,8},{204,12},{208,16},{212,20},{216,24},{220,2... | collective-permute-start | bytes 3342344 | tf_op jit(solution)/shard_map/ppermute | solution.py:728
  47.8 15.9 %collective-permute-start.4 = (bf16[16,144,128]{2,1,0:T(8,128)(2,1)}, bf16[16,144,128]{2,1,0:T(8,128)(2,1)S(1)}, u32[]{:S(2)}, u32[]{:S(2)}) collective-permute-start(bf16[16,144,128]{2,1,0:T(8,128)(2,1)} %get-tuple-element.40), channel_id=1, source_target_pairs={{64,0},{68,4},{72,8},{76,12},{80,16},{84,20},{88,24},{92,28},{96,3... | collective-permute-start | bytes 1769480 | tf_op jit(solution)/shard_map/ppermute | solution.py:729
  74.4 54.1 %all-to-all-start = ((bf16[16,400,128]{2,1,0:T(8,128)(2,1)}), bf16[16,400,128]{2,1,0:T(8,128)(2,1)}, u32[]{:S(2)}, u32[]{:S(2)}) async-start(bf16[16,400,128]{2,1,0:T(8,128)(2,1)} %insert.1), calls=%async_computation | async-start | bytes 3276800 | tf_op jit(solution)/shard_map/all_to_all | solution.py:716
  82.5 10.2 %collective-permute-start.5 = (bf16[256,512]{1,0:T(8,128)(2,1)S(1)}, bf16[256,512]{1,0:T(8,128)(2,1)S(1)}, u32[]{:S(2)}, u32[]{:S(2)}) collective-permute-start(bf16[256,512]{1,0:T(8,128)(2,1)S(1)} %get-tuple-element.42), channel_id=1, source_target_pairs={{0,1},{1,2},{2,3},{3,0},{4,5},{5,6},{6,7},{7,4},{8,9},{9,10},{10,1... | collective-permute-start | bytes 786440 | tf_op jit(solution)/shard_map/ppermute | solution.py:157
  83.6 14.5 %collective-permute-start.6 = (bf16[256,512]{1,0:T(8,128)(2,1)S(1)}, bf16[256,512]{1,0:T(8,128)(2,1)S(1)}, u32[]{:S(2)}, u32[]{:S(2)}) collective-permute-start(bf16[256,512]{1,0:T(8,128)(2,1)S(1)} %get-tuple-element.43), channel_id=1, source_target_pairs={{0,2},{1,3},{2,0},{3,1},{4,6},{5,7},{6,4},{7,5},{8,10},{9,11},{10,... | collective-permute-start | bytes 786440 | tf_op jit(solution)/shard_map/ppermute | solution.py:157
  86.0 12.6 %collective-permute-start.7 = (bf16[256,512]{1,0:T(8,128)(2,1)S(1)}, bf16[256,512]{1,0:T(8,128)(2,1)S(1)}, u32[]{:S(2)}, u32[]{:S(2)}) collective-permute-start(bf16[256,512]{1,0:T(8,128)(2,1)S(1)} %get-tuple-element.44), channel_id=1, source_target_pairs={{0,3},{1,0},{2,1},{3,2},{4,7},{5,4},{6,5},{7,6},{8,11},{9,8},{10,9... | collective-permute-start | bytes 786440 | tf_op jit(solution)/shard_map/ppermute | solution.py:157
  99.3 26.3 %collective-permute-start.8 = (bf16[1024,512]{1,0:T(8,128)(2,1)S(1)}, bf16[1024,512]{1,0:T(8,128)(2,1)S(1)}, u32[]{:S(2)}, u32[]{:S(2)}) collective-permute-start(bf16[1024,512]{1,0:T(8,128)(2,1)S(1)} %join.1.refs_2_.kv), channel_id=1, source_target_pairs={{0,64},{4,68},{8,72},{12,76},{16,80},{20,84},{24,88},{28,92},{32,9... | collective-permute-start | bytes 3145736 | tf_op jit(solution)/shard_map/ppermute | solution.py:732
  100.6 27.9 %collective-permute-start.9 = (bf16[1024,512]{1,0:T(8,128)(2,1)S(1)}, bf16[1024,512]{1,0:T(8,128)(2,1)S(1)}, u32[]{:S(2)}, u32[]{:S(2)}) collective-permute-start(bf16[1024,512]{1,0:T(8,128)(2,1)S(1)} %join.1.refs_2_.kv), channel_id=1, source_target_pairs={{64,192},{68,196},{72,200},{76,204},{80,208},{84,212},{88,216},{92... | collective-permute-start | bytes 3145736 | tf_op jit(solution)/shard_map/ppermute | solution.py:733
  142.2 47.3 %all-to-all-start.2 = ((bf16[16,400,128]{2,1,0:T(8,128)(2,1)}), bf16[16,400,128]{2,1,0:T(8,128)(2,1)S(1)}, u32[]{:S(2)}, u32[]{:S(2)}) async-start(bf16[16,400,128]{2,1,0:T(8,128)(2,1)} %get-tuple-element.46), calls=%async_computation.2 | async-start | bytes 3276800 | tf_op jit(solution)/shard_map/all_to_all | solution.py:716
  189.5 32.9 %all-to-all-start.3 = ((bf16[16,272,128]{2,1,0:T(8,128)(2,1)}), bf16[16,272,128]{2,1,0:T(8,128)(2,1)S(1)}, u32[]{:S(2)}, u32[]{:S(2)}) async-start(bf16[16,272,128]{2,1,0:T(8,128)(2,1)} %get-tuple-element.48), calls=%async_computation.3 | async-start | bytes 2228224 | tf_op jit(solution)/shard_map/all_to_all | solution.py:716
  194.3 31.7 %copy-start.14 = (s32[2]{0:T(128)S(1)}, s32[2]{0:T(128)}, u32[]{:S(2)}) copy-start(s32[2]{0:T(128)} %pad_add_fusion.meta.refs_0_) | copy-start | bytes 28
  194.4 31.7 %copy-start.16 = (f32[32,128]{1,0:T(8,128)S(1)}, f32[32,128]{1,0:T(8,128)}, u32[]{:S(2)}) copy-start(f32[32,128]{1,0:T(8,128)} %get-tuple-element.52.refs_7_) | copy-start | bytes 49156
  195.7 30.3 %collective-permute-start.10 = (bf16[16,272,128]{2,1,0:T(8,128)(2,1)}, bf16[16,272,128]{2,1,0:T(8,128)(2,1)}, u32[]{:S(2)}, u32[]{:S(2)}) collective-permute-start(bf16[16,272,128]{2,1,0:T(8,128)(2,1)} %get-tuple-element.49), channel_id=1, source_target_pairs={{0,192},{4,196},{8,200},{12,204},{16,208},{20,212},{24,216},{28,22... | collective-permute-start | bytes 3342344 | tf_op jit(solution)/shard_map/ppermute | solution.py:741
  197.0 25.4 %collective-permute-start.11 = (bf16[16,144,128]{2,1,0:T(8,128)(2,1)}, bf16[16,144,128]{2,1,0:T(8,128)(2,1)S(1)}, u32[]{:S(2)}, u32[]{:S(2)}) collective-permute-start(bf16[16,144,128]{2,1,0:T(8,128)(2,1)} %get-tuple-element.50), channel_id=1, source_target_pairs={{0,64},{4,68},{8,72},{12,76},{16,80},{20,84},{24,88},{28,92},{32,9... | collective-permute-start | bytes 1769480 | tf_op jit(solution)/shard_map/ppermute | solution.py:742
  227.7 11.7 %copy-start.1 = (f32[512,1024]{1,0:T(8,128)S(1)}, f32[512,1024]{1,0:T(8,128)}, u32[]{:S(2)}) copy-start(f32[512,1024]{1,0:T(8,128)} %get-tuple-element.57.refs_6_) | copy-start | bytes 6291460
  227.7 11.7 %copy-start.15 = (f32[32,128]{1,0:T(8,128)S(1)}, f32[32,128]{1,0:T(8,128)}, u32[]{:S(2)}) copy-start(f32[32,128]{1,0:T(8,128)} %get-tuple-element.58.refs_7_) | copy-start | bytes 49156
  233.3 14.6 %collective-permute-start.12 = (bf16[128,1024]{1,0:T(8,128)(2,1)S(1)}, bf16[128,1024]{1,0:T(8,128)(2,1)S(1)}, u32[]{:S(2)}, u32[]{:S(2)}) collective-permute-start(bf16[128,1024]{1,0:T(8,128)(2,1)S(1)} %get-tuple-element.54), channel_id=1, source_target_pairs={{0,1},{1,2},{2,3},{3,0},{4,5},{5,6},{6,7},{7,4},{8,9},{9,10},{10,1... | collective-permute-start | bytes 786440 | tf_op jit(solution)/shard_map/ppermute | solution.py:157
  236.6 14.3 %collective-permute-start.13 = (bf16[128,1024]{1,0:T(8,128)(2,1)S(1)}, bf16[128,1024]{1,0:T(8,128)(2,1)S(1)}, u32[]{:S(2)}, u32[]{:S(2)}) collective-permute-start(bf16[128,1024]{1,0:T(8,128)(2,1)S(1)} %get-tuple-element.55), channel_id=1, source_target_pairs={{0,2},{1,3},{2,0},{3,1},{4,6},{5,7},{6,4},{7,5},{8,10},{9,11},{10,... | collective-permute-start | bytes 786440 | tf_op jit(solution)/shard_map/ppermute | solution.py:157
  238.1 12.8 %collective-permute-start.14 = (bf16[128,1024]{1,0:T(8,128)(2,1)S(1)}, bf16[128,1024]{1,0:T(8,128)(2,1)S(1)}, u32[]{:S(2)}, u32[]{:S(2)}) collective-permute-start(bf16[128,1024]{1,0:T(8,128)(2,1)S(1)} %get-tuple-element.56), channel_id=1, source_target_pairs={{0,3},{1,0},{2,1},{3,2},{4,7},{5,4},{6,5},{7,6},{8,11},{9,8},{10,9... | collective-permute-start | bytes 786440 | tf_op jit(solution)/shard_map/ppermute | solution.py:157
  245.0 11.5 %collective-permute-start.15 = (bf16[128,1024]{1,0:T(8,128)(2,1)S(1)}, bf16[128,1024]{1,0:T(8,128)(2,1)S(1)}, u32[]{:S(2)}, u32[]{:S(2)}) collective-permute-start(bf16[128,1024]{1,0:T(8,128)(2,1)S(1)} %get-tuple-element.60), channel_id=1, source_target_pairs={{0,1},{1,2},{2,3},{3,0},{4,5},{5,6},{6,7},{7,4},{8,9},{9,10},{10,1... | collective-permute-start | bytes 786440 | tf_op jit(solution)/shard_map/ppermute | solution.py:157
  245.8 14.9 %collective-permute-start.16 = (bf16[128,1024]{1,0:T(8,128)(2,1)S(1)}, bf16[128,1024]{1,0:T(8,128)(2,1)S(1)}, u32[]{:S(2)}, u32[]{:S(2)}) collective-permute-start(bf16[128,1024]{1,0:T(8,128)(2,1)S(1)} %get-tuple-element.61), channel_id=1, source_target_pairs={{0,2},{1,3},{2,0},{3,1},{4,6},{5,7},{6,4},{7,5},{8,10},{9,11},{10,... | collective-permute-start | bytes 786440 | tf_op jit(solution)/shard_map/ppermute | solution.py:157
  247.9 12.9 %collective-permute-start.17 = (bf16[128,1024]{1,0:T(8,128)(2,1)S(1)}, bf16[128,1024]{1,0:T(8,128)(2,1)S(1)}, u32[]{:S(2)}, u32[]{:S(2)}) collective-permute-start(bf16[128,1024]{1,0:T(8,128)(2,1)S(1)} %get-tuple-element.62), channel_id=1, source_target_pairs={{0,3},{1,0},{2,1},{3,2},{4,7},{5,4},{6,5},{7,6},{8,11},{9,8},{10,9... | collective-permute-start | bytes 786440 | tf_op jit(solution)/shard_map/ppermute | solution.py:157
  (12 other events, 27.9 us)

commit v4 on v3

--- a/solution.py
+++ b/solution.py
@@ -14,7 +14,6 @@
 ROW = 16
 R = TILE
 SLOTS = 5
-GROUP = 4
 EXTRA = 16
 SEND = (2 * R + EXTRA, 3 * R + EXTRA)
 LOG_AT = 2 * R
@@ -479,16 +478,24 @@
                 logs[j, pl.ds(s, 1), :] = high
                 logs[j, pl.ds(8 + s, 1), :] = log - high
 
-        def whole(n, _, batch=batch):
-            batch(n * GROUP, GROUP)
+        eights = lax.shift_right_logical(count, 3)
+        rest = count - 8 * eights
+        fours = lax.shift_right_logical(rest + 1, 2)
+
+        def eight(n, _, batch=batch):
+            batch(8 * n, 8)
             return 0
 
-        fours = lax.shift_right_logical(count + 1, 2)
-        lax.fori_loop(0, fours, whole, 0)
-
-        @pl.when(count > GROUP * fours)
-        def _(batch=batch, fours=fours):
-            batch(GROUP * fours, 2)
+        def four(n, _, batch=batch, eights=eights):
+            batch(8 * eights + 4 * n, 4)
+            return 0
+
+        lax.fori_loop(0, eights, eight, 0)
+        lax.fori_loop(0, fours, four, 0)
+
+        @pl.when(rest > 4 * fours)
+        def _(batch=batch, eights=eights, fours=fours):
+            batch(8 * eights + 4 * fours, 2)
 
         if i == 1:
             save(0, 2 * R)
@@ -646,7 +653,7 @@
             done[rows, cols] = mixed.astype(BF16)
         return 0
 
-    lax.fori_loop(0, N_HEAD, each, 0)
+    lax.fori_loop(0, N_HEAD, each, 0, unroll=N_HEAD)
     pairs = []
     for step, ref in enumerate((o0, o1, o2, o3)):
         target = lax.rem(y + step, N_HEAD)

time: 264 us -> 276 us (1.045); the launches traced: 263 us -> 271 us
  Pallas kernels: 68 us -> 78.2 us
    pallas_call x2, Pallas kernels: 21 us -> 32.4 us  [gate(): pl.pallas_call(kernel, out_shape=[shaped((ROW, SEND[part], HEAD_DIM))] +...]
where the time goes in v4:
time: 276 us; the launch traced here: 271 us
  waiting for transfers between devices  126 us (46%)
  Pallas kernels  78.2 us (28%)
  starting transfers between devices  58.2 us (21%)
  local copies, waits for them, and re-layouts  7.52 us (3%)
    all_to_all x4, waiting for transfers between devices, over_row(): lax.all_to_all(x, 'ctx', split_axis=0, concat_axis=0, tiled=True, axis_in...  47.9 us
    ppermute x12, waiting for transfers between devices, over_head(): got.append(lax.ppermute(parts[step], 'head', pairs))  39.9 us
    pallas_call x2, Pallas kernels, gate(): pl.pallas_call(kernel, out_shape=[shaped((ROW, SEND[part], HEAD_DIM))] +...  32.4 us
    all_to_all x4, starting transfers between devices, over_row(): lax.all_to_all(x, 'ctx', split_axis=0, concat_axis=0, tiled=True, axis_in...  27.1 us
    ppermute x12, starting transfers between devices, over_head(): got.append(lax.ppermute(parts[step], 'head', pairs))  20.4 us
    pallas_call x1, Pallas kernels, own(): pl.pallas_call(own_kernel, out_shape=(out, out, logs, logs, shaped(held.s...  15.2 us
    ppermute x1, waiting for transfers between devices, local(): kv_one = lax.ppermute(kv, 'ctx', rows_to([(0, 1), (1, 2), (2, 3)]))  14.2 us
    pallas_call x2, Pallas kernels, merge(): pl.pallas_call(kernel, out_shape=[shaped((R, wide))] * N_HEAD, in_specs=[...  10 us
  transfers between devices with their start and end apart: 22, of which 15 were waited for; matrix products, arithmetic and copies ran while one was open for 0% of the time, Pallas kernels for 15%

profile of v4, /device:TPU:6, one launch (start us, length us, event | category | flops | bytes accessed | tf_op | source)
XLA Modules:
  0.0 270.8 jit_solution(8531011581220559346)
XLA Ops:
  0.6 3.0 %split.2 = (bf16[256,1024]{1,0:T(8,128)(2,1)}, bf16[256,1024]{1,0:T(8,128)(2,1)}, bf16[256,1024]{1,0:T(8,128)(2,1)}) custom-call(s32[2]{0:T(128)} %pad_add_fusion.meta.refs_0_, bf16[256,4096]{1,0:T(8,128)(2,1)} %q0.1), custom_call_target="tpu_custom_call" | custom-call | bytes 3145728 | tf_op jit(solution)/shard_map/split/pallas_call | solution.py:136
  5.3 2.9 %collective-permute-start.1 = (bf16[256,1024]{1,0:T(8,128)(2,1)}, bf16[256,1024]{1,0:T(8,128)(2,1)S(1)}, u32[]{:S(2)}, u32[]{:S(2)}) collective-permute-start(bf16[256,1024]{1,0:T(8,128)(2,1)} %get-tuple-element.37), channel_id=1, source_target_pairs={{0,2},{1,3},{2,0},{3,1},{4,6},{5,7},{6,4},{7,5},{8,10},{9,11},{10,... | collective-permute-start | bytes 1572872 | tf_op jit(solution)/shard_map/ppermute | solution.py:156
  9.8 4.7 %plan.1 = (s32[128]{0:T(128)S(1)}, s32[192]{0:T(256)S(1)}) custom-call(s32[2]{0:T(128)S(1)} %copy-done.12, s32[192]{0:T(256)S(1)} %reshape.3.gates), custom_call_target="tpu_custom_call" | custom-call | tf_op jit(solution)/shard_map/plan/pallas_call | solution.py:96
  15.0 3.8 %collective-permute-done.refs_3_.q1 = bf16[256,1024]{1,0:T(8,128)(2,1)S(1)} collective-permute-done((bf16[256,1024]{1,0:T(8,128)(2,1)}, bf16[256,1024]{1,0:T(8,128)(2,1)S(1)}, u32[]{:S(2)}, u32[]{:S(2)}) %collective-permute-start) | collective-permute-done | bytes 524320 | tf_op jit(solution)/shard_map/ppermute | solution.py:156
  18.8 12.4 %collective-permute-done.1.refs_4_.q2 = bf16[256,1024]{1,0:T(8,128)(2,1)S(1)} collective-permute-done((bf16[256,1024]{1,0:T(8,128)(2,1)}, bf16[256,1024]{1,0:T(8,128)(2,1)S(1)}, u32[]{:S(2)}, u32[]{:S(2)}) %collective-permute-start.1) | collective-permute-done | bytes 524320 | tf_op jit(solution)/shard_map/ppermute | solution.py:156
  32.2 4.3 %pack.3 = (bf16[16,272,128]{2,1,0:T(8,128)(2,1)}, bf16[16,144,128]{2,1,0:T(8,128)(2,1)}, bf16[16,272,128]{2,1,0:T(8,128)(2,1)}) custom-call(s32[2]{0:T(128)} %pad_add_fusion.meta.refs_0_, s32[128]{0:T(128)} %copy-done.17, bf16[256,4096]{1,0:T(8,128)(2,1)} %q0.1, bf16[256,1024]{1,0:T(8,128)(2,1)} %copy-done.3, bf16[256,1024]{1,0:T(8,128)(2,1)} %copy-done.5, ...), custom_call_target="tpu_custom_call" | custom-call | bytes 4915200 | tf_op jit(solution)/shard_map/pack/pallas_call | solution.py:266
  36.6 8.8 %all-to-all-start.1 = ((bf16[16,272,128]{2,1,0:T(8,128)(2,1)}), bf16[16,272,128]{2,1,0:T(8,128)(2,1)}, u32[]{:S(2)}, u32[]{:S(2)}) async-start(bf16[16,272,128]{2,1,0:T(8,128)(2,1)} %get-tuple-element.45), calls=%async_computation.1 | async-start | bytes 2228224 | tf_op jit(solution)/shard_map/all_to_all | solution.py:723
  45.4 2.5 collective-permute-start.3
  47.8 2.8 %collective-permute-start.4 = (bf16[16,144,128]{2,1,0:T(8,128)(2,1)}, bf16[16,144,128]{2,1,0:T(8,128)(2,1)S(1)}, u32[]{:S(2)}, u32[]{:S(2)}) collective-permute-start(bf16[16,144,128]{2,1,0:T(8,128)(2,1)} %get-tuple-element.40), channel_id=1, source_target_pairs={{64,0},{68,4},{72,8},{76,12},{80,16},{84,20},{88,24},{92,28},{96,3... | collective-permute-start | bytes 1769480 | tf_op jit(solution)/shard_map/ppermute | solution.py:736
  55.3 8.4 %collective-permute-done.4.near.refs_3_ = bf16[16,144,128]{2,1,0:T(8,128)(2,1)S(1)} collective-permute-done((bf16[16,144,128]{2,1,0:T(8,128)(2,1)}, bf16[16,144,128]{2,1,0:T(8,128)(2,1)S(1)}, u32[]{:S(2)}, u32[]{:S(2)}) %collective-permute-start.4) | collective-permute-done | bytes 589856 | tf_op jit(solution)/shard_map/ppermute | solution.py:736
  63.7 8.6 %collective-permute-done.3.far = bf16[16,272,128]{2,1,0:T(8,128)(2,1)S(1)} collective-permute-done((bf16[16,272,128]{2,1,0:T(8,128)(2,1)}, bf16[16,272,128]{2,1,0:T(8,128)(2,1)S(1)}, u32[]{:S(2)}, u32[]{:S(2)}) %collective-permute-start.3) | collective-permute-done | bytes 1114144 | tf_op jit(solution)/shard_map/ppermute | solution.py:735
  74.4 7.1 %all-to-all-start = ((bf16[16,400,128]{2,1,0:T(8,128)(2,1)}), bf16[16,400,128]{2,1,0:T(8,128)(2,1)}, u32[]{:S(2)}, u32[]{:S(2)}) async-start(bf16[16,400,128]{2,1,0:T(8,128)(2,1)} %insert.1), calls=%async_computation | async-start | bytes 3276800 | tf_op jit(solution)/shard_map/all_to_all | solution.py:723
  83.7 2.3 collective-permute-start.6
  87.6 5.1 %collective-permute-done.5.refs_1_ = bf16[256,512]{1,0:T(8,128)(2,1)S(1)} collective-permute-done((bf16[256,512]{1,0:T(8,128)(2,1)S(1)}, bf16[256,512]{1,0:T(8,128)(2,1)S(1)}, u32[]{:S(2)}, u32[]{:S(2)}) %collective-permute-start.5) | collective-permute-done | bytes 262176 | tf_op jit(solution)/shard_map/ppermute | solution.py:156
  92.7 5.5 %collective-permute-done.6.refs_2_ = bf16[256,512]{1,0:T(8,128)(2,1)S(1)} collective-permute-done((bf16[256,512]{1,0:T(8,128)(2,1)S(1)}, bf16[256,512]{1,0:T(8,128)(2,1)S(1)}, u32[]{:S(2)}, u32[]{:S(2)}) %collective-permute-start.6) | collective-permute-done | bytes 262176 | tf_op jit(solution)/shard_map/ppermute | solution.py:156
  101.9 9.4 %gate.2.refs_5_ = bf16[16,272,128]{2,1,0:T(8,128)(2,1)} custom-call(s32[2]{0:T(128)} %pad_add_fusion.meta.refs_0_, bf16[16,272,128]{2,1,0:T(8,128)(2,1)} %all-to-all-done.1.refs_1_, bf16[1024,512]{1,0:T(8,128)(2,1)} %copy-done.9), custom_call_target="tpu_custom_call" | custom-call | flops 2147483648 | bytes 8388608 | tf_op jit(solution)/shard_map/gate/pallas_call | solution.py:518
  111.3 14.2 %collective-permute-done.8.refs_3_ = bf16[1024,512]{1,0:T(8,128)(2,1)S(1)} collective-permute-done((bf16[1024,512]{1,0:T(8,128)(2,1)S(1)}, bf16[1024,512]{1,0:T(8,128)(2,1)S(1)}, u32[]{:S(2)}, u32[]{:S(2)}) %collective-permute-start.8) | collective-permute-done | bytes 1048608 | tf_op jit(solution)/shard_map/ppermute | solution.py:739
  125.5 2.9 %collective-permute-done.9.refs_4_ = bf16[1024,512]{1,0:T(8,128)(2,1)S(1)} collective-permute-done((bf16[1024,512]{1,0:T(8,128)(2,1)S(1)}, bf16[1024,512]{1,0:T(8,128)(2,1)S(1)}, u32[]{:S(2)}, u32[]{:S(2)}) %collective-permute-start.9) | collective-permute-done | bytes 1048608 | tf_op jit(solution)/shard_map/ppermute | solution.py:740
  129.5 23.0 %gate.3 = (bf16[16,400,128]{2,1,0:T(8,128)(2,1)}, bf16[16,272,128]{2,1,0:T(8,128)(2,1)}) custom-call(s32[2]{0:T(128)} %pad_add_fusion.meta.refs_0_, bf16[16,400,128]{2,1,0:T(8,128)(2,1)} %all-to-all-done.refs_1_, bf16[1024,512]{1,0:T(8,128)(2,1)} %copy-done.9, bf16[1024,512]{1,0:T(8,128)(2,1)} %copy-done.20, ...), custom_call_target="tpu_custom_call", output_to_operand_aliasing={{1}: (5, {})} | custom-call | flops 3221225472 | bytes 8388608 | tf_op jit(solution)/shard_map/gate/pallas_call | solution.py:518
  152.5 6.4 %all-to-all-start.2 = ((bf16[16,400,128]{2,1,0:T(8,128)(2,1)}), bf16[16,400,128]{2,1,0:T(8,128)(2,1)S(1)}, u32[]{:S(2)}, u32[]{:S(2)}) async-start(bf16[16,400,128]{2,1,0:T(8,128)(2,1)} %get-tuple-element.46), calls=%async_computation.2 | async-start | bytes 3276800 | tf_op jit(solution)/shard_map/all_to_all | solution.py:723
  158.8 15.2 %own.1 = (f32[512,1024]{1,0:T(8,128)}, f32[512,1024]{1,0:T(8,128)}, f32[32,128]{1,0:T(8,128)}, f32[32,128]{1,0:T(8,128)}, bf16[16,272,128]{2,1,0:T(8,128)(2,1)}) custom-call(s32[2]{0:T(128)} %pad_add_fusion.meta.refs_0_, bf16[256,4096]{1,0:T(8,128)(2,1)} %q0.1, bf16[256,1024]{1,0:T(8,128)(2,1)} %copy-done.3, ...), custom_call_target="tpu_custom_call", output_to_operand_aliasing={{4}: (6, {})} | custom-call | flops 2684354560 | bytes 8388608 | tf_op jit(solution)/shard_map/own/pallas_call | solution.py:588
  174.0 24.1 %all-to-all-done.2.back.refs_2_ = bf16[16,400,128]{2,1,0:T(8,128)(2,1)S(1)} async-done(((bf16[16,400,128]{2,1,0:T(8,128)(2,1)}), bf16[16,400,128]{2,1,0:T(8,128)(2,1)S(1)}, u32[]{:S(2)}, u32[]{:S(2)}) %all-to-all-start.2) | async-done | bytes 1638432 | tf_op jit(solution)/shard_map/all_to_all | solution.py:723
  198.1 4.8 %all-to-all-start.3 = ((bf16[16,272,128]{2,1,0:T(8,128)(2,1)}), bf16[16,272,128]{2,1,0:T(8,128)(2,1)S(1)}, u32[]{:S(2)}, u32[]{:S(2)}) async-start(bf16[16,272,128]{2,1,0:T(8,128)(2,1)} %get-tuple-element.48), calls=%async_computation.3 | async-start | bytes 2228224 | tf_op jit(solution)/shard_map/all_to_all | solution.py:723
  207.1 23.8 %all-to-all-done.3.refs_3_ = bf16[16,272,128]{2,1,0:T(8,128)(2,1)S(1)} async-done(((bf16[16,272,128]{2,1,0:T(8,128)(2,1)}), bf16[16,272,128]{2,1,0:T(8,128)(2,1)S(1)}, u32[]{:S(2)}, u32[]{:S(2)}) %all-to-all-start.3) | async-done | bytes 1114144 | tf_op jit(solution)/shard_map/all_to_all | solution.py:723
  231.0 3.7 %collective-permute-done.10.refs_4_ = bf16[16,272,128]{2,1,0:T(8,128)(2,1)} collective-permute-done((bf16[16,272,128]{2,1,0:T(8,128)(2,1)}, bf16[16,272,128]{2,1,0:T(8,128)(2,1)}, u32[]{:S(2)}, u32[]{:S(2)}) %collective-permute-start.10) | collective-permute-done | bytes 1114144 | tf_op jit(solution)/shard_map/ppermute | solution.py:748
  236.3 5.0 %merge.2 = (bf16[128,1024]{1,0:T(8,128)(2,1)S(1)}, bf16[128,1024]{1,0:T(8,128)(2,1)S(1)}, bf16[128,1024]{1,0:T(8,128)(2,1)S(1)}, bf16[128,1024]{1,0:T(8,128)(2,1)S(1)}) custom-call(s32[2]{0:T(128)S(1)} %copy-done.14, s32[192]{0:T(256)S(1)} %get-tuple-element.34.refs_1_, bf16[16,400,128]{2,1,0:T(8,128)(2,1)S(1)} %all-to-all-done.2.back.refs_2_, ...), custom_call_target="tpu_custom_call" | custom-call | flops 10485760 | bytes 8388608 | tf_op jit(solution)/shard_map/merge/pallas_call | solution.py:671
  241.3 3.1 %collective-permute-start.12 = (bf16[128,1024]{1,0:T(8,128)(2,1)S(1)}, bf16[128,1024]{1,0:T(8,128)(2,1)S(1)}, u32[]{:S(2)}, u32[]{:S(2)}) collective-permute-start(bf16[128,1024]{1,0:T(8,128)(2,1)S(1)} %get-tuple-element.54), channel_id=1, source_target_pairs={{0,1},{1,2},{2,3},{3,0},{4,5},{5,6},{6,7},{7,4},{8,9},{9,10},{10,1... | collective-permute-start | bytes 786440 | tf_op jit(solution)/shard_map/ppermute | solution.py:156
  247.3 5.0 %merge.3 = (bf16[128,1024]{1,0:T(8,128)(2,1)S(1)}, bf16[128,1024]{1,0:T(8,128)(2,1)S(1)}, bf16[128,1024]{1,0:T(8,128)(2,1)S(1)}, bf16[128,1024]{1,0:T(8,128)(2,1)S(1)}) custom-call(s32[2]{0:T(128)S(1)} %copy-done.14, s32[192]{0:T(256)S(1)} %get-tuple-element.34.refs_1_, bf16[16,400,128]{2,1,0:T(8,128)(2,1)S(1)} %all-to-all-done.2.back.refs_2_, ...), custom_call_target="tpu_custom_call" | custom-call | flops 10485760 | bytes 8388608 | tf_op jit(solution)/shard_map/merge/pallas_call | solution.py:671
  252.8 2.2 collective-permute-start.16
  255.7 2.8 %collective-permute-done.13.refs_2_ = bf16[128,1024]{1,0:T(8,128)(2,1)S(1)} collective-permute-done((bf16[128,1024]{1,0:T(8,128)(2,1)S(1)}, bf16[128,1024]{1,0:T(8,128)(2,1)S(1)}, u32[]{:S(2)}, u32[]{:S(2)}) %collective-permute-start.13) | collective-permute-done | bytes 262176 | tf_op jit(solution)/shard_map/ppermute | solution.py:156
  258.5 5.6 %collective-permute-done.15.refs_5_ = bf16[128,1024]{1,0:T(8,128)(2,1)S(1)} collective-permute-done((bf16[128,1024]{1,0:T(8,128)(2,1)S(1)}, bf16[128,1024]{1,0:T(8,128)(2,1)S(1)}, u32[]{:S(2)}, u32[]{:S(2)}) %collective-permute-start.15) | collective-permute-done | bytes 262176 | tf_op jit(solution)/shard_map/ppermute | solution.py:156
  264.1 4.3 %collective-permute-done.16.refs_6_ = bf16[128,1024]{1,0:T(8,128)(2,1)S(1)} collective-permute-done((bf16[128,1024]{1,0:T(8,128)(2,1)S(1)}, bf16[128,1024]{1,0:T(8,128)(2,1)S(1)}, u32[]{:S(2)}, u32[]{:S(2)}) %collective-permute-start.16) | collective-permute-done | bytes 262176 | tf_op jit(solution)/shard_map/ppermute | solution.py:156
  (73 shorter events, 32.2 us)
Async XLA Ops:
  0.0 9.5 %copy-start.19 = (s32[8,8,3]{1,0,2:T(8,128)S(1)}, s32[8,8,3]{1,0,2:T(8,128)}, u32[]{:S(2)}) copy-start(s32[8,8,3]{1,0,2:T(8,128)} %param.7) | copy-start | bytes 2308
  0.6 9.2 %copy-start.12 = (s32[2]{0:T(128)S(1)}, s32[2]{0:T(128)}, u32[]{:S(2)}) copy-start(s32[2]{0:T(128)} %pad_add_fusion.meta.refs_0_) | copy-start | bytes 28
  3.6 15.2 %collective-permute-start = (bf16[256,1024]{1,0:T(8,128)(2,1)}, bf16[256,1024]{1,0:T(8,128)(2,1)S(1)}, u32[]{:S(2)}, u32[]{:S(2)}) collective-permute-start(bf16[256,1024]{1,0:T(8,128)(2,1)} %get-tuple-element.36), channel_id=1, source_target_pairs={{0,1},{1,2},{2,3},{3,0},{4,5},{5,6},{6,7},{7,4},{8,9},{9,10},{10,1... | collective-permute-start | bytes 1572872 | tf_op jit(solution)/shard_map/ppermute | solution.py:156
  5.3 26.0 %collective-permute-start.1 = (bf16[256,1024]{1,0:T(8,128)(2,1)}, bf16[256,1024]{1,0:T(8,128)(2,1)S(1)}, u32[]{:S(2)}, u32[]{:S(2)}) collective-permute-start(bf16[256,1024]{1,0:T(8,128)(2,1)} %get-tuple-element.37), channel_id=1, source_target_pairs={{0,2},{1,3},{2,0},{3,1},{4,6},{5,7},{6,4},{7,5},{8,10},{9,11},{10,... | collective-permute-start | bytes 1572872 | tf_op jit(solution)/shard_map/ppermute | solution.py:156
  8.2 23.1 %collective-permute-start.2 = (bf16[256,1024]{1,0:T(8,128)(2,1)}, bf16[256,1024]{1,0:T(8,128)(2,1)S(1)}, u32[]{:S(2)}, u32[]{:S(2)}) collective-permute-start(bf16[256,1024]{1,0:T(8,128)(2,1)} %get-tuple-element.38), channel_id=1, source_target_pairs={{0,3},{1,0},{2,1},{3,2},{4,7},{5,4},{6,5},{7,6},{8,11},{9,8},{10,9... | collective-permute-start | bytes 1572872 | tf_op jit(solution)/shard_map/ppermute | solution.py:156
  18.8 12.4 %copy-start.3 = (bf16[256,1024]{1,0:T(8,128)(2,1)}, bf16[256,1024]{1,0:T(8,128)(2,1)S(1)}, u32[]{:S(2)}) copy-start(bf16[256,1024]{1,0:T(8,128)(2,1)S(1)} %collective-permute-done.refs_3_.q1) | copy-start | bytes 1572868
  36.6 14.1 %copy-start = (bf16[256,4096]{1,0:T(8,128)(2,1)S(1)}, bf16[256,4096]{1,0:T(8,128)(2,1)}, u32[]{:S(2)}) copy-start(bf16[256,4096]{1,0:T(8,128)(2,1)} %q0.1) | copy-start | bytes 6291460
  36.6 14.1 %copy-start.13 = (s32[2]{0:T(128)S(1)}, s32[2]{0:T(128)}, u32[]{:S(2)}) copy-start(s32[2]{0:T(128)} %pad_add_fusion.meta.refs_0_) | copy-start | bytes 28
  36.6 14.1 %copy-start.18 = (s32[128]{0:T(128)S(1)}, s32[128]{0:T(128)}, u32[]{:S(2)}) copy-start(s32[128]{0:T(128)} %copy-done.17) | copy-start | bytes 1540
  36.6 37.8 %all-to-all-start.1 = ((bf16[16,272,128]{2,1,0:T(8,128)(2,1)}), bf16[16,272,128]{2,1,0:T(8,128)(2,1)}, u32[]{:S(2)}, u32[]{:S(2)}) async-start(bf16[16,272,128]{2,1,0:T(8,128)(2,1)} %get-tuple-element.45), calls=%async_computation.1 | async-start | bytes 2228224 | tf_op jit(solution)/shard_map/all_to_all | solution.py:723
  45.4 27.0 %collective-permute-start.3 = (bf16[16,272,128]{2,1,0:T(8,128)(2,1)}, bf16[16,272,128]{2,1,0:T(8,128)(2,1)S(1)}, u32[]{:S(2)}, u32[]{:S(2)}) collective-permute-start(bf16[16,272,128]{2,1,0:T(8,128)(2,1)} %get-tuple-element.39), channel_id=1, source_target_pairs={{192,0},{196,4},{200,8},{204,12},{208,16},{212,20},{216,24},{220,2... | collective-permute-start | bytes 3342344 | tf_op jit(solution)/shard_map/ppermute | solution.py:735
  47.8 15.9 %collective-permute-start.4 = (bf16[16,144,128]{2,1,0:T(8,128)(2,1)}, bf16[16,144,128]{2,1,0:T(8,128)(2,1)S(1)}, u32[]{:S(2)}, u32[]{:S(2)}) collective-permute-start(bf16[16,144,128]{2,1,0:T(8,128)(2,1)} %get-tuple-element.40), channel_id=1, source_target_pairs={{64,0},{68,4},{72,8},{76,12},{80,16},{84,20},{88,24},{92,28},{96,3... | collective-permute-start | bytes 1769480 | tf_op jit(solution)/shard_map/ppermute | solution.py:736
  74.4 54.1 %all-to-all-start = ((bf16[16,400,128]{2,1,0:T(8,128)(2,1)}), bf16[16,400,128]{2,1,0:T(8,128)(2,1)}, u32[]{:S(2)}, u32[]{:S(2)}) async-start(bf16[16,400,128]{2,1,0:T(8,128)(2,1)} %insert.1), calls=%async_computation | async-start | bytes 3276800 | tf_op jit(solution)/shard_map/all_to_all | solution.py:723
  82.5 10.2 %collective-permute-start.5 = (bf16[256,512]{1,0:T(8,128)(2,1)S(1)}, bf16[256,512]{1,0:T(8,128)(2,1)S(1)}, u32[]{:S(2)}, u32[]{:S(2)}) collective-permute-start(bf16[256,512]{1,0:T(8,128)(2,1)S(1)} %get-tuple-element.42), channel_id=1, source_target_pairs={{0,1},{1,2},{2,3},{3,0},{4,5},{5,6},{6,7},{7,4},{8,9},{9,10},{10,1... | collective-permute-start | bytes 786440 | tf_op jit(solution)/shard_map/ppermute | solution.py:156
  83.7 14.5 %collective-permute-start.6 = (bf16[256,512]{1,0:T(8,128)(2,1)S(1)}, bf16[256,512]{1,0:T(8,128)(2,1)S(1)}, u32[]{:S(2)}, u32[]{:S(2)}) collective-permute-start(bf16[256,512]{1,0:T(8,128)(2,1)S(1)} %get-tuple-element.43), channel_id=1, source_target_pairs={{0,2},{1,3},{2,0},{3,1},{4,6},{5,7},{6,4},{7,5},{8,10},{9,11},{10,... | collective-permute-start | bytes 786440 | tf_op jit(solution)/shard_map/ppermute | solution.py:156
  86.0 12.6 %collective-permute-start.7 = (bf16[256,512]{1,0:T(8,128)(2,1)S(1)}, bf16[256,512]{1,0:T(8,128)(2,1)S(1)}, u32[]{:S(2)}, u32[]{:S(2)}) collective-permute-start(bf16[256,512]{1,0:T(8,128)(2,1)S(1)} %get-tuple-element.44), channel_id=1, source_target_pairs={{0,3},{1,0},{2,1},{3,2},{4,7},{5,4},{6,5},{7,6},{8,11},{9,8},{10,9... | collective-permute-start | bytes 786440 | tf_op jit(solution)/shard_map/ppermute | solution.py:156
  99.3 26.3 %collective-permute-start.8 = (bf16[1024,512]{1,0:T(8,128)(2,1)S(1)}, bf16[1024,512]{1,0:T(8,128)(2,1)S(1)}, u32[]{:S(2)}, u32[]{:S(2)}) collective-permute-start(bf16[1024,512]{1,0:T(8,128)(2,1)S(1)} %join.1.refs_2_.kv), channel_id=1, source_target_pairs={{0,64},{4,68},{8,72},{12,76},{16,80},{20,84},{24,88},{28,92},{32,9... | collective-permute-start | bytes 3145736 | tf_op jit(solution)/shard_map/ppermute | solution.py:739
  100.6 27.9 %collective-permute-start.9 = (bf16[1024,512]{1,0:T(8,128)(2,1)S(1)}, bf16[1024,512]{1,0:T(8,128)(2,1)S(1)}, u32[]{:S(2)}, u32[]{:S(2)}) collective-permute-start(bf16[1024,512]{1,0:T(8,128)(2,1)S(1)} %join.1.refs_2_.kv), channel_id=1, source_target_pairs={{64,192},{68,196},{72,200},{76,204},{80,208},{84,212},{88,216},{92... | collective-permute-start | bytes 3145736 | tf_op jit(solution)/shard_map/ppermute | solution.py:740
  152.5 45.7 %all-to-all-start.2 = ((bf16[16,400,128]{2,1,0:T(8,128)(2,1)}), bf16[16,400,128]{2,1,0:T(8,128)(2,1)S(1)}, u32[]{:S(2)}, u32[]{:S(2)}) async-start(bf16[16,400,128]{2,1,0:T(8,128)(2,1)} %get-tuple-element.46), calls=%async_computation.2 | async-start | bytes 3276800 | tf_op jit(solution)/shard_map/all_to_all | solution.py:723
  198.1 32.9 %all-to-all-start.3 = ((bf16[16,272,128]{2,1,0:T(8,128)(2,1)}), bf16[16,272,128]{2,1,0:T(8,128)(2,1)S(1)}, u32[]{:S(2)}, u32[]{:S(2)}) async-start(bf16[16,272,128]{2,1,0:T(8,128)(2,1)} %get-tuple-element.48), calls=%async_computation.3 | async-start | bytes 2228224 | tf_op jit(solution)/shard_map/all_to_all | solution.py:723
  202.9 31.7 %copy-start.14 = (s32[2]{0:T(128)S(1)}, s32[2]{0:T(128)}, u32[]{:S(2)}) copy-start(s32[2]{0:T(128)} %pad_add_fusion.meta.refs_0_) | copy-start | bytes 28
  203.0 31.7 %copy-start.16 = (f32[32,128]{1,0:T(8,128)S(1)}, f32[32,128]{1,0:T(8,128)}, u32[]{:S(2)}) copy-start(f32[32,128]{1,0:T(8,128)} %get-tuple-element.52.refs_7_) | copy-start | bytes 49156
  204.3 30.3 %collective-permute-start.10 = (bf16[16,272,128]{2,1,0:T(8,128)(2,1)}, bf16[16,272,128]{2,1,0:T(8,128)(2,1)}, u32[]{:S(2)}, u32[]{:S(2)}) collective-permute-start(bf16[16,272,128]{2,1,0:T(8,128)(2,1)} %get-tuple-element.49), channel_id=1, source_target_pairs={{0,192},{4,196},{8,200},{12,204},{16,208},{20,212},{24,216},{28,22... | collective-permute-start | bytes 3342344 | tf_op jit(solution)/shard_map/ppermute | solution.py:748
  205.6 25.4 %collective-permute-start.11 = (bf16[16,144,128]{2,1,0:T(8,128)(2,1)}, bf16[16,144,128]{2,1,0:T(8,128)(2,1)S(1)}, u32[]{:S(2)}, u32[]{:S(2)}) collective-permute-start(bf16[16,144,128]{2,1,0:T(8,128)(2,1)} %get-tuple-element.50), channel_id=1, source_target_pairs={{0,64},{4,68},{8,72},{12,76},{16,80},{20,84},{24,88},{28,92},{32,9... | collective-permute-start | bytes 1769480 | tf_op jit(solution)/shard_map/ppermute | solution.py:749
  236.3 11.1 %copy-start.1 = (f32[512,1024]{1,0:T(8,128)S(1)}, f32[512,1024]{1,0:T(8,128)}, u32[]{:S(2)}) copy-start(f32[512,1024]{1,0:T(8,128)} %get-tuple-element.57.refs_6_) | copy-start | bytes 6291460
  236.3 11.1 %copy-start.15 = (f32[32,128]{1,0:T(8,128)S(1)}, f32[32,128]{1,0:T(8,128)}, u32[]{:S(2)}) copy-start(f32[32,128]{1,0:T(8,128)} %get-tuple-element.58.refs_7_) | copy-start | bytes 49156
  241.3 13.8 %collective-permute-start.12 = (bf16[128,1024]{1,0:T(8,128)(2,1)S(1)}, bf16[128,1024]{1,0:T(8,128)(2,1)S(1)}, u32[]{:S(2)}, u32[]{:S(2)}) collective-permute-start(bf16[128,1024]{1,0:T(8,128)(2,1)S(1)} %get-tuple-element.54), channel_id=1, source_target_pairs={{0,1},{1,2},{2,3},{3,0},{4,5},{5,6},{6,7},{7,4},{8,9},{9,10},{10,1... | collective-permute-start | bytes 786440 | tf_op jit(solution)/shard_map/ppermute | solution.py:156
  244.4 14.1 %collective-permute-start.13 = (bf16[128,1024]{1,0:T(8,128)(2,1)S(1)}, bf16[128,1024]{1,0:T(8,128)(2,1)S(1)}, u32[]{:S(2)}, u32[]{:S(2)}) collective-permute-start(bf16[128,1024]{1,0:T(8,128)(2,1)S(1)} %get-tuple-element.55), channel_id=1, source_target_pairs={{0,2},{1,3},{2,0},{3,1},{4,6},{5,7},{6,4},{7,5},{8,10},{9,11},{10,... | collective-permute-start | bytes 786440 | tf_op jit(solution)/shard_map/ppermute | solution.py:156
  245.7 12.8 %collective-permute-start.14 = (bf16[128,1024]{1,0:T(8,128)(2,1)S(1)}, bf16[128,1024]{1,0:T(8,128)(2,1)S(1)}, u32[]{:S(2)}, u32[]{:S(2)}) collective-permute-start(bf16[128,1024]{1,0:T(8,128)(2,1)S(1)} %get-tuple-element.56), channel_id=1, source_target_pairs={{0,3},{1,0},{2,1},{3,2},{4,7},{5,4},{6,5},{7,6},{8,11},{9,8},{10,9... | collective-permute-start | bytes 786440 | tf_op jit(solution)/shard_map/ppermute | solution.py:156
  252.4 11.8 %collective-permute-start.15 = (bf16[128,1024]{1,0:T(8,128)(2,1)S(1)}, bf16[128,1024]{1,0:T(8,128)(2,1)S(1)}, u32[]{:S(2)}, u32[]{:S(2)}) collective-permute-start(bf16[128,1024]{1,0:T(8,128)(2,1)S(1)} %get-tuple-element.60), channel_id=1, source_target_pairs={{0,1},{1,2},{2,3},{3,0},{4,5},{5,6},{6,7},{7,4},{8,9},{9,10},{10,1... | collective-permute-start | bytes 786440 | tf_op jit(solution)/shard_map/ppermute | solution.py:156
  252.8 15.6 %collective-permute-start.16 = (bf16[128,1024]{1,0:T(8,128)(2,1)S(1)}, bf16[128,1024]{1,0:T(8,128)(2,1)S(1)}, u32[]{:S(2)}, u32[]{:S(2)}) collective-permute-start(bf16[128,1024]{1,0:T(8,128)(2,1)S(1)} %get-tuple-element.61), channel_id=1, source_target_pairs={{0,2},{1,3},{2,0},{3,1},{4,6},{5,7},{6,4},{7,5},{8,10},{9,11},{10,... | collective-permute-start | bytes 786440 | tf_op jit(solution)/shard_map/ppermute | solution.py:156
  255.1 13.3 %collective-permute-start.17 = (bf16[128,1024]{1,0:T(8,128)(2,1)S(1)}, bf16[128,1024]{1,0:T(8,128)(2,1)S(1)}, u32[]{:S(2)}, u32[]{:S(2)}) collective-permute-start(bf16[128,1024]{1,0:T(8,128)(2,1)S(1)} %get-tuple-element.62), channel_id=1, source_target_pairs={{0,3},{1,0},{2,1},{3,2},{4,7},{5,4},{6,5},{7,6},{8,11},{9,8},{10,9... | collective-permute-start | bytes 786440 | tf_op jit(solution)/shard_map/ppermute | solution.py:156
  (12 other events, 27.9 us)
